TPU v7x, 32 devices: a whole 2x2x4 slice. The times are simulated.
32 devices in a mesh: dp: 2 (over core), seq: 16 (over z, y, x).
Axes of the slice: x: 2, y: 2, z: 4, core: 2. Of those that a mesh axis runs over, the one named last changes fastest.
Arguments:
- query: bfloat16 [4096, 4096], P('dp', 'seq'), parts along dimension 0, may hold values from -6 to 6
- key_seq: bfloat16 [4096, 512], P(('dp', 'seq')), parts along dimension 0, may hold values from -6 to 6
- value_seq: bfloat16 [4096, 512], P(('dp', 'seq')), parts along dimension 0, may hold values from -6 to 6
- attn_out: bfloat16 [4096, 4096], P(('dp', 'seq')), parts along dimension 0, may hold values from -6 to 6
- grad_out: bfloat16 [4096, 4096], P(('dp', 'seq')), parts along dimension 0, may hold values from -6 to 6
- lse: float32 [32, 4096], P('seq', 'dp'), parts along dimension 1, as said below
Outputs:
- query_grad: bfloat16 [4096, 4096], P(('dp', 'seq')), parts along dimension 0
- key_grad: bfloat16 [4096, 512], P(('dp', 'seq')), parts along dimension 0
- value_grad: bfloat16 [4096, 512], P(('dp', 'seq')), parts along dimension 0
There are 2 independent parts, one for each index of `dp`. A program takes and returns all parts, laid end to end along the dimension named above; each array names one. Nothing has to cross between parts.
Inputs may be any that keep to these rules, and one draw needn't show every extreme that they name: lse[h, i] is the log of the sum over k <= i of exp(q_h[i] . k_g(h)[k] / sqrt(128)), computed from these query and key_seq arrays.
All inputs are finite; a program needn't handle non-finite values.
Results may differ from a plain program's by a relative error of at most 0.0054.
Values may be sent and summed in bfloat16 or wider, within the bound.
No kernel may reach another device: no remote copies, remote signals or barrier semaphores. Data moves between devices by JAX's collectives and lax.ppermute only.
A program may use at most 128 MiB of HBM per device.

v0:
```python
import math

import jax
import jax.numpy as jnp
from jax import lax
from jax.sharding import PartitionSpec as P

DH = 128


def per_device(query, key_seq, value_seq, attn_out, grad_out, lse):
    seq_count = lax.axis_size("seq")
    local_rows = key_seq.shape[0]
    total_rows = local_rows * seq_count
    kv_heads = key_seq.shape[1] // DH
    heads_here = lse.shape[0]
    copies = seq_count // kv_heads
    scale_factor = DH ** (-0.5)
    key_send = jnp.repeat(key_seq.reshape(local_rows, kv_heads, DH), copies, axis=1)
    value_send = jnp.repeat(value_seq.reshape(local_rows, kv_heads, DH), copies, axis=1)
    key_all, value_all = (
        lax.all_to_all(key_send, "seq", split_axis=1, concat_axis=0, tiled=True),
        lax.all_to_all(value_send, "seq", split_axis=1, concat_axis=0, tiled=True),
    )
    key_all = key_all.reshape(total_rows, DH)
    value_all = value_all.reshape(total_rows, DH)
    grad_split = grad_out.reshape(local_rows, seq_count, heads_here * DH)
    out_split = attn_out.reshape(local_rows, seq_count, heads_here * DH)
    grad_heads, out_heads = (
        lax.all_to_all(grad_split, "seq", split_axis=1, concat_axis=0, tiled=True),
        lax.all_to_all(out_split, "seq", split_axis=1, concat_axis=0, tiled=True),
    )
    products = grad_heads.astype(jnp.float32) * out_heads.astype(jnp.float32)
    delta = products.reshape(total_rows, heads_here, DH).sum(axis=2).astype(jnp.bfloat16)
    delta_first = delta.T
    grad_first = grad_heads.reshape(total_rows, heads_here, DH).transpose(1, 0, 2)
    query_first = query.reshape(total_rows, heads_here, DH).transpose(1, 0, 2)
    block_rows = math.gcd(total_rows, 512)
    block_count = total_rows // block_rows
    key_terms = []
    value_terms = []
    query_parts = []
    for number in range(block_count):
        start = number * block_rows
        finish = start + block_rows
        query_block = query_first[:, start:finish]
        grad_block = grad_first[:, start:finish]
        keys_seen = key_all[:finish]
        values_seen = value_all[:finish]
        scores = (
            jnp.einsum("hqd,kd->hqk", query_block, keys_seen, preferred_element_type=jnp.float32)
            * scale_factor
        )
        row_ids = start + lax.broadcasted_iota(jnp.int32, (block_rows, finish), 0)
        col_ids = lax.broadcasted_iota(jnp.int32, (block_rows, finish), 1)
        scores = jnp.where((col_ids <= row_ids)[None], scores, -1e30)
        probs = jnp.exp(scores - lse[:, start:finish][:, :, None])
        probs_low = probs.astype(jnp.bfloat16)
        value_terms.append(
            jnp.einsum("hqk,hqd->kd", probs_low, grad_block, preferred_element_type=jnp.float32)
        )
        grad_probs = jnp.einsum(
            "hqd,kd->hqk", grad_block, values_seen, preferred_element_type=jnp.float32
        )
        delta_block = delta_first[:, start:finish].astype(jnp.float32)[:, :, None]
        score_grad = (probs * (grad_probs - delta_block)).astype(jnp.bfloat16)
        query_block_grad = (
            jnp.einsum("hqk,kd->hqd", score_grad, keys_seen, preferred_element_type=jnp.float32)
            * scale_factor
        )
        query_parts.append(query_block_grad.astype(jnp.bfloat16))
        key_terms.append(
            jnp.einsum("hqk,hqd->kd", score_grad, query_block, preferred_element_type=jnp.float32)
            * scale_factor
        )
    key_blocks = []
    value_blocks = []
    for target in range(block_count):
        low = target * block_rows
        high = low + block_rows
        key_blocks.append(
            sum((key_terms[source][low:high] for source in range(target, block_count)))
        )
        value_blocks.append(
            sum((value_terms[source][low:high] for source in range(target, block_count)))
        )
    key_accum = jnp.concatenate(key_blocks, axis=0)
    value_accum = jnp.concatenate(value_blocks, axis=0)
    query_local = (
        jnp.concatenate(query_parts, axis=1)
        .transpose(1, 0, 2)
        .reshape(seq_count, local_rows, heads_here * DH)
    )
    returned = lax.all_to_all(query_local, "seq", split_axis=0, concat_axis=2, tiled=True)
    query_grad = returned.reshape(local_rows, seq_count * heads_here * DH)
    key_parts, value_parts = (
        lax.all_to_all(
            key_accum.reshape(seq_count, local_rows, DH),
            "seq",
            split_axis=0,
            concat_axis=2,
            tiled=True,
        ),
        lax.all_to_all(
            value_accum.reshape(seq_count, local_rows, DH),
            "seq",
            split_axis=0,
            concat_axis=2,
            tiled=True,
        ),
    )
    key_sum = (
        key_parts.reshape(local_rows, kv_heads, copies, DH)
        .sum(axis=2)
        .reshape(local_rows, kv_heads * DH)
    )
    value_sum = (
        value_parts.reshape(local_rows, kv_heads, copies, DH)
        .sum(axis=2)
        .reshape(local_rows, kv_heads * DH)
    )
    return (query_grad, key_sum.astype(jnp.bfloat16), value_sum.astype(jnp.bfloat16))


def solution(mesh):
    placed = (
        P("dp", "seq"),
        P(("dp", "seq"), None),
        P(("dp", "seq"), None),
        P(("dp", "seq"), None),
        P(("dp", "seq"), None),
        P("seq", "dp"),
    )
    return jax.shard_map(
        per_device,
        mesh=mesh,
        in_specs=placed,
        out_specs=(P(("dp", "seq"), None), P(("dp", "seq"), None), P(("dp", "seq"), None)),
        check_vma=False,
    )
```

profile of v0, /device:TPU:0, one launch (start us, length us, event | category | flops | bytes accessed | tf_op | source)
XLA Modules:
  0.0 214.8 jit_solution(16931844245605818445)
XLA Ops:
  2.5 8.3 %all-to-all-start.2 = ((bf16[128,16,128]{2,0,1:T(8,128)(2,1)}), bf16[128,16,128]{2,0,1:T(8,128)(2,1)S(1)}, u32[]{:S(2)}, u32[]{:S(2)}) async-start(bf16[128,16,128]{2,0,1:T(8,128)(2,1)} %bitcast.11), calls=%async_computation.2 | async-start | bytes 1048576 | tf_op jit(solution)/shard_map/all_to_all | solution.py:23
  11.7 14.2 %all-to-all-done.2 = bf16[128,16,128]{2,0,1:T(8,128)(2,1)S(1)} async-done(((bf16[128,16,128]{2,0,1:T(8,128)(2,1)}), bf16[128,16,128]{2,0,1:T(8,128)(2,1)S(1)}, u32[]{:S(2)}, u32[]{:S(2)}) %all-to-all-start.2) | async-done | bytes 524320 | tf_op jit(solution)/shard_map/all_to_all | solution.py:23
  26.9 3.9 %all-to-all-start = ((bf16[128,16,128]{2,0,1:T(8,128)(2,1)}), bf16[128,16,128]{2,0,1:T(8,128)(2,1)S(1)}, u32[]{:S(2)}, u32[]{:S(2)}) async-start(bf16[128,16,128]{2,0,1:T(8,128)(2,1)} %bitcast.2), calls=%async_computation | async-start | bytes 1048576 | tf_op jit(solution)/shard_map/all_to_all | solution.py:22
  32.1 13.1 %all-to-all-done = bf16[128,16,128]{2,0,1:T(8,128)(2,1)S(1)} async-done(((bf16[128,16,128]{2,0,1:T(8,128)(2,1)}), bf16[128,16,128]{2,0,1:T(8,128)(2,1)S(1)}, u32[]{:S(2)}, u32[]{:S(2)}) %all-to-all-start) | async-done | bytes 524320 | tf_op jit(solution)/shard_map/all_to_all | solution.py:22
  45.2 4.0 %all-to-all-start.3 = ((bf16[128,16,256]{0,2,1:T(8,128)(2,1)}), bf16[128,16,256]{0,2,1:T(8,128)(2,1)S(1)}, u32[]{:S(2)}, u32[]{:S(2)}) async-start(bf16[128,16,256]{0,2,1:T(8,128)(2,1)} %bitcast.16), calls=%async_computation.3 | async-start | bytes 2097152 | tf_op jit(solution)/shard_map/all_to_all | solution.py:31
  53.1 1.7 iota_compare_fusion
  54.8 18.0 %all-to-all-done.3 = bf16[128,16,256]{0,2,1:T(8,128)(2,1)S(1)} async-done(((bf16[128,16,256]{0,2,1:T(8,128)(2,1)}), bf16[128,16,256]{0,2,1:T(8,128)(2,1)S(1)}, u32[]{:S(2)}, u32[]{:S(2)}) %all-to-all-start.3) | async-done | bytes 1048608 | tf_op jit(solution)/shard_map/all_to_all | solution.py:31
  72.8 5.9 %all-to-all-start.1 = ((bf16[128,16,256]{0,2,1:T(8,128)(2,1)}), bf16[128,16,256]{0,2,1:T(8,128)(2,1)}, u32[]{:S(2)}, u32[]{:S(2)}) async-start(bf16[128,16,256]{0,2,1:T(8,128)(2,1)} %bitcast.7), calls=%async_computation.1 | async-start | bytes 2097152 | tf_op jit(solution)/shard_map/all_to_all | solution.py:30
  80.7 1.6 copy.74
  84.9 2.7 %fusion.49 = f32[2,512,1024]{2,1,0:T(8,128)} fusion(bf16[1024,128,1]{1,0,2:T(8,128)(2,1)S(1)} %bitcast.186, bf16[2,2048,128]{2,1,0:T(8,128)(2,1)S(1)} %bitcast.157), kind=kOutput, calls=%fused_computation.74 | convolution fusion | flops 268435456 | bytes 4718592 | tf_op jit(solution)/shard_map/hqd,kd->hqk/dot_general | solution.py:51
  87.6 3.7 %fusion.44 = f32[2,512,1536]{2,1,0:T(8,128)} fusion(bf16[1536,128,1]{1,0,2:T(8,128)(2,1)S(1)} %bitcast.184, bf16[2,2048,128]{2,1,0:T(8,128)(2,1)S(1)} %bitcast.158), kind=kOutput, calls=%fused_computation.69 | convolution fusion | flops 402653184 | bytes 6946816 | tf_op jit(solution)/shard_map/hqd,kd->hqk/dot_general | solution.py:51
  91.3 4.6 %fusion.39 = f32[2,512,2048]{2,1,0:T(8,128)} fusion(bf16[2048,128,1]{1,0,2:T(8,128)(2,1)S(1)} %bitcast.167, bf16[2,2048,128]{2,1,0:T(8,128)(2,1)S(1)} %bitcast.159), kind=kOutput, calls=%fused_computation.64 | convolution fusion | flops 536870912 | bytes 9175040 | tf_op jit(solution)/shard_map/hqd,kd->hqk/dot_general | solution.py:51
  96.1 2.6 %copy.81 = f32[16,128,1,256]{1,0,3,2:T(8,128)} copy(f32[16,128,1,256]{1,3,0,2:T(8,128)S(1)} %convert_bitcast_fusion) | data formatting | bytes 4194304 | tf_op jit(solution)/shard_map/convert_element_type | solution.py:33
  98.6 2.7 %reshape.154 = f32[2048,2,128]{0,2,1:T(8,128)} reshape(f32[16,128,1,256]{1,0,3,2:T(8,128)} %copy.81) | data formatting | bytes 4194304 | tf_op jit(solution)/shard_map/convert_element_type | solution.py:33
  101.7 2.9 %copy.77 = bf16[16,128,1,256]{1,0,3,2:T(8,128)(2,1)} copy(bf16[16,128,1,256]{1,3,0,2:T(8,128)(2,1)} %bitcast.9) | data formatting | bytes 2097152 | tf_op jit(solution)/shard_map/all_to_all | solution.py:30
  104.6 1.5 reshape.142
  107.4 1.9 multiply_reduce_fusion
  109.4 3.8 %fusion.20 = f32[1024,128]{1,0:T(8,128)S(1)} fusion(f32[2,512,1024]{2,1,0:T(8,128)} %fusion.49, f32[2,512]{1,0:T(2,128)} %get-tuple-element.19, pred[512,1024]{1,0:T(8,128)(4,1)} %iota_compare_fusion.2, bf16[2,2048,128]{2,1,0:T(8,128)(2,1)} %bitcast.176), kind=kOutput, calls=%fused_computation.31 | convolution fusion | flops 272629760 | bytes 5509120 | tf_op jit(solution)/shard_map/hqk,hqd->kd/dot_general | solution.py:60
  113.5 1.9 multiply_convert_fusion.2
  116.8 5.2 %fusion.9 = f32[1536,128]{1,0:T(8,128)S(1)} fusion(f32[2,512,1536]{2,1,0:T(8,128)} %fusion.44, f32[2,512]{1,0:T(2,128)S(1)} %copy-done.32, pred[512,1536]{1,0:T(8,128)(4,1)S(1)} %copy-done.25, bf16[2,2048,128]{2,1,0:T(8,128)(2,1)S(1)} %bitcast.181), kind=kOutput, calls=%fused_computation.15 | convolution fusion | flops 408944640 | bytes 8130560 | tf_op jit(solution)/shard_map/hqk,hqd->kd/dot_general | solution.py:60
  122.0 2.6 %fusion.12 = f32[2048,128]{1,0:T(8,128)S(1)} fusion(f32[2,512,2048]{2,1,0:T(8,128)S(1)} %bitcast.153, f32[2,512]{1,0:T(2,128)S(1)} %get-tuple-element.20, pred[512,2048]{1,0:T(8,128)(4,1)S(1)} %copy-done.23, bf16[2,2048,128]{2,1,0:T(8,128)(2,1)S(1)} %bitcast.182), kind=kOutput, calls=%fused_computation.16 | convolution fusion | flops 545259520 | bytes 10752000 | tf_op jit(solution)/shard_map/hqk,hqd->kd/dot_general | solution.py:60
  126.3 6.6 %all-to-all-start.6 = ((f32[16,128,128]{2,1,0:T(8,128)}), f32[16,128,128]{2,1,0:T(8,128)}, u32[]{:S(2)}, u32[]{:S(2)}) async-start(f32[16,128,128]{2,1,0:T(8,128)} %bitcast.51), calls=%async_computation.6 | async-start | bytes 2097152 | tf_op jit(solution)/shard_map/all_to_all | solution.py:104
  132.8 1.5 multiply_convert_fusion.3
  134.4 5.5 %multiply_convert_fusion.1 = bf16[2,512,1536]{2,1,0:T(8,128)(2,1)S(1)} fusion(f32[2,512,1536]{2,1,0:T(8,128)} %fusion.44, bf16[1536,128,1]{1,0,2:T(8,128)(2,1)} %bitcast.193, f32[2,512]{1,0:T(2,128)S(1)} %get-tuple-element.24, f32[2,512]{1,0:T(2,128)S(1)} %copy-done.33, pred[512,1536]{1,0:T(8,128)(4,1)} %iota_compare_fusion.1, ...), kind=kOutput, calls=%fused_computation.3 | convolution fusion | flops 412090368 | bytes 10887168 | tf_op jit(solution)/shard_map/hqd,kd->hqk/dot_general | solution.py:62
  142.5 4.0 %multiply_convert_fusion = bf16[2,512,2048]{2,1,0:T(8,128)(2,1)S(1)} fusion(f32[2,512,2048]{2,1,0:T(8,128)S(1)} %bitcast.155, bf16[2048,128,1]{1,0,2:T(8,128)(2,1)S(1)} %bitcast.175, f32[2,512]{1,0:T(2,128)S(1)} %get-tuple-element.23, f32[2,512]{1,0:T(2,128)S(1)} %get-tuple-element.20, pred[512,2048]{1,0:T(8,128)(4,1)S(1)} %copy-done.24, ...), kind=kOutput, calls=%fused_computation | convolution fusion | flops 549453824 | bytes 14426112 | tf_op jit(solution)/shard_map/hqd,kd->hqk/dot_general | solution.py:62
  152.5 3.5 %all-to-all-done.6 = f32[16,128,128]{2,1,0:T(8,128)} async-done(((f32[16,128,128]{2,1,0:T(8,128)}), f32[16,128,128]{2,1,0:T(8,128)}, u32[]{:S(2)}, u32[]{:S(2)}) %all-to-all-start.6) | async-done | bytes 1048608 | tf_op jit(solution)/shard_map/all_to_all | solution.py:104
  156.0 6.0 %all-to-all-start.4 = ((bf16[16,128,256]{1,2,0:T(8,128)(2,1)}), bf16[16,128,256]{1,2,0:T(8,128)(2,1)}, u32[]{:S(2)}, u32[]{:S(2)}) async-start(bf16[16,128,256]{1,2,0:T(8,128)(2,1)} %copy.83), calls=%async_computation.4 | async-start | bytes 2097152 | tf_op jit(solution)/shard_map/all_to_all | solution.py:94
  162.0 2.5 %fusion.23 = f32[1024,128]{1,0:T(8,128)S(1)} fusion(bf16[2,512,1024]{2,1,0:T(8,128)(2,1)} %copy-done.7, bf16[2,2048,128]{2,1,0:T(8,128)(2,1)S(1)} %bitcast.160), kind=kOutput, calls=%fused_computation.33 | convolution fusion | flops 268566528 | bytes 2883584 | tf_op jit(solution)/shard_map/hqk,hqd->kd/dot_general | solution.py:73
  168.7 16.2 %all-to-all-done.4 = bf16[16,128,256]{1,2,0:T(8,128)(2,1)} async-done(((bf16[16,128,256]{1,2,0:T(8,128)(2,1)}), bf16[16,128,256]{1,2,0:T(8,128)(2,1)}, u32[]{:S(2)}, u32[]{:S(2)}) %all-to-all-start.4) | async-done | bytes 1048608 | tf_op jit(solution)/shard_map/all_to_all | solution.py:94
  184.9 6.0 %all-to-all-start.5 = ((f32[16,128,128]{2,1,0:T(8,128)}), f32[16,128,128]{2,1,0:T(8,128)S(1)}, u32[]{:S(2)}, u32[]{:S(2)}) async-start(f32[16,128,128]{2,1,0:T(8,128)} %bitcast.42), calls=%async_computation.5 | async-start | bytes 2097152 | tf_op jit(solution)/shard_map/all_to_all | solution.py:97
  193.1 2.3 %copy.94 = bf16[128,4096]{1,0:T(8,128)(2,1)} copy(bf16[128,4096]{0,1:T(8,128)(2,1)} %bitcast.37) | data formatting | bytes 2097152
  195.4 18.4 %all-to-all-done.5 = f32[16,128,128]{2,1,0:T(8,128)S(1)} async-done(((f32[16,128,128]{2,1,0:T(8,128)}), f32[16,128,128]{2,1,0:T(8,128)S(1)}, u32[]{:S(2)}, u32[]{:S(2)}) %all-to-all-start.5) | async-done | bytes 1048608 | tf_op jit(solution)/shard_map/all_to_all | solution.py:97
  (127 shorter events, 34.6 us)
Async XLA Ops:
  0.6 30.2 %copy-start.20 = (bf16[128,4096]{1,0:T(8,128)(2,1)S(1)}, bf16[128,4096]{1,0:T(8,128)(2,1)}, u32[]{:S(2)}) copy-start(bf16[128,4096]{1,0:T(8,128)(2,1)} %param.9) | copy-start | bytes 3145732
  0.7 48.6 %copy-start.21 = (bf16[128,4096]{1,0:T(8,128)(2,1)S(1)}, bf16[128,4096]{1,0:T(8,128)(2,1)}, u32[]{:S(2)}) copy-start(bf16[128,4096]{1,0:T(8,128)(2,1)} %param.10) | copy-start | bytes 3145732
  2.5 23.5 %all-to-all-start.2 = ((bf16[128,16,128]{2,0,1:T(8,128)(2,1)}), bf16[128,16,128]{2,0,1:T(8,128)(2,1)S(1)}, u32[]{:S(2)}, u32[]{:S(2)}) async-start(bf16[128,16,128]{2,0,1:T(8,128)(2,1)} %bitcast.11), calls=%async_computation.2 | async-start | bytes 1048576 | tf_op jit(solution)/shard_map/all_to_all | solution.py:23
  25.9 57.4 %copy-start.15 = (bf16[128,16,128]{2,0,1:T(8,128)(2,1)}, bf16[128,16,128]{2,0,1:T(8,128)(2,1)S(1)}, u32[]{:S(2)}) copy-start(bf16[128,16,128]{2,0,1:T(8,128)(2,1)S(1)} %all-to-all-done.2) | copy-start | bytes 1572868
  26.9 18.3 %all-to-all-start = ((bf16[128,16,128]{2,0,1:T(8,128)(2,1)}), bf16[128,16,128]{2,0,1:T(8,128)(2,1)S(1)}, u32[]{:S(2)}, u32[]{:S(2)}) async-start(bf16[128,16,128]{2,0,1:T(8,128)(2,1)} %bitcast.2), calls=%async_computation | async-start | bytes 1048576 | tf_op jit(solution)/shard_map/all_to_all | solution.py:22
  45.2 38.9 %copy-start.4 = (bf16[128,16,128]{2,0,1:T(8,128)(2,1)}, bf16[128,16,128]{2,0,1:T(8,128)(2,1)S(1)}, u32[]{:S(2)}) copy-start(bf16[128,16,128]{2,0,1:T(8,128)(2,1)S(1)} %all-to-all-done) | copy-start | bytes 1572868
  45.2 33.5 %copy-start.31 = (f32[2,2048]{1,0:T(2,128)S(1)}, f32[2,2048]{1,0:T(2,128)}, u32[]{:S(2)}) copy-start(f32[2,2048]{1,0:T(2,128)} %param.11) | copy-start | bytes 49156
  45.2 27.6 %all-to-all-start.3 = ((bf16[128,16,256]{0,2,1:T(8,128)(2,1)}), bf16[128,16,256]{0,2,1:T(8,128)(2,1)S(1)}, u32[]{:S(2)}, u32[]{:S(2)}) async-start(bf16[128,16,256]{0,2,1:T(8,128)(2,1)} %bitcast.16), calls=%async_computation.3 | async-start | bytes 2097152 | tf_op jit(solution)/shard_map/all_to_all | solution.py:31
  50.5 28.8 %copy-start.22 = (bf16[2048,256]{1,0:T(8,128)(2,1)S(1)}, bf16[2048,256]{1,0:T(8,128)(2,1)}, u32[]{:S(2)}) copy-start(bf16[2048,256]{1,0:T(8,128)(2,1)} %param.6) | copy-start | bytes 3145732
  72.8 11.3 %copy-start.12 = (bf16[128,16,256]{0,2,1:T(8,128)(2,1)}, bf16[128,16,256]{0,2,1:T(8,128)(2,1)S(1)}, u32[]{:S(2)}) copy-start(bf16[128,16,256]{0,2,1:T(8,128)(2,1)S(1)} %all-to-all-done.3) | copy-start | bytes 3145732
  72.8 28.9 %all-to-all-start.1 = ((bf16[128,16,256]{0,2,1:T(8,128)(2,1)}), bf16[128,16,256]{0,2,1:T(8,128)(2,1)}, u32[]{:S(2)}, u32[]{:S(2)}) async-start(bf16[128,16,256]{0,2,1:T(8,128)(2,1)} %bitcast.7), calls=%async_computation.1 | async-start | bytes 2097152 | tf_op jit(solution)/shard_map/all_to_all | solution.py:30
  82.3 9.0 %copy-start.2 = (bf16[2048,2,128]{2,0,1:T(8,128)(2,1)}, bf16[2048,2,128]{2,0,1:T(8,128)(2,1)S(1)}, u32[]{:S(2)}) copy-start(bf16[2048,2,128]{2,0,1:T(8,128)(2,1)S(1)} %copy.74) | copy-start | bytes 3145732
  84.2 7.1 %copy-start.18 = (bf16[12,128,1,128]{3,1,0,2:T(8,128)(2,1)}, bf16[12,128,1,128]{3,1,0,2:T(8,128)(2,1)S(1)}, u32[]{:S(2)}) copy-start(bf16[12,128,1,128]{3,1,0,2:T(8,128)(2,1)S(1)} %slice.195) | copy-start | bytes 1179652
  91.3 4.6 %copy-start.13 = (bf16[128,16,256]{0,2,1:T(8,128)(2,1)S(1)}, bf16[128,16,256]{0,2,1:T(8,128)(2,1)}, u32[]{:S(2)}) copy-start(bf16[128,16,256]{0,2,1:T(8,128)(2,1)} %copy-done.12) | copy-start | bytes 3145732
  109.3 4.0 %copy-start.17 = (bf16[2048,2,128]{2,0,1:T(8,128)(2,1)S(1)}, bf16[2048,2,128]{2,0,1:T(8,128)(2,1)}, u32[]{:S(2)}) copy-start(bf16[2048,2,128]{2,0,1:T(8,128)(2,1)} %copy.78) | copy-start | bytes 3145732
  109.3 4.1 %copy-start.26 = (pred[512,1024]{1,0:T(8,128)(4,1)S(1)}, pred[512,1024]{1,0:T(8,128)(4,1)}, u32[]{:S(2)}) copy-start(pred[512,1024]{1,0:T(8,128)(4,1)} %iota_compare_fusion.2) | copy-start | bytes 1572868
  109.3 4.2 %copy-start.29 = (bf16[8,128,1,128]{3,1,0,2:T(8,128)(2,1)S(1)}, bf16[8,128,1,128]{3,1,0,2:T(8,128)(2,1)}, u32[]{:S(2)}) copy-start(bf16[8,128,1,128]{3,1,0,2:T(8,128)(2,1)} %slice.192) | copy-start | bytes 786436
  109.3 4.1 %copy-start.34 = (f32[2,512]{1,0:T(2,128)S(1)}, f32[2,512]{1,0:T(2,128)}, u32[]{:S(2)}) copy-start(f32[2,512]{1,0:T(2,128)} %get-tuple-element.19) | copy-start | bytes 12292
  113.5 8.5 %slice-start = ((s8[8388608]{0:T(1024)(128)(4,1)}), s8[4194304]{0:T(1024)(128)(4,1)S(1)}, s32[]{:S(2)}) async-start(s8[8388608]{0:T(1024)(128)(4,1)} %bitcast.152), calls=%async_computation.7 | async-start | bytes 8388608
  115.4 6.6 %copy-start.7 = (bf16[2,512,1024]{2,1,0:T(8,128)(2,1)}, bf16[2,512,1024]{2,1,0:T(8,128)(2,1)S(1)}, u32[]{:S(2)}) copy-start(bf16[2,512,1024]{2,1,0:T(8,128)(2,1)S(1)} %multiply_convert_fusion.2) | copy-start | bytes 6291460
  115.4 6.6 %slice-start.1 = ((s8[8388608]{0:T(1024)(128)(4,1)}), s8[4194304]{0:T(1024)(128)(4,1)S(1)}, s32[]{:S(2)}) async-start(s8[8388608]{0:T(1024)(128)(4,1)} %bitcast.152), calls=%async_computation.8 | async-start | bytes 8388608
  116.8 5.2 %copy-start.23 = (pred[512,2048]{1,0:T(8,128)(4,1)S(1)}, pred[512,2048]{1,0:T(8,128)(4,1)}, u32[]{:S(2)}) copy-start(pred[512,2048]{1,0:T(8,128)(4,1)} %iota_compare_fusion) | copy-start | bytes 3145732
  125.2 9.2 %copy-start.33 = (f32[2,512]{1,0:T(2,128)S(1)}, f32[2,512]{1,0:T(2,128)}, u32[]{:S(2)}) copy-start(f32[2,512]{1,0:T(2,128)} %get-tuple-element.21) | copy-start | bytes 12292
  126.3 29.7 %all-to-all-start.6 = ((f32[16,128,128]{2,1,0:T(8,128)}), f32[16,128,128]{2,1,0:T(8,128)}, u32[]{:S(2)}, u32[]{:S(2)}) async-start(f32[16,128,128]{2,1,0:T(8,128)} %bitcast.51), calls=%async_computation.6 | async-start | bytes 2097152 | tf_op jit(solution)/shard_map/all_to_all | solution.py:104
  132.8 8.7 %slice-start.2 = ((s8[8388608]{0:T(1024)(128)(4,1)}), s8[4194304]{0:T(1024)(128)(4,1)S(1)}, s32[]{:S(2)}) async-start(s8[8388608]{0:T(1024)(128)(4,1)} %bitcast.154), calls=%async_computation.9 | async-start | bytes 8388608
  134.4 5.5 %copy-start.28 = (bf16[4,128,1,128]{3,1,0,2:T(8,128)(2,1)S(1)}, bf16[4,128,1,128]{3,1,0,2:T(8,128)(2,1)}, u32[]{:S(2)}) copy-start(bf16[4,128,1,128]{3,1,0,2:T(8,128)(2,1)} %copy-done.27) | copy-start | bytes 393220
  134.4 6.0 %copy-start.19 = (bf16[12,128,1,128]{3,1,0,2:T(8,128)(2,1)S(1)}, bf16[12,128,1,128]{3,1,0,2:T(8,128)(2,1)}, u32[]{:S(2)}) copy-start(bf16[12,128,1,128]{3,1,0,2:T(8,128)(2,1)} %copy-done.18) | copy-start | bytes 1179652
  134.4 7.1 %slice-start.3 = ((s8[8388608]{0:T(1024)(128)(4,1)}), s8[4194304]{0:T(1024)(128)(4,1)S(1)}, s32[]{:S(2)}) async-start(s8[8388608]{0:T(1024)(128)(4,1)} %bitcast.154), calls=%async_computation.10 | async-start | bytes 8388608
  148.5 13.5 %copy-start.3 = (bf16[2048,2,128]{2,0,1:T(8,128)(2,1)S(1)}, bf16[2048,2,128]{2,0,1:T(8,128)(2,1)}, u32[]{:S(2)}) copy-start(bf16[2048,2,128]{2,0,1:T(8,128)(2,1)} %copy-done.2) | copy-start | bytes 3145732
  156.0 28.9 %all-to-all-start.4 = ((bf16[16,128,256]{1,2,0:T(8,128)(2,1)}), bf16[16,128,256]{1,2,0:T(8,128)(2,1)}, u32[]{:S(2)}, u32[]{:S(2)}) async-start(bf16[16,128,256]{1,2,0:T(8,128)(2,1)} %copy.83), calls=%async_computation.4 | async-start | bytes 2097152 | tf_op jit(solution)/shard_map/all_to_all | solution.py:94
  167.7 47.1 %copy-start.1 = (bf16[128,512]{1,0:T(8,128)(2,1)S(1)}, bf16[128,512]{1,0:T(8,128)(2,1)}, u32[]{:S(2)}) copy-start(bf16[128,512]{1,0:T(8,128)(2,1)} %param.8) | copy-start | bytes 393220
  184.9 28.9 %all-to-all-start.5 = ((f32[16,128,128]{2,1,0:T(8,128)}), f32[16,128,128]{2,1,0:T(8,128)S(1)}, u32[]{:S(2)}, u32[]{:S(2)}) async-start(f32[16,128,128]{2,1,0:T(8,128)} %bitcast.42), calls=%async_computation.5 | async-start | bytes 2097152 | tf_op jit(solution)/shard_map/all_to_all | solution.py:97
  (14 other events, 38.5 us)
where the time goes:
time: 216 us; the launch traced here: 215 us
  waiting for transfers between devices  83.7 us (39%)
  matrix products  45.8 us (21%)
  starting transfers between devices  40.6 us (19%)
  local copies, waits for them, and re-layouts  33.2 us (15%)
  other arithmetic  10.1 us (5%)
    all_to_all x1, waiting for transfers between devices, per_device(): lax.all_to_all(key_accum.reshape(seq_count, local_rows, DH), 'seq', split...  18.4 us
    all_to_all x1, waiting for transfers between devices, per_device(): lax.all_to_all(out_split, 'seq', split_axis=1, concat_axis=0, tiled=True)  18 us
    all_to_all x1, waiting for transfers between devices, per_device(): lax.all_to_all(query_local, 'seq', split_axis=0, concat_axis=2, tiled=True)  16.2 us
    all_to_all x1, waiting for transfers between devices, per_device(): lax.all_to_all(value_send, 'seq', split_axis=1, concat_axis=0, tiled=True)  14.2 us
    all_to_all x1, waiting for transfers between devices, per_device(): lax.all_to_all(key_send, 'seq', split_axis=1, concat_axis=0, tiled=True)  13.1 us
    dot_general x4, matrix products, per_device(): jnp.einsum('hqd,kd->hqk', grad_block, values_seen, preferred_element_type...  12.9 us
    unnamed x85, local copies, waits for them, and re-layouts  12.7 us
    dot_general x4, matrix products, per_device(): jnp.einsum('hqk,hqd->kd', probs_low, grad_block, preferred_element_type=j...  12 us
  transfers between devices with their start and end apart: 7, of which 7 were waited for; matrix products, arithmetic and copies ran while one was open for 27% of the time, Pallas kernels for 0%

commit v1 on v0

v1 whole, which is shorter than its diff:
```python
import functools

import jax
import jax.numpy as jnp
from jax import lax
from jax.experimental import pallas as pl
from jax.experimental.pallas import tpu as pltpu
from jax.sharding import PartitionSpec as P

DH = 128
SCALE = DH ** (-0.5)
LOG2E = 1.4426950408889634
NT = (((1,), (1,)), ((), ()))
NN = (((1,), (0,)), ((), ()))
VMEM = pl.BlockSpec(memory_space=pltpu.VMEM)
SMEM = pl.BlockSpec(memory_space=pltpu.SMEM)
LIMIT = 56 << 20


def dot(a, b, dims):
    return lax.dot_general(a, b, dims, preferred_element_type=jnp.float32)


def call(body, out_shape, in_specs, out_specs, flops=0, exps=0, **kw):
    return pl.pallas_call(
        body,
        out_shape=out_shape,
        in_specs=in_specs,
        out_specs=out_specs,
        compiler_params=pltpu.CompilerParams(vmem_limit_bytes=LIMIT),
        cost_estimate=pl.CostEstimate(
            flops=flops, transcendentals=exps, bytes_accessed=4 << 20
        ),
        **kw,
    )


def pack(key, value, out, grad, seq_count, kv_heads, heads_here, pad):
    rows = key.shape[0]
    width = heads_here * DH
    group = heads_here * seq_count // kv_heads

    def body(k_ref, v_ref, o_ref, g_ref, grad_ref, kvd_ref):
        for d in range(seq_count):
            grad_ref[d] = g_ref[:, d * width : (d + 1) * width]
        for g in range(kv_heads):
            kvd_ref[g, :rows, :DH] = k_ref[:, g * DH : (g + 1) * DH]
            kvd_ref[g, :rows, DH:] = v_ref[:, g * DH : (g + 1) * DH]
            cols = []
            for h in range(g * group, (g + 1) * group):
                c = slice(h * DH, (h + 1) * DH)
                prod = g_ref[:, c].astype(jnp.float32) * o_ref[:, c].astype(jnp.float32)
                cols.append(jnp.sum(prod, axis=1, keepdims=True))
            cols.append(jnp.zeros((rows, pad - group), jnp.float32))
            delta = jnp.concatenate(cols, axis=1).T
            fill = jnp.zeros((pad, 2 * DH - rows), jnp.float32)
            kvd_ref[g, rows:, :] = jnp.concatenate([delta, fill], axis=1).astype(jnp.bfloat16)

    return call(
        body,
        (
            jax.ShapeDtypeStruct((seq_count, rows, width), jnp.bfloat16),
            jax.ShapeDtypeStruct((kv_heads, rows + pad, 2 * DH), jnp.bfloat16),
        ),
        [VMEM] * 4,
        (VMEM, VMEM),
    )(key, value, out, grad)


def unpack(pos, lse, pieces, rows, heads_here, kv_heads, pad):
    copies = len(pieces)
    total = rows * copies * kv_heads

    def body(pos_ref, lse_ref, *refs):
        ins, (kv_ref, kt_ref, delta_ref, lse_out) = refs[:copies], refs[copies:]
        plane, place = pos_ref[0], pos_ref[1]
        lse_out[...] = lse_ref[...] * LOG2E
        for s in range(copies):
            source = lax.rem(place - s + copies, copies)
            for r in range(kv_heads):
                owner = lax.rem(plane - r + kv_heads, kv_heads) * copies + source
                start = pl.multiple_of(owner * rows, rows)
                kv_ref[pl.ds(start, rows), :] = ins[s][r, :rows, :]
                low = ins[s][r, rows:, :rows].astype(jnp.float32)
                ids = lax.broadcasted_iota(jnp.int32, (pad, rows), 0)
                for h in range(heads_here):
                    mine = ids == place * heads_here + h
                    row = jnp.sum(jnp.where(mine, low, 0.0), axis=0, keepdims=True)
                    delta_ref[h : h + 1, pl.ds(start, rows)] = row
        kt_ref[...] = kv_ref[:, :DH].T

    return call(
        body,
        (
            jax.ShapeDtypeStruct((total, 2 * DH), jnp.bfloat16),
            jax.ShapeDtypeStruct((DH, total), jnp.bfloat16),
            jax.ShapeDtypeStruct((heads_here, total), jnp.float32),
            jax.ShapeDtypeStruct((heads_here, total), jnp.float32),
        ),
        [SMEM, VMEM] + [VMEM] * copies,
        (VMEM,) * 4,
    )(pos, lse, *pieces)


def probs_and_grads(kb, vb, qb, gb, lse, delta, k0, q0):
    s = dot(kb, qb, NT) * (SCALE * LOG2E) - lse
    if k0 + kb.shape[0] > q0:
        key_ids = k0 + lax.broadcasted_iota(jnp.int32, s.shape, 0)
        query_ids = q0 + lax.broadcasted_iota(jnp.int32, s.shape, 1)
        s = jnp.where(key_ids <= query_ids, s, -1e30)
    p = jnp.exp2(s)
    ds = (p * (dot(vb, gb, NT) - delta)).astype(jnp.bfloat16)
    return p, ds


def query_kernel(q, g, kv, kt, lse, delta, bq, bk):
    total = q.shape[0]
    heads = q.shape[1] // DH

    def body(q_ref, g_ref, kv_ref, kt_ref, l_ref, d_ref, o_ref):
        for q0 in range(0, total, bq):
            q1 = q0 + bq
            for h in range(heads):
                c = slice(h * DH, (h + 1) * DH)
                acc = None
                for k0 in range(0, q1, bk):
                    k1 = min(k0 + bk, q1)
                    _, ds = probs_and_grads(
                        kv_ref[k0:k1, :DH],
                        kv_ref[k0:k1, DH:],
                        q_ref[q0:q1, c],
                        g_ref[q0:q1, c],
                        l_ref[h : h + 1, q0:q1],
                        d_ref[h : h + 1, q0:q1],
                        k0,
                        q0,
                    )
                    t = dot(kt_ref[:, k0:k1], ds, NN)
                    acc = t if acc is None else acc + t
                o_ref[q0:q1, c] = (acc * SCALE).T.astype(jnp.bfloat16)

    return call(
        body,
        jax.ShapeDtypeStruct(q.shape, jnp.bfloat16),
        [VMEM] * 6,
        VMEM,
        flops=6 * heads * total * total * DH // 2,
        exps=heads * total * total // 2,
    )(q, g, kv, kt, lse, delta)


def key_kernel(pos, q, g, kv, lse, delta, rows, copies, bq, bk):
    total = q.shape[0]
    heads = q.shape[1] // DH
    planes = total // (rows * copies)

    def body(pos_ref, q_ref, g_ref, kv_ref, l_ref, d_ref, o_ref):
        place = pos_ref[1]
        for k0 in range(0, total, bk):
            k1 = k0 + bk
            dk = dv = None
            for q0 in range(k0, total, bq):
                q1 = q0 + bq
                for h in range(heads):
                    c = slice(h * DH, (h + 1) * DH)
                    qb, gb = q_ref[q0:q1, c], g_ref[q0:q1, c]
                    p, ds = probs_and_grads(
                        kv_ref[k0:k1, :DH],
                        kv_ref[k0:k1, DH:],
                        qb,
                        gb,
                        l_ref[h : h + 1, q0:q1],
                        d_ref[h : h + 1, q0:q1],
                        k0,
                        q0,
                    )
                    t = dot(p.astype(jnp.bfloat16), gb, NN)
                    dv = t if dv is None else dv + t
                    t = dot(ds, qb, NN)
                    dk = t if dk is None else dk + t
            both = jnp.concatenate([dk * SCALE, dv], axis=1).astype(jnp.bfloat16)
            for n in range(bk // rows):
                owner = k0 // rows + n
                slot = lax.rem(owner % copies - place + copies, copies)
                o_ref[slot, owner // copies] = both[n * rows : (n + 1) * rows]

    return call(
        body,
        jax.ShapeDtypeStruct((copies, planes, rows, 2 * DH), jnp.bfloat16),
        [SMEM] + [VMEM] * 5,
        VMEM,
        flops=8 * heads * total * total * DH // 2,
        exps=heads * total * total // 2,
    )(pos, q, g, kv, lse, delta)


def finish_kv(pos, blocks):
    kv_heads = len(blocks)
    rows = blocks[0].shape[0]

    def body(pos_ref, *refs):
        ins, (k_ref, v_ref) = refs[:kv_heads], refs[kv_heads:]
        for r in range(kv_heads):
            g = lax.rem(pos_ref[0] - r + kv_heads, kv_heads)
            cols = pl.ds(pl.multiple_of(g * DH, DH), DH)
            k_ref[:, cols] = ins[r][:, :DH]
            v_ref[:, cols] = ins[r][:, DH:]

    out = jax.ShapeDtypeStruct((rows, kv_heads * DH), jnp.bfloat16)
    return call(body, (out, out), [SMEM] + [VMEM] * kv_heads, (VMEM, VMEM))(pos, *blocks)


def per_device(query, key_seq, value_seq, attn_out, grad_out, lse):
    seq_count = lax.axis_size("seq")
    rows = key_seq.shape[0]
    total = rows * seq_count
    kv_heads = key_seq.shape[1] // DH
    heads_here = lse.shape[0]
    copies = seq_count // kv_heads
    group = heads_here * copies
    pad = -(-group // 16) * 16
    me = lax.axis_index("seq")
    plane, place = me // copies, me % copies
    pos = jnp.stack([plane, place]).astype(jnp.int32)

    def across(x, r):
        turn = [(j, (j + r * copies) % seq_count) for j in range(seq_count)]
        return lax.ppermute(x, "seq", turn)

    def inside(x, s):
        turn = [(j, j // copies * copies + (j + s) % copies) for j in range(seq_count)]
        return lax.ppermute(x, "seq", turn)

    grad_send, kvd = pack(
        key_seq, value_seq, attn_out, grad_out, seq_count, kv_heads, heads_here, pad
    )
    grad = lax.all_to_all(
        grad_send.reshape(total, heads_here * DH), "seq", split_axis=0, concat_axis=0, tiled=True
    )

    def pick(x, n):
        return lax.dynamic_index_in_dim(x, n % x.shape[0], 0, keepdims=False)

    got = [pick(kvd, plane)] + [across(pick(kvd, plane + r), r) for r in range(1, kv_heads)]
    mine = jnp.stack(got)
    pieces = [mine] + [inside(mine, s) for s in range(1, copies)]
    kv, kt, delta, lse2 = unpack(pos, lse, pieces, rows, heads_here, kv_heads, pad)

    big = min(512, total)
    query_local = query_kernel(query, grad, kv, kt, lse2, delta, big, min(1024, total))
    back = lax.all_to_all(query_local, "seq", split_axis=0, concat_axis=0, tiled=True)
    query_grad = (
        back.reshape(seq_count, rows, heads_here * DH)
        .transpose(1, 0, 2)
        .reshape(rows, seq_count * heads_here * DH)
    )
    partial = key_kernel(pos, query, grad, kv, lse2, delta, rows, copies, big, big)
    parts = [partial[0]] + [inside(partial[s], s) for s in range(1, copies)]
    summed = functools.reduce(
        lambda a, b: a + b, (part.astype(jnp.float32) for part in parts)
    ).astype(jnp.bfloat16)
    blocks = [pick(summed, plane)] + [
        across(pick(summed, plane + r), r) for r in range(1, kv_heads)
    ]
    key_grad, value_grad = finish_kv(pos, blocks)
    return query_grad, key_grad, value_grad


def solution(mesh):
    tokens = P(("dp", "seq"), None)
    return jax.shard_map(
        per_device,
        mesh=mesh,
        in_specs=(P("dp", "seq"), tokens, tokens, tokens, tokens, P("seq", "dp")),
        out_specs=(tokens, tokens, tokens),
        check_vma=False,
    )
```

time: 216 us -> 127 us (0.59)
  matrix products: 45.8 us -> 0 us
  Pallas kernels: 0 us -> 32.5 us
  waiting for transfers between devices: 83.7 us -> 55.7 us
  local copies, waits for them, and re-layouts: 33.2 us -> 5.92 us
  starting transfers between devices: 40.6 us -> 29.9 us
  other arithmetic: 10.1 us -> 1.79 us
    all_to_all x7 -> x2, waiting for transfers between devices: 83.7 us -> 0.01 us  [the longest x1 0.01 us: per_device(): lax.all_to_all(query_local, 'seq', split_axis=0, concat_axis=0, tiled=True)]
    ppermute x0 -> x12, waiting for transfers between devices: none -> 55.7 us  [the longest x6 33 us: across(): return lax.ppermute(x, 'seq', turn)]
    dot_general x20 -> x0, matrix products: 45.8 us -> none  [the longest x4 12.9 us: per_device(): jnp.einsum('hqd,kd->hqk', grad_block, values_seen, preferred_element_type...]
    pallas_call x0 -> x5, Pallas kernels: none -> 32.5 us  [the longest x1 13.9 us: key_kernel(): call(body, jax.ShapeDtypeStruct((copies, planes, rows, 2 * DH), jnp.bfloa...]
    all_to_all x7 -> x2, starting transfers between devices: 40.6 us -> 12.3 us  [the longest x1 8.44 us: per_device(): lax.all_to_all(grad_send.reshape(total, heads_here * DH), 'seq', split_ax...]
    ppermute x0 -> x12, starting transfers between devices: none -> 17.7 us  [the longest x6 9.39 us: across(): return lax.ppermute(x, 'seq', turn)]
    unnamed x85 -> x18, local copies, waits for them, and re-layouts: 12.7 us -> 3 us
    convert_element_type x4 -> x0, local copies, waits for them, and re-layouts: 5.56 us -> none  [the longest x2 5.3 us: per_device(): products = grad_heads.astype(jnp.float32) * out_heads.astype(jnp.float32)]
  transfers between devices with their start and end apart: 7 -> 14, of which waited for: 7 -> 9; matrix products, arithmetic and copies ran while one was open for 27% -> 3% of each run, Pallas kernels for 0% -> 14%
where the time goes in v1:
time: 127 us
  waiting for transfers between devices  55.7 us (44%)
  Pallas kernels  32.5 us (26%)
  starting transfers between devices  29.9 us (24%)
  local copies, waits for them, and re-layouts  5.92 us (5%)
  other arithmetic  1.79 us (1%)
    ppermute x6, waiting for transfers between devices, across(): return lax.ppermute(x, 'seq', turn)  33 us
    ppermute x6, waiting for transfers between devices, inside(): return lax.ppermute(x, 'seq', turn)  22.7 us
    pallas_call x1, Pallas kernels, key_kernel(): call(body, jax.ShapeDtypeStruct((copies, planes, rows, 2 * DH), jnp.bfloa...  13.9 us
    pallas_call x1, Pallas kernels, query_kernel(): call(body, jax.ShapeDtypeStruct(q.shape, jnp.bfloat16), [VMEM] * 6, VMEM,...  10.9 us
    ppermute x6, starting transfers between devices, across(): return lax.ppermute(x, 'seq', turn)  9.39 us
    all_to_all x1, starting transfers between devices, per_device(): lax.all_to_all(grad_send.reshape(total, heads_here * DH), 'seq', split_ax...  8.44 us
    ppermute x6, starting transfers between devices, inside(): return lax.ppermute(x, 'seq', turn)  8.27 us
    all_to_all x1, starting transfers between devices, per_device(): lax.all_to_all(query_local, 'seq', split_axis=0, concat_axis=0, tiled=True)  3.83 us
  transfers between devices with their start and end apart: 14, of which 9 were waited for; matrix products, arithmetic and copies ran while one was open for 3% of the time, Pallas kernels for 14%

profile of v1, /device:TPU:0, one launch (start us, length us, event | category | flops | bytes accessed | tf_op | source)
XLA Modules:
  0.0 126.6 jit_solution(13533604880824919687)
XLA Ops:
  0.6 3.5 %shard_map.85 = (bf16[16,128,256]{2,1,0:T(8,128)(2,1)}, bf16[4,144,256]{2,1,0:T(8,128)(2,1)}) custom-call(bf16[128,512]{1,0:T(8,128)(2,1)} %k_ref.1, bf16[128,512]{1,0:T(8,128)(2,1)} %v_ref.1, bf16[128,4096]{1,0:T(8,128)(2,1)} %o_ref.1, bf16[128,4096]{1,0:T(8,128)(2,1)} %g_ref.1), custom_call_target="tpu_custom_call" | custom-call | bytes 4194304 | tf_op jit(solution)/shard_map/pallas_call | solution.py:59
  4.1 8.4 %all-to-all-start = ((bf16[16,128,256]{2,1,0:T(8,128)(2,1)}), bf16[16,128,256]{2,1,0:T(8,128)(2,1)S(1)}, u32[]{:S(2)}, u32[]{:S(2)}) async-start(bf16[16,128,256]{2,1,0:T(8,128)(2,1)} %get-tuple-element.11), calls=%async_computation | async-start | bytes 2097152 | tf_op jit(solution)/shard_map/all_to_all | solution.py:237
  12.7 3.7 %collective-permute-start.2 = (bf16[144,256]{1,0:T(8,128)(2,1)S(1)}, bf16[144,256]{1,0:T(8,128)(2,1)S(1)}, u32[]{:S(2)}, u32[]{:S(2)}) collective-permute-start(bf16[144,256]{1,0:T(8,128)(2,1)S(1)} %get-tuple-element.23), channel_id=1, source_target_pairs={{0,12},{1,13},{2,14},{3,15},{4,0},{5,1},{6,2},{7,3},{8,4},{9,5},{1... | collective-permute-start | bytes 221192 | tf_op jit(solution)/shard_map/ppermute | solution.py:228
  16.4 1.1 collective-permute-start
  17.5 14.8 %collective-permute-done.2 = bf16[144,256]{1,0:T(8,128)(2,1)S(1)} collective-permute-done((bf16[144,256]{1,0:T(8,128)(2,1)S(1)}, bf16[144,256]{1,0:T(8,128)(2,1)S(1)}, u32[]{:S(2)}, u32[]{:S(2)}) %collective-permute-start.2) | collective-permute-done | bytes 73760 | tf_op jit(solution)/shard_map/ppermute | solution.py:228
  32.3 12.3 %collective-permute-done.1 = bf16[144,256]{1,0:T(8,128)(2,1)S(1)} collective-permute-done((bf16[144,256]{1,0:T(8,128)(2,1)S(1)}, bf16[144,256]{1,0:T(8,128)(2,1)S(1)}, u32[]{:S(2)}, u32[]{:S(2)}) %collective-permute-start.1) | collective-permute-done | bytes 73760 | tf_op jit(solution)/shard_map/ppermute | solution.py:228
  44.6 2.5 %collective-permute-start.5 = (bf16[4,144,256]{2,1,0:T(8,128)(2,1)S(1)}, bf16[4,144,256]{2,1,0:T(8,128)(2,1)S(1)}, u32[]{:S(2)}, u32[]{:S(2)}) collective-permute-start(bf16[4,144,256]{2,1,0:T(8,128)(2,1)S(1)} %pad_maximum_fusion.refs_0_), channel_id=1, source_target_pairs={{0,3},{1,0},{2,1},{3,2},{4,7},{5,4},{6,5},{7,6},{8,11},{9,8},{10,9... | collective-permute-start | bytes 884744 | tf_op jit(solution)/shard_map/ppermute | solution.py:232
  47.6 0.7 collective-permute-start.3
  48.3 0.7 pad_add_fusion.pos_ref
  48.9 5.7 %collective-permute-done.5.refs_3_ = bf16[4,144,256]{2,1,0:T(8,128)(2,1)S(1)} collective-permute-done((bf16[4,144,256]{2,1,0:T(8,128)(2,1)S(1)}, bf16[4,144,256]{2,1,0:T(8,128)(2,1)S(1)}, u32[]{:S(2)}, u32[]{:S(2)}) %collective-permute-start.5) | collective-permute-done | bytes 294944 | tf_op jit(solution)/shard_map/ppermute | solution.py:232
  54.6 6.2 %collective-permute-done.4.refs_2_ = bf16[4,144,256]{2,1,0:T(8,128)(2,1)S(1)} collective-permute-done((bf16[4,144,256]{2,1,0:T(8,128)(2,1)S(1)}, bf16[4,144,256]{2,1,0:T(8,128)(2,1)S(1)}, u32[]{:S(2)}, u32[]{:S(2)}) %collective-permute-start.4) | collective-permute-done | bytes 294944 | tf_op jit(solution)/shard_map/ppermute | solution.py:232
  60.9 0.7 copy-done.4
  61.6 0.7 copy-done.5
  62.3 2.5 %shard_map.86 = (bf16[2048,256]{1,0:T(8,128)(2,1)}, bf16[128,2048]{1,0:T(8,128)(2,1)}, f32[2,2048]{1,0:T(2,128)}, f32[2,2048]{1,0:T(2,128)}) custom-call(s32[2]{0:T(128)} %pad_add_fusion.pos_ref, f32[2,2048]{1,0:T(2,128)} %lse_ref.1, bf16[4,144,256]{2,1,0:T(8,128)(2,1)} %copy-done, bf16[4,144,256]{2,1,0:T(8,128)(2,1)} %copy-done.5, ...), custom_call_target="tpu_custom_call" | custom-call | bytes 4194304 | tf_op jit(solution)/shard_map/pallas_call | solution.py:92
  64.8 1.0 copy-done.1
  65.7 10.9 %shard_map.87 = bf16[2048,256]{1,0:T(8,128)(2,1)} custom-call(bf16[2048,256]{1,0:T(8,128)(2,1)} %q_ref.3, bf16[2048,256]{1,0:T(8,128)(2,1)} %bitcast.36, bf16[2048,256]{1,0:T(8,128)(2,1)} %get-tuple-element.13.kv_ref, bf16[128,2048]{1,0:T(8,128)(2,1)} %get-tuple-element.14.kt_ref, f32[2,2048]{1,0:T(2,128)} %get-tuple-element.15.l_ref, ...), custom_call_target="tpu_custom_call" | custom-call | flops 3221225472 | bytes 4194304 | tf_op jit(solution)/shard_map/pallas_call | solution.py:142
  76.6 3.8 %all-to-all-start.1 = ((bf16[16,128,256]{2,1,0:T(8,128)(2,1)}), bf16[16,128,256]{2,1,0:T(8,128)(2,1)S(1)}, u32[]{:S(2)}, u32[]{:S(2)}) async-start(bf16[16,128,256]{2,1,0:T(8,128)(2,1)} %bitcast.38), calls=%async_computation.1 | async-start | bytes 2097152 | tf_op jit(solution)/shard_map/all_to_all | solution.py:251
  80.5 13.9 %shard_map.88 = bf16[4,4,128,256]{3,2,1,0:T(8,128)(2,1)} custom-call(s32[2]{0:T(128)} %pad_add_fusion.pos_ref, bf16[2048,256]{1,0:T(8,128)(2,1)} %q_ref.3, bf16[2048,256]{1,0:T(8,128)(2,1)} %bitcast.37, bf16[2048,256]{1,0:T(8,128)(2,1)} %get-tuple-element.13.kv_ref, f32[2,2048]{1,0:T(2,128)} %get-tuple-element.15.l_ref, f32[2,2048]{1,0:T(2,128)} %get-tuple-element.16.d_ref), custom_call_target="tpu_custom_call" | custom-call | flops 4294967296 | bytes 4194304 | tf_op jit(solution)/shard_map/pallas_call | solution.py:187
  94.4 1.2 slice_bitcast_fusion.2
  95.6 1.7 %collective-permute-start.6 = (bf16[4,128,256]{2,1,0:T(8,128)(2,1)S(1)}, bf16[4,128,256]{2,1,0:T(8,128)(2,1)S(1)}, u32[]{:S(2)}, u32[]{:S(2)}) collective-permute-start(bf16[4,128,256]{2,1,0:T(8,128)(2,1)S(1)} %get-tuple-element.19), channel_id=1, source_target_pairs={{0,1},{1,2},{2,3},{3,0},{4,5},{5,6},{6,7},{7,4},{8,9},{9,10},{10,1... | collective-permute-start | bytes 786440 | tf_op jit(solution)/shard_map/ppermute | solution.py:232
  97.2 1.3 %collective-permute-start.8 = (bf16[4,128,256]{2,1,0:T(8,128)(2,1)S(1)}, bf16[4,128,256]{2,1,0:T(8,128)(2,1)S(1)}, u32[]{:S(2)}, u32[]{:S(2)}) collective-permute-start(bf16[4,128,256]{2,1,0:T(8,128)(2,1)S(1)} %get-tuple-element.20), channel_id=1, source_target_pairs={{0,3},{1,0},{2,1},{3,2},{4,7},{5,4},{6,5},{7,6},{8,11},{9,8},{10,9... | collective-permute-start | bytes 786440 | tf_op jit(solution)/shard_map/ppermute | solution.py:232
  98.5 1.6 %collective-permute-start.7 = (bf16[4,128,256]{2,1,0:T(8,128)(2,1)S(1)}, bf16[4,128,256]{2,1,0:T(8,128)(2,1)S(1)}, u32[]{:S(2)}, u32[]{:S(2)}) collective-permute-start(bf16[4,128,256]{2,1,0:T(8,128)(2,1)S(1)} %get-tuple-element.21), channel_id=1, source_target_pairs={{0,2},{1,3},{2,0},{3,1},{4,6},{5,7},{6,4},{7,5},{8,10},{9,11},{10,... | collective-permute-start | bytes 786440 | tf_op jit(solution)/shard_map/ppermute | solution.py:232
  100.2 7.3 %collective-permute-done.6 = bf16[4,128,256]{2,1,0:T(8,128)(2,1)S(1)} collective-permute-done((bf16[4,128,256]{2,1,0:T(8,128)(2,1)S(1)}, bf16[4,128,256]{2,1,0:T(8,128)(2,1)S(1)}, u32[]{:S(2)}, u32[]{:S(2)}) %collective-permute-start.6) | collective-permute-done | bytes 262176 | tf_op jit(solution)/shard_map/ppermute | solution.py:232
  107.5 3.4 %collective-permute-done.8 = bf16[4,128,256]{2,1,0:T(8,128)(2,1)S(1)} collective-permute-done((bf16[4,128,256]{2,1,0:T(8,128)(2,1)S(1)}, bf16[4,128,256]{2,1,0:T(8,128)(2,1)S(1)}, u32[]{:S(2)}, u32[]{:S(2)}) %collective-permute-start.8) | collective-permute-done | bytes 262176 | tf_op jit(solution)/shard_map/ppermute | solution.py:232
  110.9 1.1 fusion.2
  112.0 0.7 dynamic-slice_bitcast_fusion.3
  112.7 4.0 %collective-permute-start.11 = (bf16[128,256]{1,0:T(8,128)(2,1)S(1)}, bf16[128,256]{1,0:T(8,128)(2,1)S(1)}, u32[]{:S(2)}, u32[]{:S(2)}) collective-permute-start(bf16[128,256]{1,0:T(8,128)(2,1)S(1)} %get-tuple-element.26), channel_id=1, source_target_pairs={{0,12},{1,13},{2,14},{3,15},{4,0},{5,1},{6,2},{7,3},{8,4},{9,5},{1... | collective-permute-start | bytes 196616 | tf_op jit(solution)/shard_map/ppermute | solution.py:228
  117.3 1.3 %collective-permute-done.11.refs_3_ = bf16[128,256]{1,0:T(8,128)(2,1)S(1)} collective-permute-done((bf16[128,256]{1,0:T(8,128)(2,1)S(1)}, bf16[128,256]{1,0:T(8,128)(2,1)S(1)}, u32[]{:S(2)}, u32[]{:S(2)}) %collective-permute-start.11) | collective-permute-done | bytes 65568 | tf_op jit(solution)/shard_map/ppermute | solution.py:228
  118.6 3.3 %collective-permute-done.10.refs_2_ = bf16[128,256]{1,0:T(8,128)(2,1)S(1)} collective-permute-done((bf16[128,256]{1,0:T(8,128)(2,1)S(1)}, bf16[128,256]{1,0:T(8,128)(2,1)S(1)}, u32[]{:S(2)}, u32[]{:S(2)}) %collective-permute-start.10) | collective-permute-done | bytes 65568 | tf_op jit(solution)/shard_map/ppermute | solution.py:228
  121.9 1.3 %collective-permute-done.9.refs_1_ = bf16[128,256]{1,0:T(8,128)(2,1)S(1)} collective-permute-done((bf16[128,256]{1,0:T(8,128)(2,1)S(1)}, bf16[128,256]{1,0:T(8,128)(2,1)S(1)}, u32[]{:S(2)}, u32[]{:S(2)}) %collective-permute-start.9) | collective-permute-done | bytes 65568 | tf_op jit(solution)/shard_map/ppermute | solution.py:228
  123.8 1.7 %shard_map.89 = (bf16[128,512]{1,0:T(8,128)(2,1)}, bf16[128,512]{1,0:T(8,128)(2,1)}) custom-call(s32[2]{0:T(128)} %pad_add_fusion.pos_ref, bf16[128,256]{1,0:T(8,128)(2,1)} %get-tuple-element.29.refs_0_, bf16[128,256]{1,0:T(8,128)(2,1)} %copy-done.8, bf16[128,256]{1,0:T(8,128)(2,1)} %copy-done.7, bf16[128,256]{1,0:T(8,128)(2,1)} %copy-done.6), custom_call_target="tpu_custom_call" | custom-call | bytes 4194304 | tf_op jit(solution)/shard_map/pallas_call | solution.py:210
  125.5 1.1 copy.10
  (26 shorter events, 1.7 us)
Async XLA Ops:
  4.1 8.6 %copy-start.2 = (bf16[4,144,256]{2,1,0:T(8,128)(2,1)S(1)}, bf16[4,144,256]{2,1,0:T(8,128)(2,1)}, u32[]{:S(2)}) copy-start(bf16[4,144,256]{2,1,0:T(8,128)(2,1)} %get-tuple-element.12) | copy-start | bytes 884740
  4.1 60.7 %all-to-all-start = ((bf16[16,128,256]{2,1,0:T(8,128)(2,1)}), bf16[16,128,256]{2,1,0:T(8,128)(2,1)S(1)}, u32[]{:S(2)}, u32[]{:S(2)}) async-start(bf16[16,128,256]{2,1,0:T(8,128)(2,1)} %get-tuple-element.11), calls=%async_computation | async-start | bytes 2097152 | tf_op jit(solution)/shard_map/all_to_all | solution.py:237
  12.7 19.6 %collective-permute-start.2 = (bf16[144,256]{1,0:T(8,128)(2,1)S(1)}, bf16[144,256]{1,0:T(8,128)(2,1)S(1)}, u32[]{:S(2)}, u32[]{:S(2)}) collective-permute-start(bf16[144,256]{1,0:T(8,128)(2,1)S(1)} %get-tuple-element.23), channel_id=1, source_target_pairs={{0,12},{1,13},{2,14},{3,15},{4,0},{5,1},{6,2},{7,3},{8,4},{9,5},{1... | collective-permute-start | bytes 221192 | tf_op jit(solution)/shard_map/ppermute | solution.py:228
  16.4 28.2 %collective-permute-start.1 = (bf16[144,256]{1,0:T(8,128)(2,1)S(1)}, bf16[144,256]{1,0:T(8,128)(2,1)S(1)}, u32[]{:S(2)}, u32[]{:S(2)}) collective-permute-start(bf16[144,256]{1,0:T(8,128)(2,1)S(1)} %get-tuple-element.24), channel_id=1, source_target_pairs={{0,8},{1,9},{2,10},{3,11},{4,12},{5,13},{6,14},{7,15},{8,0},{9,1},... | collective-permute-start | bytes 221192 | tf_op jit(solution)/shard_map/ppermute | solution.py:228
  16.4 28.2 %collective-permute-start = (bf16[144,256]{1,0:T(8,128)(2,1)S(1)}, bf16[144,256]{1,0:T(8,128)(2,1)S(1)}, u32[]{:S(2)}, u32[]{:S(2)}) collective-permute-start(bf16[144,256]{1,0:T(8,128)(2,1)S(1)} %get-tuple-element.25), channel_id=1, source_target_pairs={{0,4},{1,5},{2,6},{3,7},{4,8},{5,9},{6,10},{7,11},{8,12},{9,13},{1... | collective-permute-start | bytes 221192 | tf_op jit(solution)/shard_map/ppermute | solution.py:228
  44.6 16.3 %copy-start = (bf16[4,144,256]{2,1,0:T(8,128)(2,1)}, bf16[4,144,256]{2,1,0:T(8,128)(2,1)S(1)}, u32[]{:S(2)}) copy-start(bf16[4,144,256]{2,1,0:T(8,128)(2,1)S(1)} %pad_maximum_fusion.refs_0_) | copy-start | bytes 884740
  44.6 10.0 %collective-permute-start.5 = (bf16[4,144,256]{2,1,0:T(8,128)(2,1)S(1)}, bf16[4,144,256]{2,1,0:T(8,128)(2,1)S(1)}, u32[]{:S(2)}, u32[]{:S(2)}) collective-permute-start(bf16[4,144,256]{2,1,0:T(8,128)(2,1)S(1)} %pad_maximum_fusion.refs_0_), channel_id=1, source_target_pairs={{0,3},{1,0},{2,1},{3,2},{4,7},{5,4},{6,5},{7,6},{8,11},{9,8},{10,9... | collective-permute-start | bytes 884744 | tf_op jit(solution)/shard_map/ppermute | solution.py:232
  47.1 13.7 %collective-permute-start.4 = (bf16[4,144,256]{2,1,0:T(8,128)(2,1)S(1)}, bf16[4,144,256]{2,1,0:T(8,128)(2,1)S(1)}, u32[]{:S(2)}, u32[]{:S(2)}) collective-permute-start(bf16[4,144,256]{2,1,0:T(8,128)(2,1)S(1)} %pad_maximum_fusion.refs_0_), channel_id=1, source_target_pairs={{0,2},{1,3},{2,0},{3,1},{4,6},{5,7},{6,4},{7,5},{8,10},{9,11},{10,... | collective-permute-start | bytes 884744 | tf_op jit(solution)/shard_map/ppermute | solution.py:232
  47.6 13.3 %collective-permute-start.3 = (bf16[4,144,256]{2,1,0:T(8,128)(2,1)S(1)}, bf16[4,144,256]{2,1,0:T(8,128)(2,1)S(1)}, u32[]{:S(2)}, u32[]{:S(2)}) collective-permute-start(bf16[4,144,256]{2,1,0:T(8,128)(2,1)S(1)} %pad_maximum_fusion.refs_0_), channel_id=1, source_target_pairs={{0,1},{1,2},{2,3},{3,0},{4,5},{5,6},{6,7},{7,4},{8,9},{9,10},{10,1... | collective-permute-start | bytes 884744 | tf_op jit(solution)/shard_map/ppermute | solution.py:232
  54.6 6.3 %copy-start.3 = (bf16[4,144,256]{2,1,0:T(8,128)(2,1)}, bf16[4,144,256]{2,1,0:T(8,128)(2,1)S(1)}, u32[]{:S(2)}) copy-start(bf16[4,144,256]{2,1,0:T(8,128)(2,1)S(1)} %collective-permute-done.5.refs_3_) | copy-start | bytes 884740
  60.9 0.7 copy-start.4
  61.6 0.7 copy-start.5
  64.8 1.0 copy-start.1
  76.6 48.9 %all-to-all-start.1 = ((bf16[16,128,256]{2,1,0:T(8,128)(2,1)}), bf16[16,128,256]{2,1,0:T(8,128)(2,1)S(1)}, u32[]{:S(2)}, u32[]{:S(2)}) async-start(bf16[16,128,256]{2,1,0:T(8,128)(2,1)} %bitcast.38), calls=%async_computation.1 | async-start | bytes 2097152 | tf_op jit(solution)/shard_map/all_to_all | solution.py:251
  95.6 11.9 %collective-permute-start.6 = (bf16[4,128,256]{2,1,0:T(8,128)(2,1)S(1)}, bf16[4,128,256]{2,1,0:T(8,128)(2,1)S(1)}, u32[]{:S(2)}, u32[]{:S(2)}) collective-permute-start(bf16[4,128,256]{2,1,0:T(8,128)(2,1)S(1)} %get-tuple-element.19), channel_id=1, source_target_pairs={{0,1},{1,2},{2,3},{3,0},{4,5},{5,6},{6,7},{7,4},{8,9},{9,10},{10,1... | collective-permute-start | bytes 786440 | tf_op jit(solution)/shard_map/ppermute | solution.py:232
  97.2 13.7 %collective-permute-start.8 = (bf16[4,128,256]{2,1,0:T(8,128)(2,1)S(1)}, bf16[4,128,256]{2,1,0:T(8,128)(2,1)S(1)}, u32[]{:S(2)}, u32[]{:S(2)}) collective-permute-start(bf16[4,128,256]{2,1,0:T(8,128)(2,1)S(1)} %get-tuple-element.20), channel_id=1, source_target_pairs={{0,3},{1,0},{2,1},{3,2},{4,7},{5,4},{6,5},{7,6},{8,11},{9,8},{10,9... | collective-permute-start | bytes 786440 | tf_op jit(solution)/shard_map/ppermute | solution.py:232
  98.5 12.4 %collective-permute-start.7 = (bf16[4,128,256]{2,1,0:T(8,128)(2,1)S(1)}, bf16[4,128,256]{2,1,0:T(8,128)(2,1)S(1)}, u32[]{:S(2)}, u32[]{:S(2)}) collective-permute-start(bf16[4,128,256]{2,1,0:T(8,128)(2,1)S(1)} %get-tuple-element.21), channel_id=1, source_target_pairs={{0,2},{1,3},{2,0},{3,1},{4,6},{5,7},{6,4},{7,5},{8,10},{9,11},{10,... | collective-permute-start | bytes 786440 | tf_op jit(solution)/shard_map/ppermute | solution.py:232
  112.7 5.9 %collective-permute-start.11 = (bf16[128,256]{1,0:T(8,128)(2,1)S(1)}, bf16[128,256]{1,0:T(8,128)(2,1)S(1)}, u32[]{:S(2)}, u32[]{:S(2)}) collective-permute-start(bf16[128,256]{1,0:T(8,128)(2,1)S(1)} %get-tuple-element.26), channel_id=1, source_target_pairs={{0,12},{1,13},{2,14},{3,15},{4,0},{5,1},{6,2},{7,3},{8,4},{9,5},{1... | collective-permute-start | bytes 196616 | tf_op jit(solution)/shard_map/ppermute | solution.py:228
  116.7 5.2 %collective-permute-start.10 = (bf16[128,256]{1,0:T(8,128)(2,1)S(1)}, bf16[128,256]{1,0:T(8,128)(2,1)S(1)}, u32[]{:S(2)}, u32[]{:S(2)}) collective-permute-start(bf16[128,256]{1,0:T(8,128)(2,1)S(1)} %get-tuple-element.27), channel_id=1, source_target_pairs={{0,8},{1,9},{2,10},{3,11},{4,12},{5,13},{6,14},{7,15},{8,0},{9,1},... | collective-permute-start | bytes 196616 | tf_op jit(solution)/shard_map/ppermute | solution.py:228
  117.1 6.1 %collective-permute-start.9 = (bf16[128,256]{1,0:T(8,128)(2,1)S(1)}, bf16[128,256]{1,0:T(8,128)(2,1)S(1)}, u32[]{:S(2)}, u32[]{:S(2)}) collective-permute-start(bf16[128,256]{1,0:T(8,128)(2,1)S(1)} %get-tuple-element.28), channel_id=1, source_target_pairs={{0,4},{1,5},{2,6},{3,7},{4,8},{5,9},{6,10},{7,11},{8,12},{9,13},{1... | collective-permute-start | bytes 196616 | tf_op jit(solution)/shard_map/ppermute | solution.py:228
  118.6 4.6 %copy-start.6 = (bf16[128,256]{1,0:T(8,128)(2,1)}, bf16[128,256]{1,0:T(8,128)(2,1)S(1)}, u32[]{:S(2)}) copy-start(bf16[128,256]{1,0:T(8,128)(2,1)S(1)} %collective-permute-done.11.refs_3_) | copy-start | bytes 196612
  121.9 1.4 %copy-start.7 = (bf16[128,256]{1,0:T(8,128)(2,1)}, bf16[128,256]{1,0:T(8,128)(2,1)S(1)}, u32[]{:S(2)}) copy-start(bf16[128,256]{1,0:T(8,128)(2,1)S(1)} %collective-permute-done.10.refs_2_) | copy-start | bytes 196612
  123.2 0.6 copy-start.8

commit v2 on v1

v2 whole, which is shorter than its diff:
```python
import functools

import jax
import jax.numpy as jnp
from jax import lax
from jax.experimental import pallas as pl
from jax.experimental.pallas import tpu as pltpu
from jax.sharding import PartitionSpec as P

DH = 128
SCALE = DH ** (-0.5)
LOG2E = 1.4426950408889634
NT = (((1,), (1,)), ((), ()))
NN = (((1,), (0,)), ((), ()))
VMEM = pl.BlockSpec(memory_space=pltpu.VMEM)
SMEM = pl.BlockSpec(memory_space=pltpu.SMEM)
LIMIT = 56 << 20


def dot(a, b, dims):
    return lax.dot_general(a, b, dims, preferred_element_type=jnp.float32)


def call(body, out_shape, in_specs, out_specs, flops=0, exps=0, **kw):
    return pl.pallas_call(
        body,
        out_shape=out_shape,
        in_specs=in_specs,
        out_specs=out_specs,
        compiler_params=pltpu.CompilerParams(vmem_limit_bytes=LIMIT),
        cost_estimate=pl.CostEstimate(
            flops=flops, transcendentals=exps, bytes_accessed=4 << 20
        ),
        **kw,
    )


def pack(out, grad, seq_count, heads_here, pad):
    rows = grad.shape[0]
    width = heads_here * DH
    steps = 4 if seq_count % 4 == 0 else 1
    here = seq_count // steps

    def body(o_ref, g_ref, send_ref):
        for d in range(here):
            c = slice(d * width, (d + 1) * width)
            block = g_ref[:, c]
            send_ref[d, :rows] = block
            prod = block.astype(jnp.float32) * o_ref[:, c].astype(jnp.float32)
            sums = [
                jnp.sum(prod[:, h * DH : (h + 1) * DH], axis=1, keepdims=True)
                for h in range(heads_here)
            ]
            sums.append(jnp.zeros((rows, pad - heads_here), jnp.float32))
            delta = jnp.concatenate(sums, axis=1).T
            if width > rows:
                fill = jnp.zeros((pad, width - rows), jnp.float32)
                delta = jnp.concatenate([delta, fill], axis=1)
            send_ref[d, rows:] = delta.astype(jnp.bfloat16)

    many = pl.BlockSpec((rows, here * width), lambda n: (0, n))
    return call(
        body,
        jax.ShapeDtypeStruct((seq_count, rows + pad, width), jnp.bfloat16),
        [many, many],
        pl.BlockSpec((here, rows + pad, width), lambda n: (n, 0, 0)),
        grid=(steps,),
    )(out, grad)


def unpack(pos, lse, pieces):
    copies = len(pieces)
    kv_heads, rows, width = pieces[0].shape
    total = rows * copies * kv_heads

    def body(pos_ref, lse_ref, *refs):
        ins, (kv_ref, kt_ref, lse_out) = refs[:copies], refs[copies:]
        plane, place = pos_ref[0], pos_ref[1]
        lse_out[...] = lse_ref[...] * LOG2E
        for s in range(copies):
            source = lax.rem(place - s + copies, copies)
            for r in range(kv_heads):
                owner = lax.rem(plane - r + kv_heads, kv_heads) * copies + source
                start = pl.multiple_of(owner * rows, rows)
                kv_ref[pl.ds(start, rows), :] = ins[s][r]
        kt_ref[...] = kv_ref[:, :DH].T

    return call(
        body,
        (
            jax.ShapeDtypeStruct((total, width), jnp.bfloat16),
            jax.ShapeDtypeStruct((DH, total), jnp.bfloat16),
            jax.ShapeDtypeStruct(lse.shape, jnp.float32),
        ),
        [SMEM, VMEM] + [VMEM] * copies,
        (VMEM,) * 3,
        flops=int(40e9),
    )(pos, lse, *pieces)


def attend(pos, q, g, kv, kt, lse, rows, copies, block):
    total = q.shape[0]
    width = q.shape[1]
    heads = width // DH
    planes = total // (rows * copies)
    owners = block // rows

    def body(pos_ref, q_ref, g_ref, kv_ref, kt_ref, l_ref, dq_ref, *refs):
        slots, (acc_ref, dkv_ref, d_ref) = refs[:copies], refs[copies:]
        for n in range(total // rows):
            d_ref[:, n * rows : (n + 1) * rows] = g_ref[n, rows:, :rows].astype(jnp.float32)
        for k0 in range(0, total, block):
            k1 = k0 + block
            kb, vb = kv_ref[k0:k1, :DH], kv_ref[k0:k1, DH:]
            dk = dv = None
            for q0 in range(k0, total, block):
                q1 = q0 + block
                n0 = q0 // rows
                for h in range(heads):
                    c = slice(h * DH, (h + 1) * DH)
                    qb = q_ref[q0:q1, c]
                    gb = g_ref[n0 : n0 + owners, :rows, c].reshape(block, DH)
                    s = dot(kb, qb, NT) * (SCALE * LOG2E) - l_ref[h : h + 1, q0:q1]
                    if k1 > q0:
                        key_ids = k0 + lax.broadcasted_iota(jnp.int32, s.shape, 0)
                        query_ids = q0 + lax.broadcasted_iota(jnp.int32, s.shape, 1)
                        s = jnp.where(key_ids <= query_ids, s, -1e30)
                    p = jnp.exp2(s)
                    t = dot(p.astype(jnp.bfloat16), gb, NN)
                    dv = t if dv is None else dv + t
                    ds = p * (dot(vb, gb, NT) - d_ref[h : h + 1, q0:q1])
                    ds = ds.astype(jnp.bfloat16)
                    t = dot(ds, qb, NN)
                    dk = t if dk is None else dk + t
                    t = dot(kt_ref[:, k0:k1], ds, NN)
                    if k0 == 0:
                        acc_ref[c, q0:q1] = t
                    else:
                        acc_ref[c, q0:q1] += t
            dkv_ref[k0:k1, :DH] = (dk * SCALE).astype(jnp.bfloat16)
            dkv_ref[k0:k1, DH:] = dv.astype(jnp.bfloat16)
        for h in range(heads):
            c = slice(h * DH, (h + 1) * DH)
            for q0 in range(0, total, block):
                q1 = q0 + block
                dq_ref[q0:q1, c] = (acc_ref[c, q0:q1] * SCALE).T.astype(jnp.bfloat16)
        for s in range(copies):
            target = lax.rem(pos_ref[1] + s, copies)
            for r in range(planes):
                start = pl.multiple_of((r * copies + target) * rows, rows)
                slots[s][r] = dkv_ref[pl.ds(start, rows), :]

    part = jax.ShapeDtypeStruct((planes, rows, 2 * DH), jnp.bfloat16)
    return call(
        body,
        (jax.ShapeDtypeStruct((total, width), jnp.bfloat16),) + (part,) * copies,
        [SMEM] + [VMEM] * 5,
        (VMEM,) * (1 + copies),
        flops=10 * heads * total * total * DH // 2,
        exps=heads * total * total // 2,
        scratch_shapes=[
            pltpu.VMEM((width, total), jnp.float32),
            pltpu.VMEM((total, 2 * DH), jnp.bfloat16),
            pltpu.VMEM((g.shape[1] - rows, total), jnp.float32),
        ],
    )(pos, q, g, kv, kt, lse)


def finish_kv(pos, blocks):
    kv_heads = len(blocks)
    rows = blocks[0].shape[0]

    def body(pos_ref, *refs):
        ins, (k_ref, v_ref) = refs[:kv_heads], refs[kv_heads:]
        for r in range(kv_heads):
            g = lax.rem(pos_ref[0] - r + kv_heads, kv_heads)
            cols = pl.ds(pl.multiple_of(g * DH, DH), DH)
            k_ref[:, cols] = ins[r][:, :DH]
            v_ref[:, cols] = ins[r][:, DH:]

    out = jax.ShapeDtypeStruct((rows, kv_heads * DH), jnp.bfloat16)
    return call(body, (out, out), [SMEM] + [VMEM] * kv_heads, (VMEM, VMEM), flops=int(16e9))(pos, *blocks)


def per_device(query, key_seq, value_seq, attn_out, grad_out, lse):
    seq_count = lax.axis_size("seq")
    rows = key_seq.shape[0]
    total = rows * seq_count
    kv_heads = key_seq.shape[1] // DH
    heads_here = lse.shape[0]
    copies = seq_count // kv_heads
    pad = -(-heads_here // 8) * 8
    me = lax.axis_index("seq")
    plane, place = me // copies, me % copies
    pos = jnp.stack([plane, place]).astype(jnp.int32)

    def across(x, r):
        turn = [(j, (j + r * copies) % seq_count) for j in range(seq_count)]
        return lax.ppermute(x, "seq", turn)

    def inside(x, s):
        turn = [(j, j // copies * copies + (j + s) % copies) for j in range(seq_count)]
        return lax.ppermute(x, "seq", turn)

    def columns(x, n):
        return lax.dynamic_slice_in_dim(x, n % kv_heads * DH, DH, axis=1)

    def pick(x, n):
        return lax.dynamic_index_in_dim(x, n % x.shape[0], 0, keepdims=False)

    got = []
    for r in range(kv_heads):
        both = jnp.concatenate([columns(key_seq, plane + r), columns(value_seq, plane + r)], axis=1)
        got.append(across(both, r) if r else both)
    mine = jnp.stack(got)
    send = pack(attn_out, grad_out, seq_count, heads_here, pad)
    send, mine = lax.optimization_barrier((send, mine))
    pieces = [mine] + [inside(mine, s) for s in range(1, copies)]
    grad = lax.all_to_all(send, "seq", split_axis=0, concat_axis=0, tiled=True)
    kv, kt, lse2 = unpack(pos, lse, pieces)

    query_local, *parts = attend(pos, query, grad, kv, kt, lse2, rows, copies, min(512, total))
    parts = parts[:1] + [inside(parts[s], s) for s in range(1, copies)]
    back = lax.all_to_all(query_local, "seq", split_axis=0, concat_axis=0, tiled=True)
    query_grad = (
        back.reshape(seq_count, rows, heads_here * DH)
        .transpose(1, 0, 2)
        .reshape(rows, seq_count * heads_here * DH)
    )
    summed = functools.reduce(
        lambda a, b: a + b, (part.astype(jnp.float32) for part in parts)
    ).astype(jnp.bfloat16)
    blocks = [pick(summed, plane)] + [
        across(pick(summed, plane + r), r) for r in range(1, kv_heads)
    ]
    key_grad, value_grad = finish_kv(pos, blocks)
    return query_grad, key_grad, value_grad


def solution(mesh):
    tokens = P(("dp", "seq"), None)
    return jax.shard_map(
        per_device,
        mesh=mesh,
        in_specs=(P("dp", "seq"), tokens, tokens, tokens, tokens, P("seq", "dp")),
        out_specs=(tokens, tokens, tokens),
        check_vma=False,
    )
```

time: 127 us -> 107 us (0.84)
  waiting for transfers between devices: 55.7 us -> 43.1 us
  Pallas kernels: 32.5 us -> 24.6 us
    ppermute x6, waiting for transfers between devices: 33 us -> 15 us  [across(): return lax.ppermute(x, 'seq', turn)]
    all_to_all x1, waiting for transfers between devices: 0.01 us -> 8.51 us  [per_device(): grad = lax.all_to_all(send, 'seq', split_axis=0, concat_axis=0, tiled=True)]
    pallas_call x5 -> x4, Pallas kernels: 32.5 us -> 24.6 us  [the longest x1 16.3 us: attend(): call(body, (jax.ShapeDtypeStruct((total, width), jnp.bfloat16),) + (part,...]
    all_to_all x1, starting transfers between devices: 8.44 us -> 5.24 us  [per_device(): grad = lax.all_to_all(send, 'seq', split_axis=0, concat_axis=0, tiled=True)]
    ppermute x6, waiting for transfers between devices: 22.7 us -> 19.6 us  [inside(): return lax.ppermute(x, 'seq', turn)]
    ppermute x6, starting transfers between devices: 9.39 us -> 12.3 us  [across(): return lax.ppermute(x, 'seq', turn)]
  transfers between devices with their start and end apart: 14 -> 14, of which waited for: 9 -> 6; matrix products, arithmetic and copies ran while one was open for 3% -> 1% of each run, Pallas kernels for 14% -> 8%
where the time goes in v2:
time: 107 us; the launch traced here: 106 us
  waiting for transfers between devices  43.1 us (40%)
  starting transfers between devices  31 us (29%)
  Pallas kernels  24.6 us (23%)
  local copies, waits for them, and re-layouts  5.73 us (5%)
    ppermute x6, waiting for transfers between devices, inside(): return lax.ppermute(x, 'seq', turn)  19.6 us
    pallas_call x1, Pallas kernels, attend(): call(body, (jax.ShapeDtypeStruct((total, width), jnp.bfloat16),) + (part,...  16.3 us
    ppermute x6, waiting for transfers between devices, across(): return lax.ppermute(x, 'seq', turn)  15 us
    ppermute x6, starting transfers between devices, across(): return lax.ppermute(x, 'seq', turn)  12.3 us
    ppermute x6, starting transfers between devices, inside(): return lax.ppermute(x, 'seq', turn)  8.56 us
    all_to_all x1, waiting for transfers between devices, per_device(): grad = lax.all_to_all(send, 'seq', split_axis=0, concat_axis=0, tiled=True)  8.51 us
    all_to_all x1, starting transfers between devices, per_device(): grad = lax.all_to_all(send, 'seq', split_axis=0, concat_axis=0, tiled=True)  5.24 us
    all_to_all x1, starting transfers between devices, per_device(): lax.all_to_all(query_local, 'seq', split_axis=0, concat_axis=0, tiled=True)  4.88 us
  transfers between devices with their start and end apart: 14, of which 6 were waited for; matrix products, arithmetic and copies ran while one was open for 1% of the time, Pallas kernels for 8%

profile of v2, /device:TPU:0, one launch (start us, length us, event | category | flops | bytes accessed | tf_op | source)
XLA Modules:
  0.0 106.2 jit_solution(6972363009415362174)
XLA Ops:
  0.7 0.9 constant_dynamic-slice_fusion.6
  1.7 4.1 %collective-permute-start.1 = (bf16[128,256]{1,0:T(8,128)(2,1)S(1)}, bf16[128,256]{1,0:T(8,128)(2,1)S(1)}, u32[]{:S(2)}, u32[]{:S(2)}) collective-permute-start(bf16[128,256]{1,0:T(8,128)(2,1)S(1)} %pad_maximum_fusion.2), channel_id=1, source_target_pairs={{0,8},{1,9},{2,10},{3,11},{4,12},{5,13},{6,14},{7,15},{8,0},{9,1},... | collective-permute-start | bytes 196616 | tf_op jit(solution)/shard_map/ppermute | solution.py:199
  5.8 1.4 %collective-permute-start.2 = (bf16[128,256]{1,0:T(8,128)(2,1)S(1)}, bf16[128,256]{1,0:T(8,128)(2,1)S(1)}, u32[]{:S(2)}, u32[]{:S(2)}) collective-permute-start(bf16[128,256]{1,0:T(8,128)(2,1)S(1)} %pad_maximum_fusion.3), channel_id=1, source_target_pairs={{0,12},{1,13},{2,14},{3,15},{4,0},{5,1},{6,2},{7,3},{8,4},{9,5},{1... | collective-permute-start | bytes 196616 | tf_op jit(solution)/shard_map/ppermute | solution.py:199
  7.2 0.7 collective-permute-start
  7.9 4.2 %shard_map.85 = bf16[16,136,256]{2,1,0:T(8,128)(2,1)} custom-call(bf16[128,4096]{1,0:T(8,128)(2,1)} %o_ref.1, bf16[128,4096]{1,0:T(8,128)(2,1)} %g_ref.1), custom_call_target="tpu_custom_call" | custom-call | bytes 4194304 | tf_op jit(solution)/shard_map/pallas_call | solution.py:62
  12.2 1.1 %collective-permute-done = bf16[128,256]{1,0:T(8,128)(2,1)S(1)} collective-permute-done((bf16[128,256]{1,0:T(8,128)(2,1)S(1)}, bf16[128,256]{1,0:T(8,128)(2,1)S(1)}, u32[]{:S(2)}, u32[]{:S(2)}) %collective-permute-start) | collective-permute-done | bytes 65568 | tf_op jit(solution)/shard_map/ppermute | solution.py:199
  13.4 2.5 %collective-permute-start.5 = (bf16[4,128,256]{2,1,0:T(8,128)(2,1)S(1)}, bf16[4,128,256]{2,1,0:T(8,128)(2,1)S(1)}, u32[]{:S(2)}, u32[]{:S(2)}) collective-permute-start(bf16[4,128,256]{2,1,0:T(8,128)(2,1)S(1)} %pad_maximum_fusion.refs_0_), channel_id=1, source_target_pairs={{0,3},{1,0},{2,1},{3,2},{4,7},{5,4},{6,5},{7,6},{8,11},{9,8},{10,9... | collective-permute-start | bytes 786440 | tf_op jit(solution)/shard_map/ppermute | solution.py:203
  15.9 0.5 collective-permute-start.4
  16.4 0.6 collective-permute-start.3
  17.0 0.7 pad_add_fusion.pos_ref
  17.6 5.2 %all-to-all-start = ((bf16[16,136,256]{2,1,0:T(8,128)(2,1)}), bf16[16,136,256]{2,1,0:T(8,128)(2,1)S(1)}, u32[]{:S(2)}, u32[]{:S(2)}) async-start(bf16[16,136,256]{2,1,0:T(8,128)(2,1)} %shard_map.85), calls=%async_computation | async-start | bytes 2228224 | tf_op jit(solution)/shard_map/all_to_all | solution.py:219
  22.9 11.5 %collective-permute-done.4.refs_2_ = bf16[4,128,256]{2,1,0:T(8,128)(2,1)S(1)} collective-permute-done((bf16[4,128,256]{2,1,0:T(8,128)(2,1)S(1)}, bf16[4,128,256]{2,1,0:T(8,128)(2,1)S(1)}, u32[]{:S(2)}, u32[]{:S(2)}) %collective-permute-start.4) | collective-permute-done | bytes 262176 | tf_op jit(solution)/shard_map/ppermute | solution.py:203
  34.4 0.7 copy-done.4
  35.1 0.7 copy-done.5
  35.8 2.4 %shard_map.86 = (bf16[2048,256]{1,0:T(8,128)(2,1)}, bf16[128,2048]{1,0:T(8,128)(2,1)}, f32[2,2048]{1,0:T(2,128)}) custom-call(s32[2]{0:T(128)} %pad_add_fusion.pos_ref, f32[2,2048]{1,0:T(2,128)} %lse_ref.1, bf16[4,128,256]{2,1,0:T(8,128)(2,1)} %copy-done.2, bf16[4,128,256]{2,1,0:T(8,128)(2,1)} %copy-done.5, bf16[4,128,256]{2,1,0:T(8,128)(2,1)} %copy-done.4, ...), custom_call_target="tpu_custom_call" | custom-call | flops 40000000000 | bytes 4194304 | tf_op jit(solution)/shard_map/pallas_call | solution.py:88
  38.2 8.5 %all-to-all-done.g_ref = bf16[16,136,256]{2,1,0:T(8,128)(2,1)S(1)} async-done(((bf16[16,136,256]{2,1,0:T(8,128)(2,1)}), bf16[16,136,256]{2,1,0:T(8,128)(2,1)S(1)}, u32[]{:S(2)}, u32[]{:S(2)}) %all-to-all-start) | async-done | bytes 1114144 | tf_op jit(solution)/shard_map/all_to_all | solution.py:219
  46.7 1.0 copy-done
  47.7 16.3 %shard_map.87 = (bf16[2048,256]{1,0:T(8,128)(2,1)}, bf16[4,128,256]{2,1,0:T(8,128)(2,1)}, bf16[4,128,256]{2,1,0:T(8,128)(2,1)}, bf16[4,128,256]{2,1,0:T(8,128)(2,1)}, bf16[4,128,256]{2,1,0:T(8,128)(2,1)}) custom-call(s32[2]{0:T(128)} %pad_add_fusion.pos_ref, bf16[2048,256]{1,0:T(8,128)(2,1)} %q_ref.1, bf16[16,136,256]{2,1,0:T(8,128)(2,1)} %copy-done, ...), custom_call_target="tpu_custom_call" | custom-call | flops 5368709120 | bytes 4194304 | tf_op jit(solution)/shard_map/pallas_call | solution.py:154
  64.0 0.8 collective-permute-start.6
  64.8 2.1 %collective-permute-start.7 = (bf16[4,128,256]{2,1,0:T(8,128)(2,1)}, bf16[4,128,256]{2,1,0:T(8,128)(2,1)S(1)}, u32[]{:S(2)}, u32[]{:S(2)}) collective-permute-start(bf16[4,128,256]{2,1,0:T(8,128)(2,1)} %get-tuple-element.23), channel_id=1, source_target_pairs={{0,2},{1,3},{2,0},{3,1},{4,6},{5,7},{6,4},{7,5},{8,10},{9,11},{10,... | collective-permute-start | bytes 786440 | tf_op jit(solution)/shard_map/ppermute | solution.py:203
  66.9 2.1 %collective-permute-start.8 = (bf16[4,128,256]{2,1,0:T(8,128)(2,1)}, bf16[4,128,256]{2,1,0:T(8,128)(2,1)S(1)}, u32[]{:S(2)}, u32[]{:S(2)}) collective-permute-start(bf16[4,128,256]{2,1,0:T(8,128)(2,1)} %get-tuple-element.24), channel_id=1, source_target_pairs={{0,3},{1,0},{2,1},{3,2},{4,7},{5,4},{6,5},{7,6},{8,11},{9,8},{10,9... | collective-permute-start | bytes 786440 | tf_op jit(solution)/shard_map/ppermute | solution.py:203
  69.0 4.9 %all-to-all-start.1 = ((bf16[16,128,256]{2,1,0:T(8,128)(2,1)}), bf16[16,128,256]{2,1,0:T(8,128)(2,1)S(1)}, u32[]{:S(2)}, u32[]{:S(2)}) async-start(bf16[16,128,256]{2,1,0:T(8,128)(2,1)} %bitcast.20), calls=%async_computation.1 | async-start | bytes 2097152 | tf_op jit(solution)/shard_map/all_to_all | solution.py:224
  73.9 8.1 %collective-permute-done.7 = bf16[4,128,256]{2,1,0:T(8,128)(2,1)S(1)} collective-permute-done((bf16[4,128,256]{2,1,0:T(8,128)(2,1)}, bf16[4,128,256]{2,1,0:T(8,128)(2,1)S(1)}, u32[]{:S(2)}, u32[]{:S(2)}) %collective-permute-start.7) | collective-permute-done | bytes 262176 | tf_op jit(solution)/shard_map/ppermute | solution.py:203
  82.0 0.1 add_convert_fusion
  82.1 0.7 dynamic-slice_bitcast_fusion
  82.8 4.6 %collective-permute-start.11 = (bf16[128,256]{1,0:T(8,128)(2,1)S(1)}, bf16[128,256]{1,0:T(8,128)(2,1)S(1)}, u32[]{:S(2)}, u32[]{:S(2)}) collective-permute-start(bf16[128,256]{1,0:T(8,128)(2,1)S(1)} %get-tuple-element.27), channel_id=1, source_target_pairs={{0,12},{1,13},{2,14},{3,15},{4,0},{5,1},{6,2},{7,3},{8,4},{9,5},{1... | collective-permute-start | bytes 196616 | tf_op jit(solution)/shard_map/ppermute | solution.py:199
  87.4 1.5 %collective-permute-start.9 = (bf16[128,256]{1,0:T(8,128)(2,1)S(1)}, bf16[128,256]{1,0:T(8,128)(2,1)S(1)}, u32[]{:S(2)}, u32[]{:S(2)}) collective-permute-start(bf16[128,256]{1,0:T(8,128)(2,1)S(1)} %get-tuple-element.29), channel_id=1, source_target_pairs={{0,4},{1,5},{2,6},{3,7},{4,8},{5,9},{6,10},{7,11},{8,12},{9,13},{1... | collective-permute-start | bytes 196616 | tf_op jit(solution)/shard_map/ppermute | solution.py:199
  88.9 2.4 %collective-permute-done.11.refs_3_ = bf16[128,256]{1,0:T(8,128)(2,1)S(1)} collective-permute-done((bf16[128,256]{1,0:T(8,128)(2,1)S(1)}, bf16[128,256]{1,0:T(8,128)(2,1)S(1)}, u32[]{:S(2)}, u32[]{:S(2)}) %collective-permute-start.11) | collective-permute-done | bytes 65568 | tf_op jit(solution)/shard_map/ppermute | solution.py:199
  91.3 11.4 %collective-permute-done.10.refs_2_ = bf16[128,256]{1,0:T(8,128)(2,1)S(1)} collective-permute-done((bf16[128,256]{1,0:T(8,128)(2,1)S(1)}, bf16[128,256]{1,0:T(8,128)(2,1)S(1)}, u32[]{:S(2)}, u32[]{:S(2)}) %collective-permute-start.10) | collective-permute-done | bytes 65568 | tf_op jit(solution)/shard_map/ppermute | solution.py:199
  102.8 0.6 copy-done.7
  103.4 1.7 %shard_map.88 = (bf16[128,512]{1,0:T(8,128)(2,1)}, bf16[128,512]{1,0:T(8,128)(2,1)}) custom-call(s32[2]{0:T(128)} %pad_add_fusion.pos_ref, bf16[128,256]{1,0:T(8,128)(2,1)} %get-tuple-element.30.refs_0_, bf16[128,256]{1,0:T(8,128)(2,1)} %copy-done.8, bf16[128,256]{1,0:T(8,128)(2,1)} %copy-done.7, bf16[128,256]{1,0:T(8,128)(2,1)} %copy-done.6), custom_call_target="tpu_custom_call" | custom-call | flops 16000000000 | bytes 4194304 | tf_op jit(solution)/shard_map/pallas_call | solution.py:182
  105.1 1.1 %copy.10 = bf16[16,16,8,256]{3,2,0,1:T(8,128)(2,1)} copy(bf16[16,16,8,256]{3,2,1,0:T(8,128)(2,1)S(1)} %bitcast.19) | data formatting | bytes 2097152 | tf_op jit(solution)/shard_map/reshape | solution.py:228
  (28 shorter events, 0.1 us)
Async XLA Ops:
  1.7 10.5 %collective-permute-start.1 = (bf16[128,256]{1,0:T(8,128)(2,1)S(1)}, bf16[128,256]{1,0:T(8,128)(2,1)S(1)}, u32[]{:S(2)}, u32[]{:S(2)}) collective-permute-start(bf16[128,256]{1,0:T(8,128)(2,1)S(1)} %pad_maximum_fusion.2), channel_id=1, source_target_pairs={{0,8},{1,9},{2,10},{3,11},{4,12},{5,13},{6,14},{7,15},{8,0},{9,1},... | collective-permute-start | bytes 196616 | tf_op jit(solution)/shard_map/ppermute | solution.py:199
  5.8 6.4 %collective-permute-start.2 = (bf16[128,256]{1,0:T(8,128)(2,1)S(1)}, bf16[128,256]{1,0:T(8,128)(2,1)S(1)}, u32[]{:S(2)}, u32[]{:S(2)}) collective-permute-start(bf16[128,256]{1,0:T(8,128)(2,1)S(1)} %pad_maximum_fusion.3), channel_id=1, source_target_pairs={{0,12},{1,13},{2,14},{3,15},{4,0},{5,1},{6,2},{7,3},{8,4},{9,5},{1... | collective-permute-start | bytes 196616 | tf_op jit(solution)/shard_map/ppermute | solution.py:199
  7.2 6.1 %collective-permute-start = (bf16[128,256]{1,0:T(8,128)(2,1)S(1)}, bf16[128,256]{1,0:T(8,128)(2,1)S(1)}, u32[]{:S(2)}, u32[]{:S(2)}) collective-permute-start(bf16[128,256]{1,0:T(8,128)(2,1)S(1)} %pad_maximum_fusion.1), channel_id=1, source_target_pairs={{0,4},{1,5},{2,6},{3,7},{4,8},{5,9},{6,10},{7,11},{8,12},{9,13},{1... | collective-permute-start | bytes 196616 | tf_op jit(solution)/shard_map/ppermute | solution.py:199
  13.3 4.3 %copy-start.2 = (bf16[4,128,256]{2,1,0:T(8,128)(2,1)}, bf16[4,128,256]{2,1,0:T(8,128)(2,1)S(1)}, u32[]{:S(2)}) copy-start(bf16[4,128,256]{2,1,0:T(8,128)(2,1)S(1)} %pad_maximum_fusion.refs_0_) | copy-start | bytes 786436
  13.4 9.5 %collective-permute-start.5 = (bf16[4,128,256]{2,1,0:T(8,128)(2,1)S(1)}, bf16[4,128,256]{2,1,0:T(8,128)(2,1)S(1)}, u32[]{:S(2)}, u32[]{:S(2)}) collective-permute-start(bf16[4,128,256]{2,1,0:T(8,128)(2,1)S(1)} %pad_maximum_fusion.refs_0_), channel_id=1, source_target_pairs={{0,3},{1,0},{2,1},{3,2},{4,7},{5,4},{6,5},{7,6},{8,11},{9,8},{10,9... | collective-permute-start | bytes 786440 | tf_op jit(solution)/shard_map/ppermute | solution.py:203
  15.9 18.5 %collective-permute-start.4 = (bf16[4,128,256]{2,1,0:T(8,128)(2,1)S(1)}, bf16[4,128,256]{2,1,0:T(8,128)(2,1)S(1)}, u32[]{:S(2)}, u32[]{:S(2)}) collective-permute-start(bf16[4,128,256]{2,1,0:T(8,128)(2,1)S(1)} %pad_maximum_fusion.refs_0_), channel_id=1, source_target_pairs={{0,2},{1,3},{2,0},{3,1},{4,6},{5,7},{6,4},{7,5},{8,10},{9,11},{10,... | collective-permute-start | bytes 786440 | tf_op jit(solution)/shard_map/ppermute | solution.py:203
  16.4 18.0 %collective-permute-start.3 = (bf16[4,128,256]{2,1,0:T(8,128)(2,1)S(1)}, bf16[4,128,256]{2,1,0:T(8,128)(2,1)S(1)}, u32[]{:S(2)}, u32[]{:S(2)}) collective-permute-start(bf16[4,128,256]{2,1,0:T(8,128)(2,1)S(1)} %pad_maximum_fusion.refs_0_), channel_id=1, source_target_pairs={{0,1},{1,2},{2,3},{3,0},{4,5},{5,6},{6,7},{7,4},{8,9},{9,10},{10,1... | collective-permute-start | bytes 786440 | tf_op jit(solution)/shard_map/ppermute | solution.py:203
  17.6 29.1 %all-to-all-start = ((bf16[16,136,256]{2,1,0:T(8,128)(2,1)}), bf16[16,136,256]{2,1,0:T(8,128)(2,1)S(1)}, u32[]{:S(2)}, u32[]{:S(2)}) async-start(bf16[16,136,256]{2,1,0:T(8,128)(2,1)} %shard_map.85), calls=%async_computation | async-start | bytes 2228224 | tf_op jit(solution)/shard_map/all_to_all | solution.py:219
  22.9 11.5 %copy-start.3 = (bf16[4,128,256]{2,1,0:T(8,128)(2,1)}, bf16[4,128,256]{2,1,0:T(8,128)(2,1)S(1)}, u32[]{:S(2)}) copy-start(bf16[4,128,256]{2,1,0:T(8,128)(2,1)S(1)} %collective-permute-done.5.refs_3_) | copy-start | bytes 786436
  34.3 0.7 copy-start.4
  35.1 0.7 copy-start.5
  46.7 1.0 copy-start
  64.0 18.0 %copy-start.1 = (bf16[4,128,256]{2,1,0:T(8,128)(2,1)S(1)}, bf16[4,128,256]{2,1,0:T(8,128)(2,1)}, u32[]{:S(2)}) copy-start(bf16[4,128,256]{2,1,0:T(8,128)(2,1)} %get-tuple-element.21) | copy-start | bytes 786436
  64.0 9.9 %collective-permute-start.6 = (bf16[4,128,256]{2,1,0:T(8,128)(2,1)}, bf16[4,128,256]{2,1,0:T(8,128)(2,1)S(1)}, u32[]{:S(2)}, u32[]{:S(2)}) collective-permute-start(bf16[4,128,256]{2,1,0:T(8,128)(2,1)} %get-tuple-element.22), channel_id=1, source_target_pairs={{0,1},{1,2},{2,3},{3,0},{4,5},{5,6},{6,7},{7,4},{8,9},{9,10},{10,1... | collective-permute-start | bytes 786440 | tf_op jit(solution)/shard_map/ppermute | solution.py:203
  64.8 17.2 %collective-permute-start.7 = (bf16[4,128,256]{2,1,0:T(8,128)(2,1)}, bf16[4,128,256]{2,1,0:T(8,128)(2,1)S(1)}, u32[]{:S(2)}, u32[]{:S(2)}) collective-permute-start(bf16[4,128,256]{2,1,0:T(8,128)(2,1)} %get-tuple-element.23), channel_id=1, source_target_pairs={{0,2},{1,3},{2,0},{3,1},{4,6},{5,7},{6,4},{7,5},{8,10},{9,11},{10,... | collective-permute-start | bytes 786440 | tf_op jit(solution)/shard_map/ppermute | solution.py:203
  66.9 15.1 %collective-permute-start.8 = (bf16[4,128,256]{2,1,0:T(8,128)(2,1)}, bf16[4,128,256]{2,1,0:T(8,128)(2,1)S(1)}, u32[]{:S(2)}, u32[]{:S(2)}) collective-permute-start(bf16[4,128,256]{2,1,0:T(8,128)(2,1)} %get-tuple-element.24), channel_id=1, source_target_pairs={{0,3},{1,0},{2,1},{3,2},{4,7},{5,4},{6,5},{7,6},{8,11},{9,8},{10,9... | collective-permute-start | bytes 786440 | tf_op jit(solution)/shard_map/ppermute | solution.py:203
  69.0 36.1 %all-to-all-start.1 = ((bf16[16,128,256]{2,1,0:T(8,128)(2,1)}), bf16[16,128,256]{2,1,0:T(8,128)(2,1)S(1)}, u32[]{:S(2)}, u32[]{:S(2)}) async-start(bf16[16,128,256]{2,1,0:T(8,128)(2,1)} %bitcast.20), calls=%async_computation.1 | async-start | bytes 2097152 | tf_op jit(solution)/shard_map/all_to_all | solution.py:224
  82.8 8.5 %collective-permute-start.11 = (bf16[128,256]{1,0:T(8,128)(2,1)S(1)}, bf16[128,256]{1,0:T(8,128)(2,1)S(1)}, u32[]{:S(2)}, u32[]{:S(2)}) collective-permute-start(bf16[128,256]{1,0:T(8,128)(2,1)S(1)} %get-tuple-element.27), channel_id=1, source_target_pairs={{0,12},{1,13},{2,14},{3,15},{4,0},{5,1},{6,2},{7,3},{8,4},{9,5},{1... | collective-permute-start | bytes 196616 | tf_op jit(solution)/shard_map/ppermute | solution.py:199
  87.4 15.3 %collective-permute-start.10 = (bf16[128,256]{1,0:T(8,128)(2,1)S(1)}, bf16[128,256]{1,0:T(8,128)(2,1)S(1)}, u32[]{:S(2)}, u32[]{:S(2)}) collective-permute-start(bf16[128,256]{1,0:T(8,128)(2,1)S(1)} %get-tuple-element.28), channel_id=1, source_target_pairs={{0,8},{1,9},{2,10},{3,11},{4,12},{5,13},{6,14},{7,15},{8,0},{9,1},... | collective-permute-start | bytes 196616 | tf_op jit(solution)/shard_map/ppermute | solution.py:199
  87.4 15.3 %collective-permute-start.9 = (bf16[128,256]{1,0:T(8,128)(2,1)S(1)}, bf16[128,256]{1,0:T(8,128)(2,1)S(1)}, u32[]{:S(2)}, u32[]{:S(2)}) collective-permute-start(bf16[128,256]{1,0:T(8,128)(2,1)S(1)} %get-tuple-element.29), channel_id=1, source_target_pairs={{0,4},{1,5},{2,6},{3,7},{4,8},{5,9},{6,10},{7,11},{8,12},{9,13},{1... | collective-permute-start | bytes 196616 | tf_op jit(solution)/shard_map/ppermute | solution.py:199
  91.3 11.4 %copy-start.6 = (bf16[128,256]{1,0:T(8,128)(2,1)}, bf16[128,256]{1,0:T(8,128)(2,1)S(1)}, u32[]{:S(2)}) copy-start(bf16[128,256]{1,0:T(8,128)(2,1)S(1)} %collective-permute-done.11.refs_3_) | copy-start | bytes 196612
  102.7 0.6 copy-start.7
  102.8 0.6 copy-start.8

commit v3 on v2

--- a/solution.py
+++ b/solution.py
@@ -13,8 +13,9 @@
 NT = (((1,), (1,)), ((), ()))
 NN = (((1,), (0,)), ((), ()))
 VMEM = pl.BlockSpec(memory_space=pltpu.VMEM)
+ANY = pl.BlockSpec(memory_space=pl.ANY)
 SMEM = pl.BlockSpec(memory_space=pltpu.SMEM)
-LIMIT = 56 << 20
+LIMIT = 36 << 20
 
 
 def dot(a, b, dims):
@@ -68,47 +69,35 @@
     )(out, grad)
 
 
-def unpack(pos, lse, pieces):
+def attend(pos, q, g, lse, pieces, block):
+    total, width = q.shape
+    heads = width // DH
     copies = len(pieces)
-    kv_heads, rows, width = pieces[0].shape
-    total = rows * copies * kv_heads
-
-    def body(pos_ref, lse_ref, *refs):
-        ins, (kv_ref, kt_ref, lse_out) = refs[:copies], refs[copies:]
+    planes, rows, _ = pieces[0].shape
+    owners = block // rows
+
+    def body(pos_ref, q_ref, g_ref, lse_ref, *refs):
+        ins, dq_ref, slots = refs[:copies], refs[copies], refs[copies + 1 : 2 * copies + 1]
+        kv_ref, kt_ref, l_ref, d_ref, acc_ref, dkv_ref, sems = refs[2 * copies + 1 :]
         plane, place = pos_ref[0], pos_ref[1]
-        lse_out[...] = lse_ref[...] * LOG2E
+        coming = []
         for s in range(copies):
             source = lax.rem(place - s + copies, copies)
-            for r in range(kv_heads):
-                owner = lax.rem(plane - r + kv_heads, kv_heads) * copies + source
+            for r in range(planes):
+                owner = lax.rem(plane - r + planes, planes) * copies + source
                 start = pl.multiple_of(owner * rows, rows)
-                kv_ref[pl.ds(start, rows), :] = ins[s][r]
-        kt_ref[...] = kv_ref[:, :DH].T
-
-    return call(
-        body,
-        (
-            jax.ShapeDtypeStruct((total, width), jnp.bfloat16),
-            jax.ShapeDtypeStruct((DH, total), jnp.bfloat16),
-            jax.ShapeDtypeStruct(lse.shape, jnp.float32),
-        ),
-        [SMEM, VMEM] + [VMEM] * copies,
-        (VMEM,) * 3,
-        flops=int(40e9),
-    )(pos, lse, *pieces)
-
-
-def attend(pos, q, g, kv, kt, lse, rows, copies, block):
-    total = q.shape[0]
-    width = q.shape[1]
-    heads = width // DH
-    planes = total // (rows * copies)
-    owners = block // rows
-
-    def body(pos_ref, q_ref, g_ref, kv_ref, kt_ref, l_ref, dq_ref, *refs):
-        slots, (acc_ref, dkv_ref, d_ref) = refs[:copies], refs[copies:]
+                copy = pltpu.make_async_copy(
+                    ins[s].at[r], kv_ref.at[pl.ds(start, rows)], sems.at[s, r]
+                )
+                copy.start()
+                coming.append(copy)
+        l_ref[...] = lse_ref[...] * LOG2E
         for n in range(total // rows):
             d_ref[:, n * rows : (n + 1) * rows] = g_ref[n, rows:, :rows].astype(jnp.float32)
+        for copy in coming:
+            copy.wait()
+        for k0 in range(0, total, block):
+            kt_ref[:, k0 : k0 + block] = kv_ref[k0 : k0 + block, :DH].T
         for k0 in range(0, total, block):
             k1 = k0 + block
             kb, vb = kv_ref[k0:k1, :DH], kv_ref[k0:k1, DH:]
@@ -145,7 +134,7 @@
                 q1 = q0 + block
                 dq_ref[q0:q1, c] = (acc_ref[c, q0:q1] * SCALE).T.astype(jnp.bfloat16)
         for s in range(copies):
-            target = lax.rem(pos_ref[1] + s, copies)
+            target = lax.rem(place + s, copies)
             for r in range(planes):
                 start = pl.multiple_of((r * copies + target) * rows, rows)
                 slots[s][r] = dkv_ref[pl.ds(start, rows), :]
@@ -154,16 +143,20 @@
     return call(
         body,
         (jax.ShapeDtypeStruct((total, width), jnp.bfloat16),) + (part,) * copies,
-        [SMEM] + [VMEM] * 5,
+        [SMEM] + [VMEM] * 3 + [ANY] * copies,
         (VMEM,) * (1 + copies),
         flops=10 * heads * total * total * DH // 2,
         exps=heads * total * total // 2,
         scratch_shapes=[
+            pltpu.VMEM((total, 2 * DH), jnp.bfloat16),
+            pltpu.VMEM((DH, total), jnp.bfloat16),
+            pltpu.VMEM(lse.shape, jnp.float32),
+            pltpu.VMEM((g.shape[1] - rows, total), jnp.float32),
             pltpu.VMEM((width, total), jnp.float32),
             pltpu.VMEM((total, 2 * DH), jnp.bfloat16),
-            pltpu.VMEM((g.shape[1] - rows, total), jnp.float32),
+            pltpu.SemaphoreType.DMA((copies, planes)),
         ],
-    )(pos, q, g, kv, kt, lse)
+    )(pos, q, g, lse, *pieces)
 
 
 def finish_kv(pos, blocks):
@@ -217,9 +210,8 @@
     send, mine = lax.optimization_barrier((send, mine))
     pieces = [mine] + [inside(mine, s) for s in range(1, copies)]
     grad = lax.all_to_all(send, "seq", split_axis=0, concat_axis=0, tiled=True)
-    kv, kt, lse2 = unpack(pos, lse, pieces)
-
-    query_local, *parts = attend(pos, query, grad, kv, kt, lse2, rows, copies, min(512, total))
+    pieces = [pltpu.with_memory_space_constraint(x, pltpu.HBM) for x in pieces]
+    query_local, *parts = attend(pos, query, grad, lse, pieces, min(512, total))
     parts = parts[:1] + [inside(parts[s], s) for s in range(1, copies)]
     back = lax.all_to_all(query_local, "seq", split_axis=0, concat_axis=0, tiled=True)
     query_grad = (

time: 107 us -> 104 us (0.972)
  Pallas kernels: 24.6 us -> 19.7 us
  waiting for transfers between devices: 43.1 us -> 45.8 us
  local copies, waits for them, and re-layouts: 5.73 us -> 4.04 us
  starting transfers between devices: 31 us -> 32.6 us
    ppermute x6, waiting for transfers between devices: 19.6 us -> 30 us  [inside(): return lax.ppermute(x, 'seq', turn)]
    all_to_all x1, waiting for transfers between devices: 8.51 us -> 0.01 us  [per_device(): grad = lax.all_to_all(send, 'seq', split_axis=0, concat_axis=0, tiled=True)]
    pallas_call x1 -> x0, Pallas kernels: 2.44 us -> none  [unpack(): call(body, (jax.ShapeDtypeStruct((total, width), jnp.bfloat16), jax.Shape...]
    ppermute x6, starting transfers between devices: 12.3 us -> 14.6 us  [across(): return lax.ppermute(x, 'seq', turn)]
    pallas_call x1, Pallas kernels: 4.22 us -> 2.59 us  [pack(): call(body, jax.ShapeDtypeStruct((seq_count, rows + pad, width), jnp.bfloa...]
    ppermute x6, starting transfers between devices: 8.56 us -> 6.93 us  [inside(): return lax.ppermute(x, 'seq', turn)]
    all_to_all x1, starting transfers between devices: 4.88 us -> 6.06 us  [per_device(): lax.all_to_all(query_local, 'seq', split_axis=0, concat_axis=0, tiled=True)]
    unnamed x18 -> x16, local copies, waits for them, and re-layouts: 3.08 us -> 1.96 us
  transfers between devices with their start and end apart: 14 -> 14, of which waited for: 6 -> 7; matrix products, arithmetic and copies ran while one was open for 1% -> 0% of each run, Pallas kernels for 8% -> 4%
where the time goes in v3:
time: 104 us; the launch traced here: 103 us
  waiting for transfers between devices  45.8 us (44%)
  starting transfers between devices  32.6 us (31%)
  Pallas kernels  19.7 us (19%)
  local copies, waits for them, and re-layouts  4.04 us (4%)
    ppermute x6, waiting for transfers between devices, inside(): return lax.ppermute(x, 'seq', turn)  30 us
    pallas_call x1, Pallas kernels, attend(): call(body, (jax.ShapeDtypeStruct((total, width), jnp.bfloat16),) + (part,...  15.9 us
    ppermute x6, waiting for transfers between devices, across(): return lax.ppermute(x, 'seq', turn)  15.8 us
    ppermute x6, starting transfers between devices, across(): return lax.ppermute(x, 'seq', turn)  14.6 us
    ppermute x6, starting transfers between devices, inside(): return lax.ppermute(x, 'seq', turn)  6.93 us
    all_to_all x1, starting transfers between devices, per_device(): lax.all_to_all(query_local, 'seq', split_axis=0, concat_axis=0, tiled=True)  6.06 us
    all_to_all x1, starting transfers between devices, per_device(): grad = lax.all_to_all(send, 'seq', split_axis=0, concat_axis=0, tiled=True)  5.03 us
    pallas_call x1, Pallas kernels, pack(): call(body, jax.ShapeDtypeStruct((seq_count, rows + pad, width), jnp.bfloa...  2.59 us
  transfers between devices with their start and end apart: 14, of which 7 were waited for; matrix products, arithmetic and copies ran while one was open for 0% of the time, Pallas kernels for 4%

profile of v3, /device:TPU:0, one launch (start us, length us, event | category | flops | bytes accessed | tf_op | source)
XLA Modules:
  0.0 103.3 jit_solution(12782518977675904633)
XLA Ops:
  0.7 1.0 constant_dynamic-slice_fusion.6
  1.7 4.1 %collective-permute-start.1 = (bf16[128,256]{1,0:T(8,128)(2,1)S(1)}, bf16[128,256]{1,0:T(8,128)(2,1)S(1)}, u32[]{:S(2)}, u32[]{:S(2)}) collective-permute-start(bf16[128,256]{1,0:T(8,128)(2,1)S(1)} %pad_maximum_fusion.2), channel_id=1, source_target_pairs={{0,8},{1,9},{2,10},{3,11},{4,12},{5,13},{6,14},{7,15},{8,0},{9,1},... | collective-permute-start | bytes 196616 | tf_op jit(solution)/shard_map/ppermute | solution.py:192
  5.8 1.4 %collective-permute-start.2 = (bf16[128,256]{1,0:T(8,128)(2,1)S(1)}, bf16[128,256]{1,0:T(8,128)(2,1)S(1)}, u32[]{:S(2)}, u32[]{:S(2)}) collective-permute-start(bf16[128,256]{1,0:T(8,128)(2,1)S(1)} %pad_maximum_fusion.3), channel_id=1, source_target_pairs={{0,12},{1,13},{2,14},{3,15},{4,0},{5,1},{6,2},{7,3},{8,4},{9,5},{1... | collective-permute-start | bytes 196616 | tf_op jit(solution)/shard_map/ppermute | solution.py:192
  7.3 0.7 collective-permute-start
  8.0 1.2 %copy-done.1 = bf16[128,4096]{1,0:T(8,128)(2,1)S(1)} copy-done((bf16[128,4096]{1,0:T(8,128)(2,1)S(1)}, bf16[128,4096]{1,0:T(8,128)(2,1)}, u32[]{:S(2)}) %copy-start.1) | copy-done | bytes 1048600
  9.2 2.6 %shard_map.85 = bf16[16,136,256]{2,1,0:T(8,128)(2,1)} custom-call(bf16[128,4096]{1,0:T(8,128)(2,1)S(1)} %copy-done, bf16[128,4096]{1,0:T(8,128)(2,1)S(1)} %copy-done.1), custom_call_target="tpu_custom_call" | custom-call | bytes 4194304 | tf_op jit(solution)/shard_map/pallas_call | solution.py:63
  11.8 0.0 collective-permute-done.1
  11.8 1.5 %collective-permute-done = bf16[128,256]{1,0:T(8,128)(2,1)S(1)} collective-permute-done((bf16[128,256]{1,0:T(8,128)(2,1)S(1)}, bf16[128,256]{1,0:T(8,128)(2,1)S(1)}, u32[]{:S(2)}, u32[]{:S(2)}) %collective-permute-start) | collective-permute-done | bytes 65568 | tf_op jit(solution)/shard_map/ppermute | solution.py:192
  13.4 0.0 copy-start.2
  13.4 0.0 copy-start.3
  13.5 5.0 %all-to-all-start = ((bf16[16,136,256]{2,1,0:T(8,128)(2,1)}), bf16[16,136,256]{2,1,0:T(8,128)(2,1)S(1)}, u32[]{:S(2)}, u32[]{:S(2)}) async-start(bf16[16,136,256]{2,1,0:T(8,128)(2,1)} %shard_map.85), calls=%async_computation | async-start | bytes 2228224 | tf_op jit(solution)/shard_map/all_to_all | solution.py:212
  18.5 2.8 %collective-permute-start.5 = (bf16[4,128,256]{2,1,0:T(8,128)(2,1)S(1)}, bf16[4,128,256]{2,1,0:T(8,128)(2,1)S(1)}, u32[]{:S(2)}, u32[]{:S(2)}) collective-permute-start(bf16[4,128,256]{2,1,0:T(8,128)(2,1)S(1)} %pad_maximum_fusion.refs_0_), channel_id=1, source_target_pairs={{0,3},{1,0},{2,1},{3,2},{4,7},{5,4},{6,5},{7,6},{8,11},{9,8},{10,9... | collective-permute-start | bytes 786440 | tf_op jit(solution)/shard_map/ppermute | solution.py:196
  21.3 0.6 collective-permute-start.4
  21.9 0.6 collective-permute-start.3
  22.4 0.1 pad_add_fusion.pos_ref
  22.5 14.2 %collective-permute-done.5.refs_3_ = bf16[4,128,256]{2,1,0:T(8,128)(2,1)S(1)} collective-permute-done((bf16[4,128,256]{2,1,0:T(8,128)(2,1)S(1)}, bf16[4,128,256]{2,1,0:T(8,128)(2,1)S(1)}, u32[]{:S(2)}, u32[]{:S(2)}) %collective-permute-start.5) | collective-permute-done | bytes 262176 | tf_op jit(solution)/shard_map/ppermute | solution.py:196
  36.7 2.7 %collective-permute-done.4.refs_2_ = bf16[4,128,256]{2,1,0:T(8,128)(2,1)S(1)} collective-permute-done((bf16[4,128,256]{2,1,0:T(8,128)(2,1)S(1)}, bf16[4,128,256]{2,1,0:T(8,128)(2,1)S(1)}, u32[]{:S(2)}, u32[]{:S(2)}) %collective-permute-start.4) | collective-permute-done | bytes 262176 | tf_op jit(solution)/shard_map/ppermute | solution.py:196
  39.4 6.1 %collective-permute-done.3.refs_1_ = bf16[4,128,256]{2,1,0:T(8,128)(2,1)S(1)} collective-permute-done((bf16[4,128,256]{2,1,0:T(8,128)(2,1)S(1)}, bf16[4,128,256]{2,1,0:T(8,128)(2,1)S(1)}, u32[]{:S(2)}, u32[]{:S(2)}) %collective-permute-start.3) | collective-permute-done | bytes 262176 | tf_op jit(solution)/shard_map/ppermute | solution.py:196
  45.5 0.7 copy-done.7
  46.2 15.9 %shard_map.86 = (bf16[2048,256]{1,0:T(8,128)(2,1)}, bf16[4,128,256]{2,1,0:T(8,128)(2,1)S(1)}, bf16[4,128,256]{2,1,0:T(8,128)(2,1)S(1)}, bf16[4,128,256]{2,1,0:T(8,128)(2,1)S(1)}, bf16[4,128,256]{2,1,0:T(8,128)(2,1)S(1)}) custom-call(s32[2]{0:T(128)S(1)} %pad_add_fusion.pos_ref, bf16[2048,256]{1,0:T(8,128)(2,1)S(1)} %copy-done.2, ...), custom_call_target="tpu_custom_call" | custom-call | flops 5368709120 | bytes 4194304 | tf_op jit(solution)/shard_map/pallas_call | solution.py:143
  62.1 0.3 collective-permute-start.6
  62.4 1.4 %collective-permute-start.7 = (bf16[4,128,256]{2,1,0:T(8,128)(2,1)S(1)}, bf16[4,128,256]{2,1,0:T(8,128)(2,1)S(1)}, u32[]{:S(2)}, u32[]{:S(2)}) collective-permute-start(bf16[4,128,256]{2,1,0:T(8,128)(2,1)S(1)} %get-tuple-element.17), channel_id=1, source_target_pairs={{0,2},{1,3},{2,0},{3,1},{4,6},{5,7},{6,4},{7,5},{8,10},{9,11},{10,... | collective-permute-start | bytes 786440 | tf_op jit(solution)/shard_map/ppermute | solution.py:196
  63.8 1.3 %collective-permute-start.8 = (bf16[4,128,256]{2,1,0:T(8,128)(2,1)S(1)}, bf16[4,128,256]{2,1,0:T(8,128)(2,1)S(1)}, u32[]{:S(2)}, u32[]{:S(2)}) collective-permute-start(bf16[4,128,256]{2,1,0:T(8,128)(2,1)S(1)} %get-tuple-element.18), channel_id=1, source_target_pairs={{0,3},{1,0},{2,1},{3,2},{4,7},{5,4},{6,5},{7,6},{8,11},{9,8},{10,9... | collective-permute-start | bytes 786440 | tf_op jit(solution)/shard_map/ppermute | solution.py:196
  65.0 6.1 %all-to-all-start.1 = ((bf16[16,128,256]{2,1,0:T(8,128)(2,1)}), bf16[16,128,256]{2,1,0:T(8,128)(2,1)S(1)}, u32[]{:S(2)}, u32[]{:S(2)}) async-start(bf16[16,128,256]{2,1,0:T(8,128)(2,1)} %bitcast.6), calls=%async_computation.1 | async-start | bytes 2097152 | tf_op jit(solution)/shard_map/all_to_all | solution.py:216
  71.2 7.1 %collective-permute-done.7 = bf16[4,128,256]{2,1,0:T(8,128)(2,1)S(1)} collective-permute-done((bf16[4,128,256]{2,1,0:T(8,128)(2,1)S(1)}, bf16[4,128,256]{2,1,0:T(8,128)(2,1)S(1)}, u32[]{:S(2)}, u32[]{:S(2)}) %collective-permute-start.7) | collective-permute-done | bytes 262176 | tf_op jit(solution)/shard_map/ppermute | solution.py:196
  78.2 0.1 add_convert_fusion
  78.4 7.7 %collective-permute-start.11 = (bf16[128,256]{1,0:T(8,128)(2,1)S(1)}, bf16[128,256]{1,0:T(8,128)(2,1)S(1)}, u32[]{:S(2)}, u32[]{:S(2)}) collective-permute-start(bf16[128,256]{1,0:T(8,128)(2,1)S(1)} %get-tuple-element.21), channel_id=1, source_target_pairs={{0,12},{1,13},{2,14},{3,15},{4,0},{5,1},{6,2},{7,3},{8,4},{9,5},{1... | collective-permute-start | bytes 196616 | tf_op jit(solution)/shard_map/ppermute | solution.py:192
  86.1 0.6 collective-permute-start.9
  86.7 1.9 %collective-permute-done.11.refs_3_ = bf16[128,256]{1,0:T(8,128)(2,1)S(1)} collective-permute-done((bf16[128,256]{1,0:T(8,128)(2,1)S(1)}, bf16[128,256]{1,0:T(8,128)(2,1)S(1)}, u32[]{:S(2)}, u32[]{:S(2)}) %collective-permute-start.11) | collective-permute-done | bytes 65568 | tf_op jit(solution)/shard_map/ppermute | solution.py:192
  88.6 12.4 %collective-permute-done.10.refs_2_ = bf16[128,256]{1,0:T(8,128)(2,1)S(1)} collective-permute-done((bf16[128,256]{1,0:T(8,128)(2,1)S(1)}, bf16[128,256]{1,0:T(8,128)(2,1)S(1)}, u32[]{:S(2)}, u32[]{:S(2)}) %collective-permute-start.10) | collective-permute-done | bytes 65568 | tf_op jit(solution)/shard_map/ppermute | solution.py:192
  101.0 1.3 %shard_map.87 = (bf16[128,512]{1,0:T(8,128)(2,1)}, bf16[128,512]{1,0:T(8,128)(2,1)}) custom-call(s32[2]{0:T(128)S(1)} %pad_add_fusion.pos_ref, bf16[128,256]{1,0:T(8,128)(2,1)S(1)} %get-tuple-element.24.refs_0_, bf16[128,256]{1,0:T(8,128)(2,1)S(1)} %collective-permute-done.9.refs_1_, bf16[128,256]{1,0:T(8,128)(2,1)S(1)} %collective-permute-done.10.refs_2_, ...), custom_call_target="tpu_custom_call" | custom-call | flops 16000000000 | bytes 4194304 | tf_op jit(solution)/shard_map/pallas_call | solution.py:175
  102.3 1.1 %copy.10 = bf16[16,16,8,256]{3,2,0,1:T(8,128)(2,1)} copy(bf16[16,16,8,256]{3,2,1,0:T(8,128)(2,1)S(1)} %bitcast.19) | data formatting | bytes 2097152 | tf_op jit(solution)/shard_map/reshape | solution.py:220
  (25 shorter events, 0.1 us)
Async XLA Ops:
  0.6 7.4 %copy-start = (bf16[128,4096]{1,0:T(8,128)(2,1)S(1)}, bf16[128,4096]{1,0:T(8,128)(2,1)}, u32[]{:S(2)}) copy-start(bf16[128,4096]{1,0:T(8,128)(2,1)} %o_ref.1) | copy-start | bytes 3145732
  1.7 10.1 %collective-permute-start.1 = (bf16[128,256]{1,0:T(8,128)(2,1)S(1)}, bf16[128,256]{1,0:T(8,128)(2,1)S(1)}, u32[]{:S(2)}, u32[]{:S(2)}) collective-permute-start(bf16[128,256]{1,0:T(8,128)(2,1)S(1)} %pad_maximum_fusion.2), channel_id=1, source_target_pairs={{0,8},{1,9},{2,10},{3,11},{4,12},{5,13},{6,14},{7,15},{8,0},{9,1},... | collective-permute-start | bytes 196616 | tf_op jit(solution)/shard_map/ppermute | solution.py:192
  5.8 6.0 %collective-permute-start.2 = (bf16[128,256]{1,0:T(8,128)(2,1)S(1)}, bf16[128,256]{1,0:T(8,128)(2,1)S(1)}, u32[]{:S(2)}, u32[]{:S(2)}) collective-permute-start(bf16[128,256]{1,0:T(8,128)(2,1)S(1)} %pad_maximum_fusion.3), channel_id=1, source_target_pairs={{0,12},{1,13},{2,14},{3,15},{4,0},{5,1},{6,2},{7,3},{8,4},{9,5},{1... | collective-permute-start | bytes 196616 | tf_op jit(solution)/shard_map/ppermute | solution.py:192
  7.3 6.1 %collective-permute-start = (bf16[128,256]{1,0:T(8,128)(2,1)S(1)}, bf16[128,256]{1,0:T(8,128)(2,1)S(1)}, u32[]{:S(2)}, u32[]{:S(2)}) collective-permute-start(bf16[128,256]{1,0:T(8,128)(2,1)S(1)} %pad_maximum_fusion.1), channel_id=1, source_target_pairs={{0,4},{1,5},{2,6},{3,7},{4,8},{5,9},{6,10},{7,11},{8,12},{9,13},{1... | collective-permute-start | bytes 196616 | tf_op jit(solution)/shard_map/ppermute | solution.py:192
  8.0 1.2 %copy-start.1 = (bf16[128,4096]{1,0:T(8,128)(2,1)S(1)}, bf16[128,4096]{1,0:T(8,128)(2,1)}, u32[]{:S(2)}) copy-start(bf16[128,4096]{1,0:T(8,128)(2,1)} %g_ref.1) | copy-start | bytes 3145732
  13.4 8.5 %copy-start.4 = (bf16[4,128,256]{2,1,0:T(8,128)(2,1)}, bf16[4,128,256]{2,1,0:T(8,128)(2,1)S(1)}, u32[]{:S(2)}) copy-start(bf16[4,128,256]{2,1,0:T(8,128)(2,1)S(1)} %pad_maximum_fusion.refs_0_) | copy-start | bytes 786436
  13.4 32.8 %copy-start.2 = (bf16[2048,256]{1,0:T(8,128)(2,1)S(1)}, bf16[2048,256]{1,0:T(8,128)(2,1)}, u32[]{:S(2)}) copy-start(bf16[2048,256]{1,0:T(8,128)(2,1)} %q_ref.1) | copy-start | bytes 3145732
  13.4 32.7 %copy-start.3 = (f32[2,2048]{1,0:T(2,128)S(1)}, f32[2,2048]{1,0:T(2,128)}, u32[]{:S(2)}) copy-start(f32[2,2048]{1,0:T(2,128)} %lse_ref.1) | copy-start | bytes 49156
  13.5 32.7 %all-to-all-start = ((bf16[16,136,256]{2,1,0:T(8,128)(2,1)}), bf16[16,136,256]{2,1,0:T(8,128)(2,1)S(1)}, u32[]{:S(2)}, u32[]{:S(2)}) async-start(bf16[16,136,256]{2,1,0:T(8,128)(2,1)} %shard_map.85), calls=%async_computation | async-start | bytes 2228224 | tf_op jit(solution)/shard_map/all_to_all | solution.py:212
  18.5 18.2 %collective-permute-start.5 = (bf16[4,128,256]{2,1,0:T(8,128)(2,1)S(1)}, bf16[4,128,256]{2,1,0:T(8,128)(2,1)S(1)}, u32[]{:S(2)}, u32[]{:S(2)}) collective-permute-start(bf16[4,128,256]{2,1,0:T(8,128)(2,1)S(1)} %pad_maximum_fusion.refs_0_), channel_id=1, source_target_pairs={{0,3},{1,0},{2,1},{3,2},{4,7},{5,4},{6,5},{7,6},{8,11},{9,8},{10,9... | collective-permute-start | bytes 786440 | tf_op jit(solution)/shard_map/ppermute | solution.py:196
  21.3 18.1 %collective-permute-start.4 = (bf16[4,128,256]{2,1,0:T(8,128)(2,1)S(1)}, bf16[4,128,256]{2,1,0:T(8,128)(2,1)S(1)}, u32[]{:S(2)}, u32[]{:S(2)}) collective-permute-start(bf16[4,128,256]{2,1,0:T(8,128)(2,1)S(1)} %pad_maximum_fusion.refs_0_), channel_id=1, source_target_pairs={{0,2},{1,3},{2,0},{3,1},{4,6},{5,7},{6,4},{7,5},{8,10},{9,11},{10,... | collective-permute-start | bytes 786440 | tf_op jit(solution)/shard_map/ppermute | solution.py:196
  21.9 23.6 %collective-permute-start.3 = (bf16[4,128,256]{2,1,0:T(8,128)(2,1)S(1)}, bf16[4,128,256]{2,1,0:T(8,128)(2,1)S(1)}, u32[]{:S(2)}, u32[]{:S(2)}) collective-permute-start(bf16[4,128,256]{2,1,0:T(8,128)(2,1)S(1)} %pad_maximum_fusion.refs_0_), channel_id=1, source_target_pairs={{0,1},{1,2},{2,3},{3,0},{4,5},{5,6},{6,7},{7,4},{8,9},{9,10},{10,1... | collective-permute-start | bytes 786440 | tf_op jit(solution)/shard_map/ppermute | solution.py:196
  36.7 8.7 %copy-start.5 = (bf16[4,128,256]{2,1,0:T(8,128)(2,1)}, bf16[4,128,256]{2,1,0:T(8,128)(2,1)S(1)}, u32[]{:S(2)}) copy-start(bf16[4,128,256]{2,1,0:T(8,128)(2,1)S(1)} %collective-permute-done.5.refs_3_) | copy-start | bytes 786436
  39.4 6.1 %copy-start.6 = (bf16[4,128,256]{2,1,0:T(8,128)(2,1)}, bf16[4,128,256]{2,1,0:T(8,128)(2,1)S(1)}, u32[]{:S(2)}) copy-start(bf16[4,128,256]{2,1,0:T(8,128)(2,1)S(1)} %collective-permute-done.4.refs_2_) | copy-start | bytes 786436
  45.5 0.7 copy-start.7
  62.1 9.1 %collective-permute-start.6 = (bf16[4,128,256]{2,1,0:T(8,128)(2,1)S(1)}, bf16[4,128,256]{2,1,0:T(8,128)(2,1)S(1)}, u32[]{:S(2)}, u32[]{:S(2)}) collective-permute-start(bf16[4,128,256]{2,1,0:T(8,128)(2,1)S(1)} %get-tuple-element.16), channel_id=1, source_target_pairs={{0,1},{1,2},{2,3},{3,0},{4,5},{5,6},{6,7},{7,4},{8,9},{9,10},{10,1... | collective-permute-start | bytes 786440 | tf_op jit(solution)/shard_map/ppermute | solution.py:196
  62.4 15.8 %collective-permute-start.7 = (bf16[4,128,256]{2,1,0:T(8,128)(2,1)S(1)}, bf16[4,128,256]{2,1,0:T(8,128)(2,1)S(1)}, u32[]{:S(2)}, u32[]{:S(2)}) collective-permute-start(bf16[4,128,256]{2,1,0:T(8,128)(2,1)S(1)} %get-tuple-element.17), channel_id=1, source_target_pairs={{0,2},{1,3},{2,0},{3,1},{4,6},{5,7},{6,4},{7,5},{8,10},{9,11},{10,... | collective-permute-start | bytes 786440 | tf_op jit(solution)/shard_map/ppermute | solution.py:196
  63.8 14.4 %collective-permute-start.8 = (bf16[4,128,256]{2,1,0:T(8,128)(2,1)S(1)}, bf16[4,128,256]{2,1,0:T(8,128)(2,1)S(1)}, u32[]{:S(2)}, u32[]{:S(2)}) collective-permute-start(bf16[4,128,256]{2,1,0:T(8,128)(2,1)S(1)} %get-tuple-element.18), channel_id=1, source_target_pairs={{0,3},{1,0},{2,1},{3,2},{4,7},{5,4},{6,5},{7,6},{8,11},{9,8},{10,9... | collective-permute-start | bytes 786440 | tf_op jit(solution)/shard_map/ppermute | solution.py:196
  65.0 37.2 %all-to-all-start.1 = ((bf16[16,128,256]{2,1,0:T(8,128)(2,1)}), bf16[16,128,256]{2,1,0:T(8,128)(2,1)S(1)}, u32[]{:S(2)}, u32[]{:S(2)}) async-start(bf16[16,128,256]{2,1,0:T(8,128)(2,1)} %bitcast.6), calls=%async_computation.1 | async-start | bytes 2097152 | tf_op jit(solution)/shard_map/all_to_all | solution.py:216
  78.4 10.2 %collective-permute-start.11 = (bf16[128,256]{1,0:T(8,128)(2,1)S(1)}, bf16[128,256]{1,0:T(8,128)(2,1)S(1)}, u32[]{:S(2)}, u32[]{:S(2)}) collective-permute-start(bf16[128,256]{1,0:T(8,128)(2,1)S(1)} %get-tuple-element.21), channel_id=1, source_target_pairs={{0,12},{1,13},{2,14},{3,15},{4,0},{5,1},{6,2},{7,3},{8,4},{9,5},{1... | collective-permute-start | bytes 196616 | tf_op jit(solution)/shard_map/ppermute | solution.py:192
  86.1 14.9 %collective-permute-start.10 = (bf16[128,256]{1,0:T(8,128)(2,1)S(1)}, bf16[128,256]{1,0:T(8,128)(2,1)S(1)}, u32[]{:S(2)}, u32[]{:S(2)}) collective-permute-start(bf16[128,256]{1,0:T(8,128)(2,1)S(1)} %get-tuple-element.22), channel_id=1, source_target_pairs={{0,8},{1,9},{2,10},{3,11},{4,12},{5,13},{6,14},{7,15},{8,0},{9,1},... | collective-permute-start | bytes 196616 | tf_op jit(solution)/shard_map/ppermute | solution.py:192
  86.1 14.9 %collective-permute-start.9 = (bf16[128,256]{1,0:T(8,128)(2,1)S(1)}, bf16[128,256]{1,0:T(8,128)(2,1)S(1)}, u32[]{:S(2)}, u32[]{:S(2)}) collective-permute-start(bf16[128,256]{1,0:T(8,128)(2,1)S(1)} %get-tuple-element.23), channel_id=1, source_target_pairs={{0,4},{1,5},{2,6},{3,7},{4,8},{5,9},{6,10},{7,11},{8,12},{9,13},{1... | collective-permute-start | bytes 196616 | tf_op jit(solution)/shard_map/ppermute | solution.py:192

commit v4 on v3

--- a/solution.py
+++ b/solution.py
@@ -1,5 +1,3 @@
-import functools
-
 import jax
 import jax.numpy as jnp
 from jax import lax
@@ -39,33 +37,31 @@
 def pack(out, grad, seq_count, heads_here, pad):
     rows = grad.shape[0]
     width = heads_here * DH
-    steps = 4 if seq_count % 4 == 0 else 1
-    here = seq_count // steps
+    cols = 4 * width if seq_count % 4 == 0 else width
+    here = cols // width
 
     def body(o_ref, g_ref, send_ref):
-        for d in range(here):
-            c = slice(d * width, (d + 1) * width)
-            block = g_ref[:, c]
-            send_ref[d, :rows] = block
-            prod = block.astype(jnp.float32) * o_ref[:, c].astype(jnp.float32)
-            sums = [
-                jnp.sum(prod[:, h * DH : (h + 1) * DH], axis=1, keepdims=True)
-                for h in range(heads_here)
-            ]
-            sums.append(jnp.zeros((rows, pad - heads_here), jnp.float32))
-            delta = jnp.concatenate(sums, axis=1).T
+        at = lax.broadcasted_iota(jnp.int32, (cols, 128), 0) // DH
+        at = at // heads_here * pad + at % heads_here
+        ones = (at == lax.broadcasted_iota(jnp.int32, (cols, 128), 1)).astype(jnp.bfloat16)
+        for n in range(0, seq_count, here):
+            c = slice(n * width, n * width + cols)
+            prod = g_ref[:, c].astype(jnp.float32) * o_ref[:, c].astype(jnp.float32)
+            high = prod.astype(jnp.bfloat16)
+            low = (prod - high.astype(jnp.float32)).astype(jnp.bfloat16)
+            delta = (dot(high, ones, NN) + dot(low, ones, NN)).T
             if width > rows:
-                fill = jnp.zeros((pad, width - rows), jnp.float32)
+                fill = jnp.zeros((128, width - rows), jnp.float32)
                 delta = jnp.concatenate([delta, fill], axis=1)
-            send_ref[d, rows:] = delta.astype(jnp.bfloat16)
-
-    many = pl.BlockSpec((rows, here * width), lambda n: (0, n))
+            for d in range(here):
+                send_ref[n + d, :rows] = g_ref[:, (n + d) * width : (n + d + 1) * width]
+                send_ref[n + d, rows:] = delta[d * pad : (d + 1) * pad].astype(jnp.bfloat16)
+
     return call(
         body,
         jax.ShapeDtypeStruct((seq_count, rows + pad, width), jnp.bfloat16),
-        [many, many],
-        pl.BlockSpec((here, rows + pad, width), lambda n: (n, 0, 0)),
-        grid=(steps,),
+        [VMEM, VMEM],
+        VMEM,
     )(out, grad)
 
 
@@ -159,12 +155,34 @@
     )(pos, q, g, lse, *pieces)
 
 
-def finish_kv(pos, blocks):
+def reduce_kv(pos, parts):
+    planes, rows, width = parts[0].shape
+
+    def body(pos_ref, *refs):
+        ins, outs = refs[: len(parts)], refs[len(parts) :]
+        for r in range(planes):
+            n = lax.rem(pos_ref[0] + r, planes)
+            total = ins[0][n].astype(jnp.float32)
+            for part in ins[1:]:
+                total = total + part[n].astype(jnp.float32)
+            outs[r][...] = total.astype(jnp.bfloat16)
+
+    out = jax.ShapeDtypeStruct((rows, width), jnp.bfloat16)
+    return call(
+        body,
+        (out,) * planes,
+        [SMEM] + [VMEM] * len(parts),
+        (VMEM,) * planes,
+        flops=int(40e9),
+    )(pos, *parts)
+
+
+def finish_kv(pos, blocks, after):
     kv_heads = len(blocks)
     rows = blocks[0].shape[0]
 
     def body(pos_ref, *refs):
-        ins, (k_ref, v_ref) = refs[:kv_heads], refs[kv_heads:]
+        ins, (_, k_ref, v_ref) = refs[:kv_heads], refs[kv_heads:]
         for r in range(kv_heads):
             g = lax.rem(pos_ref[0] - r + kv_heads, kv_heads)
             cols = pl.ds(pl.multiple_of(g * DH, DH), DH)
@@ -172,7 +190,9 @@
             v_ref[:, cols] = ins[r][:, DH:]
 
     out = jax.ShapeDtypeStruct((rows, kv_heads * DH), jnp.bfloat16)
-    return call(body, (out, out), [SMEM] + [VMEM] * kv_heads, (VMEM, VMEM), flops=int(16e9))(pos, *blocks)
+    return call(body, (out, out), [SMEM] + [VMEM] * kv_heads + [ANY], (VMEM, VMEM))(
+        pos, *blocks, after
+    )
 
 
 def per_device(query, key_seq, value_seq, attn_out, grad_out, lse):
@@ -219,13 +239,9 @@
         .transpose(1, 0, 2)
         .reshape(rows, seq_count * heads_here * DH)
     )
-    summed = functools.reduce(
-        lambda a, b: a + b, (part.astype(jnp.float32) for part in parts)
-    ).astype(jnp.bfloat16)
-    blocks = [pick(summed, plane)] + [
-        across(pick(summed, plane + r), r) for r in range(1, kv_heads)
-    ]
-    key_grad, value_grad = finish_kv(pos, blocks)
+    sums = reduce_kv(pos, parts)
+    blocks = [sums[0]] + [across(sums[r], r) for r in range(1, kv_heads)]
+    key_grad, value_grad = finish_kv(pos, blocks, query_grad)
     return query_grad, key_grad, value_grad
 
 

time: 104 us -> 102 us (0.981)
    ppermute x6, waiting for transfers between devices: 15.8 us -> 5.56 us  [across(): return lax.ppermute(x, 'seq', turn)]
    all_to_all x1, waiting for transfers between devices: 0.01 us -> 9.59 us  [per_device(): lax.all_to_all(query_local, 'seq', split_axis=0, concat_axis=0, tiled=True)]
  transfers between devices with their start and end apart: 14 -> 14, of which waited for: 7 -> 7; matrix products, arithmetic and copies ran while one was open for 0% -> 0% of each run, Pallas kernels for 4% -> 3%
where the time goes in v4:
time: 102 us
  waiting for transfers between devices  45.9 us (45%)
  starting transfers between devices  31.8 us (31%)
  Pallas kernels  19.8 us (19%)
  local copies, waits for them, and re-layouts  3.04 us (3%)
    ppermute x6, waiting for transfers between devices, inside(): return lax.ppermute(x, 'seq', turn)  30.7 us
    pallas_call x1, Pallas kernels, attend(): call(body, (jax.ShapeDtypeStruct((total, width), jnp.bfloat16),) + (part,...  15.9 us
    ppermute x6, starting transfers between devices, across(): return lax.ppermute(x, 'seq', turn)  14 us
    all_to_all x1, waiting for transfers between devices, per_device(): lax.all_to_all(query_local, 'seq', split_axis=0, concat_axis=0, tiled=True)  9.59 us
    ppermute x6, starting transfers between devices, inside(): return lax.ppermute(x, 'seq', turn)  6.93 us
    all_to_all x1, starting transfers between devices, per_device(): lax.all_to_all(query_local, 'seq', split_axis=0, concat_axis=0, tiled=True)  6.05 us
    ppermute x6, waiting for transfers between devices, across(): return lax.ppermute(x, 'seq', turn)  5.56 us
    all_to_all x1, starting transfers between devices, per_device(): grad = lax.all_to_all(send, 'seq', split_axis=0, concat_axis=0, tiled=True)  4.81 us
  transfers between devices with their start and end apart: 14, of which 7 were waited for; matrix products, arithmetic and copies ran while one was open for 0% of the time, Pallas kernels for 3%

profile of v4, /device:TPU:0, one launch (start us, length us, event | category | flops | bytes accessed | tf_op | source)
XLA Modules:
  0.0 101.6 jit_solution(16238730002391287421)
XLA Ops:
  0.7 1.0 constant_dynamic-slice_fusion.6
  1.7 4.1 %collective-permute-start.1 = (bf16[128,256]{1,0:T(8,128)(2,1)S(1)}, bf16[128,256]{1,0:T(8,128)(2,1)S(1)}, u32[]{:S(2)}, u32[]{:S(2)}) collective-permute-start(bf16[128,256]{1,0:T(8,128)(2,1)S(1)} %pad_maximum_fusion.2), channel_id=1, source_target_pairs={{0,8},{1,9},{2,10},{3,11},{4,12},{5,13},{6,14},{7,15},{8,0},{9,1},... | collective-permute-start | bytes 196616 | tf_op jit(solution)/shard_map/ppermute | solution.py:212
  5.8 1.4 %collective-permute-start.2 = (bf16[128,256]{1,0:T(8,128)(2,1)S(1)}, bf16[128,256]{1,0:T(8,128)(2,1)S(1)}, u32[]{:S(2)}, u32[]{:S(2)}) collective-permute-start(bf16[128,256]{1,0:T(8,128)(2,1)S(1)} %pad_maximum_fusion.3), channel_id=1, source_target_pairs={{0,12},{1,13},{2,14},{3,15},{4,0},{5,1},{6,2},{7,3},{8,4},{9,5},{1... | collective-permute-start | bytes 196616 | tf_op jit(solution)/shard_map/ppermute | solution.py:212
  7.3 0.7 collective-permute-start
  8.0 1.2 %copy-done.2 = bf16[128,4096]{1,0:T(8,128)(2,1)S(1)} copy-done((bf16[128,4096]{1,0:T(8,128)(2,1)S(1)}, bf16[128,4096]{1,0:T(8,128)(2,1)}, u32[]{:S(2)}) %copy-start.2) | copy-done | bytes 1048600
  9.2 1.9 %shard_map.85 = bf16[16,136,256]{2,1,0:T(8,128)(2,1)} custom-call(bf16[128,4096]{1,0:T(8,128)(2,1)S(1)} %copy-done.1, bf16[128,4096]{1,0:T(8,128)(2,1)S(1)} %copy-done.2), custom_call_target="tpu_custom_call" | custom-call | bytes 4194304 | tf_op jit(solution)/shard_map/pallas_call | solution.py:60
  11.2 2.2 %collective-permute-done = bf16[128,256]{1,0:T(8,128)(2,1)S(1)} collective-permute-done((bf16[128,256]{1,0:T(8,128)(2,1)S(1)}, bf16[128,256]{1,0:T(8,128)(2,1)S(1)}, u32[]{:S(2)}, u32[]{:S(2)}) %collective-permute-start) | collective-permute-done | bytes 65568 | tf_op jit(solution)/shard_map/ppermute | solution.py:212
  13.4 0.0 copy-start.3
  13.4 0.0 copy-start.4
  13.4 4.8 %all-to-all-start = ((bf16[16,136,256]{2,1,0:T(8,128)(2,1)}), bf16[16,136,256]{2,1,0:T(8,128)(2,1)S(1)}, u32[]{:S(2)}, u32[]{:S(2)}) async-start(bf16[16,136,256]{2,1,0:T(8,128)(2,1)} %shard_map.85), calls=%async_computation | async-start | bytes 2228224 | tf_op jit(solution)/shard_map/all_to_all | solution.py:232
  18.3 2.8 %collective-permute-start.5 = (bf16[4,128,256]{2,1,0:T(8,128)(2,1)S(1)}, bf16[4,128,256]{2,1,0:T(8,128)(2,1)S(1)}, u32[]{:S(2)}, u32[]{:S(2)}) collective-permute-start(bf16[4,128,256]{2,1,0:T(8,128)(2,1)S(1)} %pad_maximum_fusion.refs_0_), channel_id=1, source_target_pairs={{0,3},{1,0},{2,1},{3,2},{4,7},{5,4},{6,5},{7,6},{8,11},{9,8},{10,9... | collective-permute-start | bytes 786440 | tf_op jit(solution)/shard_map/ppermute | solution.py:216
  21.1 0.6 collective-permute-start.4
  21.7 0.6 collective-permute-start.3
  22.2 0.1 pad_add_fusion.pos_ref
  22.3 14.2 %collective-permute-done.5.refs_3_ = bf16[4,128,256]{2,1,0:T(8,128)(2,1)S(1)} collective-permute-done((bf16[4,128,256]{2,1,0:T(8,128)(2,1)S(1)}, bf16[4,128,256]{2,1,0:T(8,128)(2,1)S(1)}, u32[]{:S(2)}, u32[]{:S(2)}) %collective-permute-start.5) | collective-permute-done | bytes 262176 | tf_op jit(solution)/shard_map/ppermute | solution.py:216
  36.5 2.9 %collective-permute-done.4.refs_2_ = bf16[4,128,256]{2,1,0:T(8,128)(2,1)S(1)} collective-permute-done((bf16[4,128,256]{2,1,0:T(8,128)(2,1)S(1)}, bf16[4,128,256]{2,1,0:T(8,128)(2,1)S(1)}, u32[]{:S(2)}, u32[]{:S(2)}) %collective-permute-start.4) | collective-permute-done | bytes 262176 | tf_op jit(solution)/shard_map/ppermute | solution.py:216
  39.4 6.1 %collective-permute-done.3.refs_1_ = bf16[4,128,256]{2,1,0:T(8,128)(2,1)S(1)} collective-permute-done((bf16[4,128,256]{2,1,0:T(8,128)(2,1)S(1)}, bf16[4,128,256]{2,1,0:T(8,128)(2,1)S(1)}, u32[]{:S(2)}, u32[]{:S(2)}) %collective-permute-start.3) | collective-permute-done | bytes 262176 | tf_op jit(solution)/shard_map/ppermute | solution.py:216
  45.4 0.7 copy-done.8
  46.1 15.9 %shard_map.86 = (bf16[2048,256]{1,0:T(8,128)(2,1)}, bf16[4,128,256]{2,1,0:T(8,128)(2,1)S(1)}, bf16[4,128,256]{2,1,0:T(8,128)(2,1)S(1)}, bf16[4,128,256]{2,1,0:T(8,128)(2,1)S(1)}, bf16[4,128,256]{2,1,0:T(8,128)(2,1)S(1)}) custom-call(s32[2]{0:T(128)S(1)} %pad_add_fusion.pos_ref, bf16[2048,256]{1,0:T(8,128)(2,1)S(1)} %copy-done.3, ...), custom_call_target="tpu_custom_call" | custom-call | flops 5368709120 | bytes 4194304 | tf_op jit(solution)/shard_map/pallas_call | solution.py:139
  62.1 0.4 collective-permute-start.6
  62.5 1.4 %collective-permute-start.7 = (bf16[4,128,256]{2,1,0:T(8,128)(2,1)S(1)}, bf16[4,128,256]{2,1,0:T(8,128)(2,1)S(1)}, u32[]{:S(2)}, u32[]{:S(2)}) collective-permute-start(bf16[4,128,256]{2,1,0:T(8,128)(2,1)S(1)} %get-tuple-element.21), channel_id=1, source_target_pairs={{0,2},{1,3},{2,0},{3,1},{4,6},{5,7},{6,4},{7,5},{8,10},{9,11},{10,... | collective-permute-start | bytes 786440 | tf_op jit(solution)/shard_map/ppermute | solution.py:216
  63.9 1.1 %collective-permute-start.8 = (bf16[4,128,256]{2,1,0:T(8,128)(2,1)S(1)}, bf16[4,128,256]{2,1,0:T(8,128)(2,1)S(1)}, u32[]{:S(2)}, u32[]{:S(2)}) collective-permute-start(bf16[4,128,256]{2,1,0:T(8,128)(2,1)S(1)} %get-tuple-element.22), channel_id=1, source_target_pairs={{0,3},{1,0},{2,1},{3,2},{4,7},{5,4},{6,5},{7,6},{8,11},{9,8},{10,9... | collective-permute-start | bytes 786440 | tf_op jit(solution)/shard_map/ppermute | solution.py:216
  65.0 6.1 %all-to-all-start.1 = ((bf16[16,128,256]{2,1,0:T(8,128)(2,1)}), bf16[16,128,256]{2,1,0:T(8,128)(2,1)S(1)}, u32[]{:S(2)}, u32[]{:S(2)}) async-start(bf16[16,128,256]{2,1,0:T(8,128)(2,1)} %bitcast.6), calls=%async_computation.1 | async-start | bytes 2097152 | tf_op jit(solution)/shard_map/all_to_all | solution.py:236
  71.1 7.6 %collective-permute-done.7.refs_2_ = bf16[4,128,256]{2,1,0:T(8,128)(2,1)S(1)} collective-permute-done((bf16[4,128,256]{2,1,0:T(8,128)(2,1)S(1)}, bf16[4,128,256]{2,1,0:T(8,128)(2,1)S(1)}, u32[]{:S(2)}, u32[]{:S(2)}) %collective-permute-start.7) | collective-permute-done | bytes 262176 | tf_op jit(solution)/shard_map/ppermute | solution.py:216
  78.7 0.7 shard_map.87
  79.4 0.3 collective-permute-start.9
  79.7 7.5 %collective-permute-start.10 = (bf16[128,256]{1,0:T(8,128)(2,1)S(1)}, bf16[128,256]{1,0:T(8,128)(2,1)S(1)}, u32[]{:S(2)}, u32[]{:S(2)}) collective-permute-start(bf16[128,256]{1,0:T(8,128)(2,1)S(1)} %get-tuple-element.25), channel_id=1, source_target_pairs={{0,8},{1,9},{2,10},{3,11},{4,12},{5,13},{6,14},{7,15},{8,0},{9,1},... | collective-permute-start | bytes 196616 | tf_op jit(solution)/shard_map/ppermute | solution.py:212
  87.2 9.6 %all-to-all-done.1 = bf16[16,128,256]{2,1,0:T(8,128)(2,1)S(1)} async-done(((bf16[16,128,256]{2,1,0:T(8,128)(2,1)}), bf16[16,128,256]{2,1,0:T(8,128)(2,1)S(1)}, u32[]{:S(2)}, u32[]{:S(2)}) %all-to-all-start.1) | async-done | bytes 1048608 | tf_op jit(solution)/shard_map/all_to_all | solution.py:236
  96.8 0.1 copy.11
  96.9 0.0 copy-start
  96.9 3.4 %collective-permute-done.10.refs_2_ = bf16[128,256]{1,0:T(8,128)(2,1)S(1)} collective-permute-done((bf16[128,256]{1,0:T(8,128)(2,1)S(1)}, bf16[128,256]{1,0:T(8,128)(2,1)S(1)}, u32[]{:S(2)}, u32[]{:S(2)}) %collective-permute-start.10) | collective-permute-done | bytes 65568 | tf_op jit(solution)/shard_map/ppermute | solution.py:212
  100.3 1.3 %shard_map.88 = (bf16[128,512]{1,0:T(8,128)(2,1)}, bf16[128,512]{1,0:T(8,128)(2,1)}) custom-call(s32[2]{0:T(128)S(1)} %pad_add_fusion.pos_ref, bf16[128,256]{1,0:T(8,128)(2,1)S(1)} %get-tuple-element.23.refs_0_, bf16[128,256]{1,0:T(8,128)(2,1)S(1)} %collective-permute-done.9.refs_1_, bf16[128,256]{1,0:T(8,128)(2,1)S(1)} %collective-permute-done.10.refs_2_, ...), custom_call_target="tpu_custom_call" | custom-call | bytes 4194304 | tf_op jit(solution)/shard_map/pallas_call | solution.py:193
  (26 shorter events, 0.1 us)
Async XLA Ops:
  0.6 7.4 %copy-start.1 = (bf16[128,4096]{1,0:T(8,128)(2,1)S(1)}, bf16[128,4096]{1,0:T(8,128)(2,1)}, u32[]{:S(2)}) copy-start(bf16[128,4096]{1,0:T(8,128)(2,1)} %o_ref.1) | copy-start | bytes 3145732
  1.7 9.5 %collective-permute-start.1 = (bf16[128,256]{1,0:T(8,128)(2,1)S(1)}, bf16[128,256]{1,0:T(8,128)(2,1)S(1)}, u32[]{:S(2)}, u32[]{:S(2)}) collective-permute-start(bf16[128,256]{1,0:T(8,128)(2,1)S(1)} %pad_maximum_fusion.2), channel_id=1, source_target_pairs={{0,8},{1,9},{2,10},{3,11},{4,12},{5,13},{6,14},{7,15},{8,0},{9,1},... | collective-permute-start | bytes 196616 | tf_op jit(solution)/shard_map/ppermute | solution.py:212
  5.8 5.3 %collective-permute-start.2 = (bf16[128,256]{1,0:T(8,128)(2,1)S(1)}, bf16[128,256]{1,0:T(8,128)(2,1)S(1)}, u32[]{:S(2)}, u32[]{:S(2)}) collective-permute-start(bf16[128,256]{1,0:T(8,128)(2,1)S(1)} %pad_maximum_fusion.3), channel_id=1, source_target_pairs={{0,12},{1,13},{2,14},{3,15},{4,0},{5,1},{6,2},{7,3},{8,4},{9,5},{1... | collective-permute-start | bytes 196616 | tf_op jit(solution)/shard_map/ppermute | solution.py:212
  7.3 6.1 %collective-permute-start = (bf16[128,256]{1,0:T(8,128)(2,1)S(1)}, bf16[128,256]{1,0:T(8,128)(2,1)S(1)}, u32[]{:S(2)}, u32[]{:S(2)}) collective-permute-start(bf16[128,256]{1,0:T(8,128)(2,1)S(1)} %pad_maximum_fusion.1), channel_id=1, source_target_pairs={{0,4},{1,5},{2,6},{3,7},{4,8},{5,9},{6,10},{7,11},{8,12},{9,13},{1... | collective-permute-start | bytes 196616 | tf_op jit(solution)/shard_map/ppermute | solution.py:212
  8.0 1.2 %copy-start.2 = (bf16[128,4096]{1,0:T(8,128)(2,1)S(1)}, bf16[128,4096]{1,0:T(8,128)(2,1)}, u32[]{:S(2)}) copy-start(bf16[128,4096]{1,0:T(8,128)(2,1)} %g_ref.1) | copy-start | bytes 3145732
  13.4 8.2 %copy-start.5 = (bf16[4,128,256]{2,1,0:T(8,128)(2,1)}, bf16[4,128,256]{2,1,0:T(8,128)(2,1)S(1)}, u32[]{:S(2)}) copy-start(bf16[4,128,256]{2,1,0:T(8,128)(2,1)S(1)} %pad_maximum_fusion.refs_0_) | copy-start | bytes 786436
  13.4 32.7 %copy-start.3 = (bf16[2048,256]{1,0:T(8,128)(2,1)S(1)}, bf16[2048,256]{1,0:T(8,128)(2,1)}, u32[]{:S(2)}) copy-start(bf16[2048,256]{1,0:T(8,128)(2,1)} %q_ref.1) | copy-start | bytes 3145732
  13.4 32.7 %copy-start.4 = (f32[2,2048]{1,0:T(2,128)S(1)}, f32[2,2048]{1,0:T(2,128)}, u32[]{:S(2)}) copy-start(f32[2,2048]{1,0:T(2,128)} %lse_ref.1) | copy-start | bytes 49156
  13.4 32.7 %all-to-all-start = ((bf16[16,136,256]{2,1,0:T(8,128)(2,1)}), bf16[16,136,256]{2,1,0:T(8,128)(2,1)S(1)}, u32[]{:S(2)}, u32[]{:S(2)}) async-start(bf16[16,136,256]{2,1,0:T(8,128)(2,1)} %shard_map.85), calls=%async_computation | async-start | bytes 2228224 | tf_op jit(solution)/shard_map/all_to_all | solution.py:232
  18.3 18.2 %collective-permute-start.5 = (bf16[4,128,256]{2,1,0:T(8,128)(2,1)S(1)}, bf16[4,128,256]{2,1,0:T(8,128)(2,1)S(1)}, u32[]{:S(2)}, u32[]{:S(2)}) collective-permute-start(bf16[4,128,256]{2,1,0:T(8,128)(2,1)S(1)} %pad_maximum_fusion.refs_0_), channel_id=1, source_target_pairs={{0,3},{1,0},{2,1},{3,2},{4,7},{5,4},{6,5},{7,6},{8,11},{9,8},{10,9... | collective-permute-start | bytes 786440 | tf_op jit(solution)/shard_map/ppermute | solution.py:216
  21.1 18.3 %collective-permute-start.4 = (bf16[4,128,256]{2,1,0:T(8,128)(2,1)S(1)}, bf16[4,128,256]{2,1,0:T(8,128)(2,1)S(1)}, u32[]{:S(2)}, u32[]{:S(2)}) collective-permute-start(bf16[4,128,256]{2,1,0:T(8,128)(2,1)S(1)} %pad_maximum_fusion.refs_0_), channel_id=1, source_target_pairs={{0,2},{1,3},{2,0},{3,1},{4,6},{5,7},{6,4},{7,5},{8,10},{9,11},{10,... | collective-permute-start | bytes 786440 | tf_op jit(solution)/shard_map/ppermute | solution.py:216
  21.7 23.8 %collective-permute-start.3 = (bf16[4,128,256]{2,1,0:T(8,128)(2,1)S(1)}, bf16[4,128,256]{2,1,0:T(8,128)(2,1)S(1)}, u32[]{:S(2)}, u32[]{:S(2)}) collective-permute-start(bf16[4,128,256]{2,1,0:T(8,128)(2,1)S(1)} %pad_maximum_fusion.refs_0_), channel_id=1, source_target_pairs={{0,1},{1,2},{2,3},{3,0},{4,5},{5,6},{6,7},{7,4},{8,9},{9,10},{10,1... | collective-permute-start | bytes 786440 | tf_op jit(solution)/shard_map/ppermute | solution.py:216
  36.5 8.9 %copy-start.6 = (bf16[4,128,256]{2,1,0:T(8,128)(2,1)}, bf16[4,128,256]{2,1,0:T(8,128)(2,1)S(1)}, u32[]{:S(2)}) copy-start(bf16[4,128,256]{2,1,0:T(8,128)(2,1)S(1)} %collective-permute-done.5.refs_3_) | copy-start | bytes 786436
  39.4 6.1 %copy-start.7 = (bf16[4,128,256]{2,1,0:T(8,128)(2,1)}, bf16[4,128,256]{2,1,0:T(8,128)(2,1)S(1)}, u32[]{:S(2)}) copy-start(bf16[4,128,256]{2,1,0:T(8,128)(2,1)S(1)} %collective-permute-done.4.refs_2_) | copy-start | bytes 786436
  45.4 0.7 copy-start.8
  62.1 9.0 %collective-permute-start.6 = (bf16[4,128,256]{2,1,0:T(8,128)(2,1)S(1)}, bf16[4,128,256]{2,1,0:T(8,128)(2,1)S(1)}, u32[]{:S(2)}, u32[]{:S(2)}) collective-permute-start(bf16[4,128,256]{2,1,0:T(8,128)(2,1)S(1)} %get-tuple-element.20), channel_id=1, source_target_pairs={{0,1},{1,2},{2,3},{3,0},{4,5},{5,6},{6,7},{7,4},{8,9},{9,10},{10,1... | collective-permute-start | bytes 786440 | tf_op jit(solution)/shard_map/ppermute | solution.py:216
  62.5 16.2 %collective-permute-start.7 = (bf16[4,128,256]{2,1,0:T(8,128)(2,1)S(1)}, bf16[4,128,256]{2,1,0:T(8,128)(2,1)S(1)}, u32[]{:S(2)}, u32[]{:S(2)}) collective-permute-start(bf16[4,128,256]{2,1,0:T(8,128)(2,1)S(1)} %get-tuple-element.21), channel_id=1, source_target_pairs={{0,2},{1,3},{2,0},{3,1},{4,6},{5,7},{6,4},{7,5},{8,10},{9,11},{10,... | collective-permute-start | bytes 786440 | tf_op jit(solution)/shard_map/ppermute | solution.py:216
  63.9 14.8 %collective-permute-start.8 = (bf16[4,128,256]{2,1,0:T(8,128)(2,1)S(1)}, bf16[4,128,256]{2,1,0:T(8,128)(2,1)S(1)}, u32[]{:S(2)}, u32[]{:S(2)}) collective-permute-start(bf16[4,128,256]{2,1,0:T(8,128)(2,1)S(1)} %get-tuple-element.22), channel_id=1, source_target_pairs={{0,3},{1,0},{2,1},{3,2},{4,7},{5,4},{6,5},{7,6},{8,11},{9,8},{10,9... | collective-permute-start | bytes 786440 | tf_op jit(solution)/shard_map/ppermute | solution.py:216
  65.0 31.7 %all-to-all-start.1 = ((bf16[16,128,256]{2,1,0:T(8,128)(2,1)}), bf16[16,128,256]{2,1,0:T(8,128)(2,1)S(1)}, u32[]{:S(2)}, u32[]{:S(2)}) async-start(bf16[16,128,256]{2,1,0:T(8,128)(2,1)} %bitcast.6), calls=%async_computation.1 | async-start | bytes 2097152 | tf_op jit(solution)/shard_map/all_to_all | solution.py:236
  79.4 17.5 %collective-permute-start.9 = (bf16[128,256]{1,0:T(8,128)(2,1)S(1)}, bf16[128,256]{1,0:T(8,128)(2,1)S(1)}, u32[]{:S(2)}, u32[]{:S(2)}) collective-permute-start(bf16[128,256]{1,0:T(8,128)(2,1)S(1)} %get-tuple-element.24), channel_id=1, source_target_pairs={{0,4},{1,5},{2,6},{3,7},{4,8},{5,9},{6,10},{7,11},{8,12},{9,13},{1... | collective-permute-start | bytes 196616 | tf_op jit(solution)/shard_map/ppermute | solution.py:212
  79.7 20.6 %collective-permute-start.10 = (bf16[128,256]{1,0:T(8,128)(2,1)S(1)}, bf16[128,256]{1,0:T(8,128)(2,1)S(1)}, u32[]{:S(2)}, u32[]{:S(2)}) collective-permute-start(bf16[128,256]{1,0:T(8,128)(2,1)S(1)} %get-tuple-element.25), channel_id=1, source_target_pairs={{0,8},{1,9},{2,10},{3,11},{4,12},{5,13},{6,14},{7,15},{8,0},{9,1},... | collective-permute-start | bytes 196616 | tf_op jit(solution)/shard_map/ppermute | solution.py:212
  87.2 13.1 %collective-permute-start.11 = (bf16[128,256]{1,0:T(8,128)(2,1)S(1)}, bf16[128,256]{1,0:T(8,128)(2,1)S(1)}, u32[]{:S(2)}, u32[]{:S(2)}) collective-permute-start(bf16[128,256]{1,0:T(8,128)(2,1)S(1)} %get-tuple-element.26), channel_id=1, source_target_pairs={{0,12},{1,13},{2,14},{3,15},{4,0},{5,1},{6,2},{7,3},{8,4},{9,5},{1... | collective-permute-start | bytes 196616 | tf_op jit(solution)/shard_map/ppermute | solution.py:212
  96.9 4.7 %copy-start = (bf16[16,16,8,256]{3,2,0,1:T(8,128)(2,1)}, bf16[16,16,8,256]{3,2,0,1:T(8,128)(2,1)S(1)}, u32[]{:S(2)}) copy-start(bf16[16,16,8,256]{3,2,0,1:T(8,128)(2,1)S(1)} %copy.11) | copy-start | bytes 3145732

commit v5 on v4

--- a/solution.py
+++ b/solution.py
@@ -50,16 +50,19 @@
             high = prod.astype(jnp.bfloat16)
             low = (prod - high.astype(jnp.float32)).astype(jnp.bfloat16)
             delta = (dot(high, ones, NN) + dot(low, ones, NN)).T
-            if width > rows:
-                fill = jnp.zeros((128, width - rows), jnp.float32)
+            if DH > rows:
+                fill = jnp.zeros((128, DH - rows), jnp.float32)
                 delta = jnp.concatenate([delta, fill], axis=1)
             for d in range(here):
-                send_ref[n + d, :rows] = g_ref[:, (n + d) * width : (n + d + 1) * width]
-                send_ref[n + d, rows:] = delta[d * pad : (d + 1) * pad].astype(jnp.bfloat16)
+                for h in range(heads_here):
+                    c = slice((n + d) * width + h * DH, (n + d) * width + (h + 1) * DH)
+                    send_ref[n + d, h * rows : (h + 1) * rows] = g_ref[:, c]
+                low = delta[d * pad : (d + 1) * pad].astype(jnp.bfloat16)
+                send_ref[n + d, heads_here * rows :] = low
 
     return call(
         body,
-        jax.ShapeDtypeStruct((seq_count, rows + pad, width), jnp.bfloat16),
+        jax.ShapeDtypeStruct((seq_count, heads_here * rows + pad, DH), jnp.bfloat16),
         [VMEM, VMEM],
         VMEM,
     )(out, grad)
@@ -89,7 +92,7 @@
                 coming.append(copy)
         l_ref[...] = lse_ref[...] * LOG2E
         for n in range(total // rows):
-            d_ref[:, n * rows : (n + 1) * rows] = g_ref[n, rows:, :rows].astype(jnp.float32)
+            d_ref[:, n * rows : (n + 1) * rows] = g_ref[n, heads * rows :, :rows].astype(jnp.float32)
         for copy in coming:
             copy.wait()
         for k0 in range(0, total, block):
@@ -104,7 +107,7 @@
                 for h in range(heads):
                     c = slice(h * DH, (h + 1) * DH)
                     qb = q_ref[q0:q1, c]
-                    gb = g_ref[n0 : n0 + owners, :rows, c].reshape(block, DH)
+                    gb = g_ref[n0 : n0 + owners, h * rows : (h + 1) * rows].reshape(block, DH)
                     s = dot(kb, qb, NT) * (SCALE * LOG2E) - l_ref[h : h + 1, q0:q1]
                     if k1 > q0:
                         key_ids = k0 + lax.broadcasted_iota(jnp.int32, s.shape, 0)
@@ -122,13 +125,11 @@
                         acc_ref[c, q0:q1] = t
                     else:
                         acc_ref[c, q0:q1] += t
+                    if q0 == k0:
+                        done = (acc_ref[c, q0:q1] * SCALE).astype(jnp.bfloat16)
+                        dq_ref[q0:q1, c] = done.T
             dkv_ref[k0:k1, :DH] = (dk * SCALE).astype(jnp.bfloat16)
             dkv_ref[k0:k1, DH:] = dv.astype(jnp.bfloat16)
-        for h in range(heads):
-            c = slice(h * DH, (h + 1) * DH)
-            for q0 in range(0, total, block):
-                q1 = q0 + block
-                dq_ref[q0:q1, c] = (acc_ref[c, q0:q1] * SCALE).T.astype(jnp.bfloat16)
         for s in range(copies):
             target = lax.rem(place + s, copies)
             for r in range(planes):
@@ -147,12 +148,21 @@
             pltpu.VMEM((total, 2 * DH), jnp.bfloat16),
             pltpu.VMEM((DH, total), jnp.bfloat16),
             pltpu.VMEM(lse.shape, jnp.float32),
-            pltpu.VMEM((g.shape[1] - rows, total), jnp.float32),
+            pltpu.VMEM((g.shape[1] - heads * rows, total), jnp.float32),
             pltpu.VMEM((width, total), jnp.float32),
             pltpu.VMEM((total, 2 * DH), jnp.bfloat16),
             pltpu.SemaphoreType.DMA((copies, planes)),
         ],
     )(pos, q, g, lse, *pieces)
+
+
+def stack(blocks):
+    def body(*refs):
+        for n, ref in enumerate(refs[:-1]):
+            refs[-1][n] = ref[...]
+
+    out = jax.ShapeDtypeStruct((len(blocks),) + blocks[0].shape, jnp.bfloat16)
+    return call(body, out, [VMEM] * len(blocks), VMEM, flops=int(20e9))(*blocks)
 
 
 def reduce_kv(pos, parts):
@@ -225,9 +235,8 @@
     for r in range(kv_heads):
         both = jnp.concatenate([columns(key_seq, plane + r), columns(value_seq, plane + r)], axis=1)
         got.append(across(both, r) if r else both)
-    mine = jnp.stack(got)
+    mine = stack(got)
     send = pack(attn_out, grad_out, seq_count, heads_here, pad)
-    send, mine = lax.optimization_barrier((send, mine))
     pieces = [mine] + [inside(mine, s) for s in range(1, copies)]
     grad = lax.all_to_all(send, "seq", split_axis=0, concat_axis=0, tiled=True)
     pieces = [pltpu.with_memory_space_constraint(x, pltpu.HBM) for x in pieces]

time: 102 us -> 99.5 us (0.975)
  waiting for transfers between devices: 45.9 us -> 41.4 us
  starting transfers between devices: 31.8 us -> 33.8 us
    ppermute x6, starting transfers between devices: 14 us -> 16.6 us  [across(): return lax.ppermute(x, 'seq', turn)]
    ppermute x6, waiting for transfers between devices: 30.7 us -> 28.4 us  [inside(): return lax.ppermute(x, 'seq', turn)]
    ppermute x6, waiting for transfers between devices: 5.56 us -> 3.39 us  [across(): return lax.ppermute(x, 'seq', turn)]
    pallas_call x1 -> x2, Pallas kernels: 1.95 us -> 2.08 us  [the longest x1 2.06 us: pack(): call(body, jax.ShapeDtypeStruct((seq_count, heads_here * rows + pad, DH),...]
  transfers between devices with their start and end apart: 14 -> 14, of which waited for: 7 -> 6; matrix products, arithmetic and copies ran while one was open for 0% -> 0% of each run, Pallas kernels for 3% -> 3%
where the time goes in v5:
time: 99.5 us; the launch traced here: 99.1 us
  waiting for transfers between devices  41.4 us (42%)
  starting transfers between devices  33.8 us (34%)
  Pallas kernels  19.9 us (20%)
  local copies, waits for them, and re-layouts  3.05 us (3%)
    ppermute x6, waiting for transfers between devices, inside(): return lax.ppermute(x, 'seq', turn)  28.4 us
    ppermute x6, starting transfers between devices, across(): return lax.ppermute(x, 'seq', turn)  16.6 us
    pallas_call x1, Pallas kernels, attend(): call(body, (jax.ShapeDtypeStruct((total, width), jnp.bfloat16),) + (part,...  15.9 us
    all_to_all x1, waiting for transfers between devices, per_device(): lax.all_to_all(query_local, 'seq', split_axis=0, concat_axis=0, tiled=True)  9.6 us
    ppermute x6, starting transfers between devices, inside(): return lax.ppermute(x, 'seq', turn)  6.98 us
    all_to_all x1, starting transfers between devices, per_device(): lax.all_to_all(query_local, 'seq', split_axis=0, concat_axis=0, tiled=True)  6.34 us
    all_to_all x1, starting transfers between devices, per_device(): grad = lax.all_to_all(send, 'seq', split_axis=0, concat_axis=0, tiled=True)  3.83 us
    ppermute x6, waiting for transfers between devices, across(): return lax.ppermute(x, 'seq', turn)  3.39 us
  transfers between devices with their start and end apart: 14, of which 6 were waited for; matrix products, arithmetic and copies ran while one was open for 0% of the time, Pallas kernels for 3%

profile of v5, /device:TPU:0, one launch (start us, length us, event | category | flops | bytes accessed | tf_op | source)
XLA Modules:
  0.0 99.1 jit_solution(17180189083929672177)
XLA Ops:
  0.7 1.0 constant_dynamic-slice_fusion
  1.7 4.1 %collective-permute-start.1 = (bf16[128,256]{1,0:T(8,128)(2,1)S(1)}, bf16[128,256]{1,0:T(8,128)(2,1)S(1)}, u32[]{:S(2)}, u32[]{:S(2)}) collective-permute-start(bf16[128,256]{1,0:T(8,128)(2,1)S(1)} %pad_maximum_fusion.2), channel_id=1, source_target_pairs={{0,8},{1,9},{2,10},{3,11},{4,12},{5,13},{6,14},{7,15},{8,0},{9,1},... | collective-permute-start | bytes 196616 | tf_op jit(solution)/shard_map/ppermute | solution.py:222
  5.8 1.6 %collective-permute-start = (bf16[128,256]{1,0:T(8,128)(2,1)S(1)}, bf16[128,256]{1,0:T(8,128)(2,1)S(1)}, u32[]{:S(2)}, u32[]{:S(2)}) collective-permute-start(bf16[128,256]{1,0:T(8,128)(2,1)S(1)} %pad_maximum_fusion.1), channel_id=1, source_target_pairs={{0,4},{1,5},{2,6},{3,7},{4,8},{5,9},{6,10},{7,11},{8,12},{9,13},{1... | collective-permute-start | bytes 196616 | tf_op jit(solution)/shard_map/ppermute | solution.py:222
  7.5 2.3 %collective-permute-start.2 = (bf16[128,256]{1,0:T(8,128)(2,1)S(1)}, bf16[128,256]{1,0:T(8,128)(2,1)S(1)}, u32[]{:S(2)}, u32[]{:S(2)}) collective-permute-start(bf16[128,256]{1,0:T(8,128)(2,1)S(1)} %pad_maximum_fusion.3), channel_id=1, source_target_pairs={{0,12},{1,13},{2,14},{3,15},{4,0},{5,1},{6,2},{7,3},{8,4},{9,5},{1... | collective-permute-start | bytes 196616 | tf_op jit(solution)/shard_map/ppermute | solution.py:222
  9.8 1.2 %copy-done.2 = bf16[128,4096]{1,0:T(8,128)(2,1)S(1)} copy-done((bf16[128,4096]{1,0:T(8,128)(2,1)S(1)}, bf16[128,4096]{1,0:T(8,128)(2,1)}, u32[]{:S(2)}) %copy-start.2) | copy-done | bytes 1048600
  11.0 2.1 %shard_map.85 = bf16[16,264,128]{2,1,0:T(8,128)(2,1)} custom-call(bf16[128,4096]{1,0:T(8,128)(2,1)S(1)} %copy-done.1, bf16[128,4096]{1,0:T(8,128)(2,1)S(1)} %copy-done.2), custom_call_target="tpu_custom_call" | custom-call | bytes 4194304 | tf_op jit(solution)/shard_map/pallas_call | solution.py:63
  13.1 3.8 %all-to-all-start = ((bf16[16,264,128]{2,1,0:T(8,128)(2,1)}), bf16[16,264,128]{2,1,0:T(8,128)(2,1)S(1)}, u32[]{:S(2)}, u32[]{:S(2)}) async-start(bf16[16,264,128]{2,1,0:T(8,128)(2,1)} %shard_map.85), calls=%async_computation | async-start | bytes 2162688 | tf_op jit(solution)/shard_map/all_to_all | solution.py:241
  16.9 0.0 copy-start.3
  16.9 0.0 copy-start.5
  17.0 0.0 collective-permute-done.1.refs_2_
  17.0 2.9 %collective-permute-start.5 = (bf16[4,128,256]{2,1,0:T(8,128)(2,1)S(1)}, bf16[4,128,256]{2,1,0:T(8,128)(2,1)S(1)}, u32[]{:S(2)}, u32[]{:S(2)}) collective-permute-start(bf16[4,128,256]{2,1,0:T(8,128)(2,1)S(1)} %shard_map.86.refs_0_), channel_id=1, source_target_pairs={{0,3},{1,0},{2,1},{3,2},{4,7},{5,4},{6,5},{7,6},{8,11},{9,8},{10,9... | collective-permute-start | bytes 786440 | tf_op jit(solution)/shard_map/ppermute | solution.py:226
  19.9 0.6 collective-permute-start.4
  20.5 0.6 collective-permute-start.3
  21.0 0.1 pad_add_fusion.pos_ref
  21.1 13.9 %collective-permute-done.5.refs_3_ = bf16[4,128,256]{2,1,0:T(8,128)(2,1)S(1)} collective-permute-done((bf16[4,128,256]{2,1,0:T(8,128)(2,1)S(1)}, bf16[4,128,256]{2,1,0:T(8,128)(2,1)S(1)}, u32[]{:S(2)}, u32[]{:S(2)}) %collective-permute-start.5) | collective-permute-done | bytes 262176 | tf_op jit(solution)/shard_map/ppermute | solution.py:226
  35.0 2.0 %collective-permute-done.4.refs_2_ = bf16[4,128,256]{2,1,0:T(8,128)(2,1)S(1)} collective-permute-done((bf16[4,128,256]{2,1,0:T(8,128)(2,1)S(1)}, bf16[4,128,256]{2,1,0:T(8,128)(2,1)S(1)}, u32[]{:S(2)}, u32[]{:S(2)}) %collective-permute-start.4) | collective-permute-done | bytes 262176 | tf_op jit(solution)/shard_map/ppermute | solution.py:226
  36.9 5.8 %collective-permute-done.3.refs_1_ = bf16[4,128,256]{2,1,0:T(8,128)(2,1)S(1)} collective-permute-done((bf16[4,128,256]{2,1,0:T(8,128)(2,1)S(1)}, bf16[4,128,256]{2,1,0:T(8,128)(2,1)S(1)}, u32[]{:S(2)}, u32[]{:S(2)}) %collective-permute-start.3) | collective-permute-done | bytes 262176 | tf_op jit(solution)/shard_map/ppermute | solution.py:226
  42.7 0.7 copy-done.8
  43.4 15.9 %shard_map.87 = (bf16[2048,256]{1,0:T(8,128)(2,1)}, bf16[4,128,256]{2,1,0:T(8,128)(2,1)S(1)}, bf16[4,128,256]{2,1,0:T(8,128)(2,1)S(1)}, bf16[4,128,256]{2,1,0:T(8,128)(2,1)S(1)}, bf16[4,128,256]{2,1,0:T(8,128)(2,1)S(1)}) custom-call(s32[2]{0:T(128)S(1)} %pad_add_fusion.pos_ref, bf16[2048,256]{1,0:T(8,128)(2,1)S(1)} %copy-done.3, ...), custom_call_target="tpu_custom_call" | custom-call | flops 5368709120 | bytes 4194304 | tf_op jit(solution)/shard_map/pallas_call | solution.py:140
  59.3 0.8 collective-permute-start.6
  60.1 1.3 %collective-permute-start.7 = (bf16[4,128,256]{2,1,0:T(8,128)(2,1)S(1)}, bf16[4,128,256]{2,1,0:T(8,128)(2,1)S(1)}, u32[]{:S(2)}, u32[]{:S(2)}) collective-permute-start(bf16[4,128,256]{2,1,0:T(8,128)(2,1)S(1)} %get-tuple-element.17), channel_id=1, source_target_pairs={{0,2},{1,3},{2,0},{3,1},{4,6},{5,7},{6,4},{7,5},{8,10},{9,11},{10,... | collective-permute-start | bytes 786440 | tf_op jit(solution)/shard_map/ppermute | solution.py:226
  61.4 0.9 collective-permute-start.8
  62.3 6.3 %all-to-all-start.1 = ((bf16[16,128,256]{2,1,0:T(8,128)(2,1)}), bf16[16,128,256]{2,1,0:T(8,128)(2,1)S(1)}, u32[]{:S(2)}, u32[]{:S(2)}) async-start(bf16[16,128,256]{2,1,0:T(8,128)(2,1)} %bitcast.2), calls=%async_computation.1 | async-start | bytes 2097152 | tf_op jit(solution)/shard_map/all_to_all | solution.py:245
  68.6 6.8 %collective-permute-done.7.refs_2_ = bf16[4,128,256]{2,1,0:T(8,128)(2,1)S(1)} collective-permute-done((bf16[4,128,256]{2,1,0:T(8,128)(2,1)S(1)}, bf16[4,128,256]{2,1,0:T(8,128)(2,1)S(1)}, u32[]{:S(2)}, u32[]{:S(2)}) %collective-permute-start.7) | collective-permute-done | bytes 262176 | tf_op jit(solution)/shard_map/ppermute | solution.py:226
  75.4 0.7 shard_map.88
  76.1 0.8 collective-permute-start.9
  76.9 7.8 %collective-permute-start.10 = (bf16[128,256]{1,0:T(8,128)(2,1)S(1)}, bf16[128,256]{1,0:T(8,128)(2,1)S(1)}, u32[]{:S(2)}, u32[]{:S(2)}) collective-permute-start(bf16[128,256]{1,0:T(8,128)(2,1)S(1)} %get-tuple-element.21), channel_id=1, source_target_pairs={{0,8},{1,9},{2,10},{3,11},{4,12},{5,13},{6,14},{7,15},{8,0},{9,1},... | collective-permute-start | bytes 196616 | tf_op jit(solution)/shard_map/ppermute | solution.py:222
  84.7 9.6 %all-to-all-done.1 = bf16[16,128,256]{2,1,0:T(8,128)(2,1)S(1)} async-done(((bf16[16,128,256]{2,1,0:T(8,128)(2,1)}), bf16[16,128,256]{2,1,0:T(8,128)(2,1)S(1)}, u32[]{:S(2)}, u32[]{:S(2)}) %all-to-all-start.1) | async-done | bytes 1048608 | tf_op jit(solution)/shard_map/all_to_all | solution.py:245
  94.3 0.1 copy.11
  94.4 0.0 copy-start
  94.4 3.4 %collective-permute-done.10.refs_2_ = bf16[128,256]{1,0:T(8,128)(2,1)S(1)} collective-permute-done((bf16[128,256]{1,0:T(8,128)(2,1)S(1)}, bf16[128,256]{1,0:T(8,128)(2,1)S(1)}, u32[]{:S(2)}, u32[]{:S(2)}) %collective-permute-start.10) | collective-permute-done | bytes 65568 | tf_op jit(solution)/shard_map/ppermute | solution.py:222
  97.8 1.3 %shard_map.89 = (bf16[128,512]{1,0:T(8,128)(2,1)}, bf16[128,512]{1,0:T(8,128)(2,1)}) custom-call(s32[2]{0:T(128)S(1)} %pad_add_fusion.pos_ref, bf16[128,256]{1,0:T(8,128)(2,1)S(1)} %get-tuple-element.19.refs_0_, bf16[128,256]{1,0:T(8,128)(2,1)S(1)} %collective-permute-done.9.refs_1_, bf16[128,256]{1,0:T(8,128)(2,1)S(1)} %collective-permute-done.10.refs_2_, ...), custom_call_target="tpu_custom_call" | custom-call | bytes 4194304 | tf_op jit(solution)/shard_map/pallas_call | solution.py:203
  (26 shorter events, 0.1 us)
Async XLA Ops:
  0.6 9.2 %copy-start.1 = (bf16[128,4096]{1,0:T(8,128)(2,1)S(1)}, bf16[128,4096]{1,0:T(8,128)(2,1)}, u32[]{:S(2)}) copy-start(bf16[128,4096]{1,0:T(8,128)(2,1)} %o_ref.1) | copy-start | bytes 3145732
  1.7 15.2 %collective-permute-start.1 = (bf16[128,256]{1,0:T(8,128)(2,1)S(1)}, bf16[128,256]{1,0:T(8,128)(2,1)S(1)}, u32[]{:S(2)}, u32[]{:S(2)}) collective-permute-start(bf16[128,256]{1,0:T(8,128)(2,1)S(1)} %pad_maximum_fusion.2), channel_id=1, source_target_pairs={{0,8},{1,9},{2,10},{3,11},{4,12},{5,13},{6,14},{7,15},{8,0},{9,1},... | collective-permute-start | bytes 196616 | tf_op jit(solution)/shard_map/ppermute | solution.py:222
  5.8 11.1 %collective-permute-start = (bf16[128,256]{1,0:T(8,128)(2,1)S(1)}, bf16[128,256]{1,0:T(8,128)(2,1)S(1)}, u32[]{:S(2)}, u32[]{:S(2)}) collective-permute-start(bf16[128,256]{1,0:T(8,128)(2,1)S(1)} %pad_maximum_fusion.1), channel_id=1, source_target_pairs={{0,4},{1,5},{2,6},{3,7},{4,8},{5,9},{6,10},{7,11},{8,12},{9,13},{1... | collective-permute-start | bytes 196616 | tf_op jit(solution)/shard_map/ppermute | solution.py:222
  7.5 9.5 %collective-permute-start.2 = (bf16[128,256]{1,0:T(8,128)(2,1)S(1)}, bf16[128,256]{1,0:T(8,128)(2,1)S(1)}, u32[]{:S(2)}, u32[]{:S(2)}) collective-permute-start(bf16[128,256]{1,0:T(8,128)(2,1)S(1)} %pad_maximum_fusion.3), channel_id=1, source_target_pairs={{0,12},{1,13},{2,14},{3,15},{4,0},{5,1},{6,2},{7,3},{8,4},{9,5},{1... | collective-permute-start | bytes 196616 | tf_op jit(solution)/shard_map/ppermute | solution.py:222
  9.8 1.2 %copy-start.2 = (bf16[128,4096]{1,0:T(8,128)(2,1)S(1)}, bf16[128,4096]{1,0:T(8,128)(2,1)}, u32[]{:S(2)}) copy-start(bf16[128,4096]{1,0:T(8,128)(2,1)} %g_ref.1) | copy-start | bytes 3145732
  13.1 30.3 %all-to-all-start = ((bf16[16,264,128]{2,1,0:T(8,128)(2,1)}), bf16[16,264,128]{2,1,0:T(8,128)(2,1)S(1)}, u32[]{:S(2)}, u32[]{:S(2)}) async-start(bf16[16,264,128]{2,1,0:T(8,128)(2,1)} %shard_map.85), calls=%async_computation | async-start | bytes 2162688 | tf_op jit(solution)/shard_map/all_to_all | solution.py:241
  16.9 26.5 %copy-start.3 = (bf16[2048,256]{1,0:T(8,128)(2,1)S(1)}, bf16[2048,256]{1,0:T(8,128)(2,1)}, u32[]{:S(2)}) copy-start(bf16[2048,256]{1,0:T(8,128)(2,1)} %q_ref.1) | copy-start | bytes 3145732
  16.9 26.5 %copy-start.5 = (f32[2,2048]{1,0:T(2,128)S(1)}, f32[2,2048]{1,0:T(2,128)}, u32[]{:S(2)}) copy-start(f32[2,2048]{1,0:T(2,128)} %lse_ref.1) | copy-start | bytes 49156
  17.0 26.4 %copy-start.4 = (bf16[4,128,256]{2,1,0:T(8,128)(2,1)}, bf16[4,128,256]{2,1,0:T(8,128)(2,1)S(1)}, u32[]{:S(2)}) copy-start(bf16[4,128,256]{2,1,0:T(8,128)(2,1)S(1)} %shard_map.86.refs_0_) | copy-start | bytes 786436
  17.0 17.9 %collective-permute-start.5 = (bf16[4,128,256]{2,1,0:T(8,128)(2,1)S(1)}, bf16[4,128,256]{2,1,0:T(8,128)(2,1)S(1)}, u32[]{:S(2)}, u32[]{:S(2)}) collective-permute-start(bf16[4,128,256]{2,1,0:T(8,128)(2,1)S(1)} %shard_map.86.refs_0_), channel_id=1, source_target_pairs={{0,3},{1,0},{2,1},{3,2},{4,7},{5,4},{6,5},{7,6},{8,11},{9,8},{10,9... | collective-permute-start | bytes 786440 | tf_op jit(solution)/shard_map/ppermute | solution.py:226
  19.9 17.0 %collective-permute-start.4 = (bf16[4,128,256]{2,1,0:T(8,128)(2,1)S(1)}, bf16[4,128,256]{2,1,0:T(8,128)(2,1)S(1)}, u32[]{:S(2)}, u32[]{:S(2)}) collective-permute-start(bf16[4,128,256]{2,1,0:T(8,128)(2,1)S(1)} %shard_map.86.refs_0_), channel_id=1, source_target_pairs={{0,2},{1,3},{2,0},{3,1},{4,6},{5,7},{6,4},{7,5},{8,10},{9,11},{10,... | collective-permute-start | bytes 786440 | tf_op jit(solution)/shard_map/ppermute | solution.py:226
  20.5 22.2 %collective-permute-start.3 = (bf16[4,128,256]{2,1,0:T(8,128)(2,1)S(1)}, bf16[4,128,256]{2,1,0:T(8,128)(2,1)S(1)}, u32[]{:S(2)}, u32[]{:S(2)}) collective-permute-start(bf16[4,128,256]{2,1,0:T(8,128)(2,1)S(1)} %shard_map.86.refs_0_), channel_id=1, source_target_pairs={{0,1},{1,2},{2,3},{3,0},{4,5},{5,6},{6,7},{7,4},{8,9},{9,10},{10,1... | collective-permute-start | bytes 786440 | tf_op jit(solution)/shard_map/ppermute | solution.py:226
  35.0 7.7 %copy-start.6 = (bf16[4,128,256]{2,1,0:T(8,128)(2,1)}, bf16[4,128,256]{2,1,0:T(8,128)(2,1)S(1)}, u32[]{:S(2)}) copy-start(bf16[4,128,256]{2,1,0:T(8,128)(2,1)S(1)} %collective-permute-done.5.refs_3_) | copy-start | bytes 786436
  36.9 5.8 %copy-start.7 = (bf16[4,128,256]{2,1,0:T(8,128)(2,1)}, bf16[4,128,256]{2,1,0:T(8,128)(2,1)S(1)}, u32[]{:S(2)}) copy-start(bf16[4,128,256]{2,1,0:T(8,128)(2,1)S(1)} %collective-permute-done.4.refs_2_) | copy-start | bytes 786436
  42.7 0.7 copy-start.8
  59.3 9.3 %collective-permute-start.6 = (bf16[4,128,256]{2,1,0:T(8,128)(2,1)S(1)}, bf16[4,128,256]{2,1,0:T(8,128)(2,1)S(1)}, u32[]{:S(2)}, u32[]{:S(2)}) collective-permute-start(bf16[4,128,256]{2,1,0:T(8,128)(2,1)S(1)} %get-tuple-element.16), channel_id=1, source_target_pairs={{0,1},{1,2},{2,3},{3,0},{4,5},{5,6},{6,7},{7,4},{8,9},{9,10},{10,1... | collective-permute-start | bytes 786440 | tf_op jit(solution)/shard_map/ppermute | solution.py:226
  60.1 15.4 %collective-permute-start.7 = (bf16[4,128,256]{2,1,0:T(8,128)(2,1)S(1)}, bf16[4,128,256]{2,1,0:T(8,128)(2,1)S(1)}, u32[]{:S(2)}, u32[]{:S(2)}) collective-permute-start(bf16[4,128,256]{2,1,0:T(8,128)(2,1)S(1)} %get-tuple-element.17), channel_id=1, source_target_pairs={{0,2},{1,3},{2,0},{3,1},{4,6},{5,7},{6,4},{7,5},{8,10},{9,11},{10,... | collective-permute-start | bytes 786440 | tf_op jit(solution)/shard_map/ppermute | solution.py:226
  61.4 14.0 %collective-permute-start.8 = (bf16[4,128,256]{2,1,0:T(8,128)(2,1)S(1)}, bf16[4,128,256]{2,1,0:T(8,128)(2,1)S(1)}, u32[]{:S(2)}, u32[]{:S(2)}) collective-permute-start(bf16[4,128,256]{2,1,0:T(8,128)(2,1)S(1)} %get-tuple-element.18), channel_id=1, source_target_pairs={{0,3},{1,0},{2,1},{3,2},{4,7},{5,4},{6,5},{7,6},{8,11},{9,8},{10,9... | collective-permute-start | bytes 786440 | tf_op jit(solution)/shard_map/ppermute | solution.py:226
  62.3 32.0 %all-to-all-start.1 = ((bf16[16,128,256]{2,1,0:T(8,128)(2,1)}), bf16[16,128,256]{2,1,0:T(8,128)(2,1)S(1)}, u32[]{:S(2)}, u32[]{:S(2)}) async-start(bf16[16,128,256]{2,1,0:T(8,128)(2,1)} %bitcast.2), calls=%async_computation.1 | async-start | bytes 2097152 | tf_op jit(solution)/shard_map/all_to_all | solution.py:245
  76.1 18.3 %collective-permute-start.9 = (bf16[128,256]{1,0:T(8,128)(2,1)S(1)}, bf16[128,256]{1,0:T(8,128)(2,1)S(1)}, u32[]{:S(2)}, u32[]{:S(2)}) collective-permute-start(bf16[128,256]{1,0:T(8,128)(2,1)S(1)} %get-tuple-element.20), channel_id=1, source_target_pairs={{0,4},{1,5},{2,6},{3,7},{4,8},{5,9},{6,10},{7,11},{8,12},{9,13},{1... | collective-permute-start | bytes 196616 | tf_op jit(solution)/shard_map/ppermute | solution.py:222
  76.9 20.9 %collective-permute-start.10 = (bf16[128,256]{1,0:T(8,128)(2,1)S(1)}, bf16[128,256]{1,0:T(8,128)(2,1)S(1)}, u32[]{:S(2)}, u32[]{:S(2)}) collective-permute-start(bf16[128,256]{1,0:T(8,128)(2,1)S(1)} %get-tuple-element.21), channel_id=1, source_target_pairs={{0,8},{1,9},{2,10},{3,11},{4,12},{5,13},{6,14},{7,15},{8,0},{9,1},... | collective-permute-start | bytes 196616 | tf_op jit(solution)/shard_map/ppermute | solution.py:222
  84.7 13.1 %collective-permute-start.11 = (bf16[128,256]{1,0:T(8,128)(2,1)S(1)}, bf16[128,256]{1,0:T(8,128)(2,1)S(1)}, u32[]{:S(2)}, u32[]{:S(2)}) collective-permute-start(bf16[128,256]{1,0:T(8,128)(2,1)S(1)} %get-tuple-element.22), channel_id=1, source_target_pairs={{0,12},{1,13},{2,14},{3,15},{4,0},{5,1},{6,2},{7,3},{8,4},{9,5},{1... | collective-permute-start | bytes 196616 | tf_op jit(solution)/shard_map/ppermute | solution.py:222
  94.4 4.7 %copy-start = (bf16[16,16,8,256]{3,2,0,1:T(8,128)(2,1)}, bf16[16,16,8,256]{3,2,0,1:T(8,128)(2,1)S(1)}, u32[]{:S(2)}) copy-start(bf16[16,16,8,256]{3,2,0,1:T(8,128)(2,1)S(1)} %copy.11) | copy-start | bytes 3145732

commit v6 on v5

--- a/solution.py
+++ b/solution.py
@@ -77,11 +77,14 @@
 
     def body(pos_ref, q_ref, g_ref, lse_ref, *refs):
         ins, dq_ref, slots = refs[:copies], refs[copies], refs[copies + 1 : 2 * copies + 1]
-        kv_ref, kt_ref, l_ref, d_ref, acc_ref, dkv_ref, sems = refs[2 * copies + 1 :]
+        kv_ref, l_ref, d_ref, acc_ref, dkv_ref, sems = refs[2 * copies + 1 :]
         plane, place = pos_ref[0], pos_ref[1]
         coming = []
         for s in range(copies):
-            source = lax.rem(place - s + copies, copies)
+            if copies & (copies - 1):
+                source = lax.rem(place - s + copies, copies)
+            else:
+                source = place ^ s
             for r in range(planes):
                 owner = lax.rem(plane - r + planes, planes) * copies + source
                 start = pl.multiple_of(owner * rows, rows)
@@ -96,10 +99,9 @@
         for copy in coming:
             copy.wait()
         for k0 in range(0, total, block):
-            kt_ref[:, k0 : k0 + block] = kv_ref[k0 : k0 + block, :DH].T
-        for k0 in range(0, total, block):
             k1 = k0 + block
             kb, vb = kv_ref[k0:k1, :DH], kv_ref[k0:k1, DH:]
+            kt = kb.T
             dk = dv = None
             for q0 in range(k0, total, block):
                 q1 = q0 + block
@@ -120,7 +122,7 @@
                     ds = ds.astype(jnp.bfloat16)
                     t = dot(ds, qb, NN)
                     dk = t if dk is None else dk + t
-                    t = dot(kt_ref[:, k0:k1], ds, NN)
+                    t = dot(kt, ds, NN)
                     if k0 == 0:
                         acc_ref[c, q0:q1] = t
                     else:
@@ -146,7 +148,6 @@
         exps=heads * total * total // 2,
         scratch_shapes=[
             pltpu.VMEM((total, 2 * DH), jnp.bfloat16),
-            pltpu.VMEM((DH, total), jnp.bfloat16),
             pltpu.VMEM(lse.shape, jnp.float32),
             pltpu.VMEM((g.shape[1] - heads * rows, total), jnp.float32),
             pltpu.VMEM((width, total), jnp.float32),
@@ -221,6 +222,11 @@
         turn = [(j, (j + r * copies) % seq_count) for j in range(seq_count)]
         return lax.ppermute(x, "seq", turn)
 
+    def swap(x, s):
+        if copies & (copies - 1):
+            return inside(x, s)
+        return lax.ppermute(x, "seq", [(j, j ^ s) for j in range(seq_count)])
+
     def inside(x, s):
         turn = [(j, j // copies * copies + (j + s) % copies) for j in range(seq_count)]
         return lax.ppermute(x, "seq", turn)
@@ -232,12 +238,12 @@
         return lax.dynamic_index_in_dim(x, n % x.shape[0], 0, keepdims=False)
 
     got = []
-    for r in range(kv_heads):
+    for r in (0, *range(kv_heads - 1, 0, -1)):
         both = jnp.concatenate([columns(key_seq, plane + r), columns(value_seq, plane + r)], axis=1)
         got.append(across(both, r) if r else both)
-    mine = stack(got)
+    mine = stack(got[:1] + got[:0:-1])
     send = pack(attn_out, grad_out, seq_count, heads_here, pad)
-    pieces = [mine] + [inside(mine, s) for s in range(1, copies)]
+    pieces = [mine] + [swap(mine, s) for s in range(1, copies)]
     grad = lax.all_to_all(send, "seq", split_axis=0, concat_axis=0, tiled=True)
     pieces = [pltpu.with_memory_space_constraint(x, pltpu.HBM) for x in pieces]
     query_local, *parts = attend(pos, query, grad, lse, pieces, min(512, total))

time: 99.5 us -> 99.5 us (level)
  starting transfers between devices: 33.8 us -> 32.3 us
  waiting for transfers between devices: 41.4 us -> 42.6 us
    ppermute x0 -> x3, waiting for transfers between devices: none -> 21.2 us  [swap(): return lax.ppermute(x, 'seq', [(j, j ^ s) for j in range(seq_count)])]
    ppermute x6 -> x3, waiting for transfers between devices: 28.4 us -> 8.45 us  [inside(): return lax.ppermute(x, 'seq', turn)]
    ppermute x0 -> x3, starting transfers between devices: none -> 3.55 us  [swap(): return lax.ppermute(x, 'seq', [(j, j ^ s) for j in range(seq_count)])]
    ppermute x6 -> x3, starting transfers between devices: 6.98 us -> 4.85 us  [inside(): return lax.ppermute(x, 'seq', turn)]
    ppermute x6, starting transfers between devices: 16.6 us -> 15 us  [across(): return lax.ppermute(x, 'seq', turn)]
    all_to_all x1, starting transfers between devices: 6.34 us -> 5.05 us  [per_device(): lax.all_to_all(query_local, 'seq', split_axis=0, concat_axis=0, tiled=True)]
  transfers between devices with their start and end apart: 14 -> 14, of which waited for: 6 -> 7; matrix products, arithmetic and copies ran while one was open for 0% -> 0% of each run, Pallas kernels for 3% -> 3%
where the time goes in v6:
time: 99.5 us; the launch traced here: 99.1 us
  waiting for transfers between devices  42.6 us (43%)
  starting transfers between devices  32.3 us (32%)
  Pallas kernels  19.9 us (20%)
  local copies, waits for them, and re-layouts  3.28 us (3%)
    ppermute x3, waiting for transfers between devices, swap(): return lax.ppermute(x, 'seq', [(j, j ^ s) for j in range(seq_count)])  21.2 us
    pallas_call x1, Pallas kernels, attend(): call(body, (jax.ShapeDtypeStruct((total, width), jnp.bfloat16),) + (part,...  15.9 us
    ppermute x6, starting transfers between devices, across(): return lax.ppermute(x, 'seq', turn)  15 us
    all_to_all x1, waiting for transfers between devices, per_device(): lax.all_to_all(query_local, 'seq', split_axis=0, concat_axis=0, tiled=True)  9.6 us
    ppermute x3, waiting for transfers between devices, inside(): return lax.ppermute(x, 'seq', turn)  8.45 us
    all_to_all x1, starting transfers between devices, per_device(): lax.all_to_all(query_local, 'seq', split_axis=0, concat_axis=0, tiled=True)  5.05 us
    ppermute x3, starting transfers between devices, inside(): return lax.ppermute(x, 'seq', turn)  4.85 us
    all_to_all x1, starting transfers between devices, per_device(): grad = lax.all_to_all(send, 'seq', split_axis=0, concat_axis=0, tiled=True)  3.83 us
  transfers between devices with their start and end apart: 14, of which 7 were waited for; matrix products, arithmetic and copies ran while one was open for 0% of the time, Pallas kernels for 3%

profile of v6, /device:TPU:0, one launch (start us, length us, event | category | flops | bytes accessed | tf_op | source)
XLA Modules:
  0.0 99.1 jit_solution(206234892544711597)
XLA Ops:
  0.7 1.0 constant_dynamic-slice_fusion
  1.7 4.1 %collective-permute-start.1 = (bf16[128,256]{1,0:T(8,128)(2,1)S(1)}, bf16[128,256]{1,0:T(8,128)(2,1)S(1)}, u32[]{:S(2)}, u32[]{:S(2)}) collective-permute-start(bf16[128,256]{1,0:T(8,128)(2,1)S(1)} %pad_maximum_fusion.2), channel_id=1, source_target_pairs={{0,8},{1,9},{2,10},{3,11},{4,12},{5,13},{6,14},{7,15},{8,0},{9,1},... | collective-permute-start | bytes 196616 | tf_op jit(solution)/shard_map/ppermute | solution.py:223
  5.8 1.6 %collective-permute-start = (bf16[128,256]{1,0:T(8,128)(2,1)S(1)}, bf16[128,256]{1,0:T(8,128)(2,1)S(1)}, u32[]{:S(2)}, u32[]{:S(2)}) collective-permute-start(bf16[128,256]{1,0:T(8,128)(2,1)S(1)} %pad_maximum_fusion.1), channel_id=1, source_target_pairs={{0,4},{1,5},{2,6},{3,7},{4,8},{5,9},{6,10},{7,11},{8,12},{9,13},{1... | collective-permute-start | bytes 196616 | tf_op jit(solution)/shard_map/ppermute | solution.py:223
  7.5 2.3 %collective-permute-start.2 = (bf16[128,256]{1,0:T(8,128)(2,1)S(1)}, bf16[128,256]{1,0:T(8,128)(2,1)S(1)}, u32[]{:S(2)}, u32[]{:S(2)}) collective-permute-start(bf16[128,256]{1,0:T(8,128)(2,1)S(1)} %pad_maximum_fusion.3), channel_id=1, source_target_pairs={{0,12},{1,13},{2,14},{3,15},{4,0},{5,1},{6,2},{7,3},{8,4},{9,5},{1... | collective-permute-start | bytes 196616 | tf_op jit(solution)/shard_map/ppermute | solution.py:223
  9.8 1.2 %copy-done.2 = bf16[128,4096]{1,0:T(8,128)(2,1)S(1)} copy-done((bf16[128,4096]{1,0:T(8,128)(2,1)S(1)}, bf16[128,4096]{1,0:T(8,128)(2,1)}, u32[]{:S(2)}) %copy-start.2) | copy-done | bytes 1048600
  11.0 2.1 %shard_map.85 = bf16[16,264,128]{2,1,0:T(8,128)(2,1)} custom-call(bf16[128,4096]{1,0:T(8,128)(2,1)S(1)} %copy-done.1, bf16[128,4096]{1,0:T(8,128)(2,1)S(1)} %copy-done.2), custom_call_target="tpu_custom_call" | custom-call | bytes 4194304 | tf_op jit(solution)/shard_map/pallas_call | solution.py:63
  13.1 3.8 %all-to-all-start = ((bf16[16,264,128]{2,1,0:T(8,128)(2,1)}), bf16[16,264,128]{2,1,0:T(8,128)(2,1)S(1)}, u32[]{:S(2)}, u32[]{:S(2)}) async-start(bf16[16,264,128]{2,1,0:T(8,128)(2,1)} %shard_map.85), calls=%async_computation | async-start | bytes 2162688 | tf_op jit(solution)/shard_map/all_to_all | solution.py:247
  16.9 0.0 copy-start.3
  16.9 0.0 copy-start.5
  17.0 2.9 %collective-permute-start.5 = (bf16[4,128,256]{2,1,0:T(8,128)(2,1)S(1)}, bf16[4,128,256]{2,1,0:T(8,128)(2,1)S(1)}, u32[]{:S(2)}, u32[]{:S(2)}) collective-permute-start(bf16[4,128,256]{2,1,0:T(8,128)(2,1)S(1)} %shard_map.86.refs_0_), channel_id=1, source_target_pairs={{0,3},{1,2},{2,1},{3,0},{4,7},{5,6},{6,5},{7,4},{8,11},{9,10},{10,... | collective-permute-start | bytes 786440 | tf_op jit(solution)/shard_map/ppermute | solution.py:228
  19.9 0.6 collective-permute-start.4
  20.5 0.1 collective-permute-start.3
  20.6 0.1 pad_add_fusion.pos_ref
  20.7 16.9 %collective-permute-done.5.refs_3_ = bf16[4,128,256]{2,1,0:T(8,128)(2,1)S(1)} collective-permute-done((bf16[4,128,256]{2,1,0:T(8,128)(2,1)S(1)}, bf16[4,128,256]{2,1,0:T(8,128)(2,1)S(1)}, u32[]{:S(2)}, u32[]{:S(2)}) %collective-permute-start.5) | collective-permute-done | bytes 262176 | tf_op jit(solution)/shard_map/ppermute | solution.py:228
  37.5 3.8 %collective-permute-done.4.refs_2_ = bf16[4,128,256]{2,1,0:T(8,128)(2,1)S(1)} collective-permute-done((bf16[4,128,256]{2,1,0:T(8,128)(2,1)S(1)}, bf16[4,128,256]{2,1,0:T(8,128)(2,1)S(1)}, u32[]{:S(2)}, u32[]{:S(2)}) %collective-permute-start.4) | collective-permute-done | bytes 262176 | tf_op jit(solution)/shard_map/ppermute | solution.py:228
  41.4 0.5 collective-permute-done.3.refs_1_
  41.9 0.2 copy-done.7
  42.1 0.7 copy-done.8
  42.8 15.9 %shard_map.87 = (bf16[2048,256]{1,0:T(8,128)(2,1)}, bf16[4,128,256]{2,1,0:T(8,128)(2,1)S(1)}, bf16[4,128,256]{2,1,0:T(8,128)(2,1)S(1)}, bf16[4,128,256]{2,1,0:T(8,128)(2,1)S(1)}, bf16[4,128,256]{2,1,0:T(8,128)(2,1)S(1)}) custom-call(s32[2]{0:T(128)S(1)} %pad_add_fusion.pos_ref, bf16[2048,256]{1,0:T(8,128)(2,1)S(1)} %copy-done.3, ...), custom_call_target="tpu_custom_call" | custom-call | flops 5368709120 | bytes 4194304 | tf_op jit(solution)/shard_map/pallas_call | solution.py:142
  58.7 1.4 %collective-permute-start.6 = (bf16[4,128,256]{2,1,0:T(8,128)(2,1)S(1)}, bf16[4,128,256]{2,1,0:T(8,128)(2,1)S(1)}, u32[]{:S(2)}, u32[]{:S(2)}) collective-permute-start(bf16[4,128,256]{2,1,0:T(8,128)(2,1)S(1)} %get-tuple-element.16), channel_id=1, source_target_pairs={{0,1},{1,2},{2,3},{3,0},{4,5},{5,6},{6,7},{7,4},{8,9},{9,10},{10,1... | collective-permute-start | bytes 786440 | tf_op jit(solution)/shard_map/ppermute | solution.py:232
  60.1 1.3 %collective-permute-start.7 = (bf16[4,128,256]{2,1,0:T(8,128)(2,1)S(1)}, bf16[4,128,256]{2,1,0:T(8,128)(2,1)S(1)}, u32[]{:S(2)}, u32[]{:S(2)}) collective-permute-start(bf16[4,128,256]{2,1,0:T(8,128)(2,1)S(1)} %get-tuple-element.17), channel_id=1, source_target_pairs={{0,2},{1,3},{2,0},{3,1},{4,6},{5,7},{6,4},{7,5},{8,10},{9,11},{10,... | collective-permute-start | bytes 786440 | tf_op jit(solution)/shard_map/ppermute | solution.py:232
  61.4 2.1 %collective-permute-start.8 = (bf16[4,128,256]{2,1,0:T(8,128)(2,1)S(1)}, bf16[4,128,256]{2,1,0:T(8,128)(2,1)S(1)}, u32[]{:S(2)}, u32[]{:S(2)}) collective-permute-start(bf16[4,128,256]{2,1,0:T(8,128)(2,1)S(1)} %get-tuple-element.18), channel_id=1, source_target_pairs={{0,3},{1,0},{2,1},{3,2},{4,7},{5,4},{6,5},{7,6},{8,11},{9,8},{10,9... | collective-permute-start | bytes 786440 | tf_op jit(solution)/shard_map/ppermute | solution.py:232
  63.5 5.0 %all-to-all-start.1 = ((bf16[16,128,256]{2,1,0:T(8,128)(2,1)}), bf16[16,128,256]{2,1,0:T(8,128)(2,1)S(1)}, u32[]{:S(2)}, u32[]{:S(2)}) async-start(bf16[16,128,256]{2,1,0:T(8,128)(2,1)} %bitcast.2), calls=%async_computation.1 | async-start | bytes 2097152 | tf_op jit(solution)/shard_map/all_to_all | solution.py:251
  68.6 0.3 collective-permute-done.6.refs_1_
  68.9 8.1 %collective-permute-done.7.refs_2_ = bf16[4,128,256]{2,1,0:T(8,128)(2,1)S(1)} collective-permute-done((bf16[4,128,256]{2,1,0:T(8,128)(2,1)S(1)}, bf16[4,128,256]{2,1,0:T(8,128)(2,1)S(1)}, u32[]{:S(2)}, u32[]{:S(2)}) %collective-permute-start.7) | collective-permute-done | bytes 262176 | tf_op jit(solution)/shard_map/ppermute | solution.py:232
  77.1 0.7 shard_map.88
  77.7 0.1 collective-permute-start.9
  77.8 6.9 %collective-permute-start.10 = (bf16[128,256]{1,0:T(8,128)(2,1)S(1)}, bf16[128,256]{1,0:T(8,128)(2,1)S(1)}, u32[]{:S(2)}, u32[]{:S(2)}) collective-permute-start(bf16[128,256]{1,0:T(8,128)(2,1)S(1)} %get-tuple-element.21), channel_id=1, source_target_pairs={{0,8},{1,9},{2,10},{3,11},{4,12},{5,13},{6,14},{7,15},{8,0},{9,1},... | collective-permute-start | bytes 196616 | tf_op jit(solution)/shard_map/ppermute | solution.py:223
  84.7 9.6 %all-to-all-done.1 = bf16[16,128,256]{2,1,0:T(8,128)(2,1)S(1)} async-done(((bf16[16,128,256]{2,1,0:T(8,128)(2,1)}), bf16[16,128,256]{2,1,0:T(8,128)(2,1)S(1)}, u32[]{:S(2)}, u32[]{:S(2)}) %all-to-all-start.1) | async-done | bytes 1048608 | tf_op jit(solution)/shard_map/all_to_all | solution.py:251
  94.3 0.1 copy.11
  94.4 3.4 %collective-permute-done.10.refs_2_ = bf16[128,256]{1,0:T(8,128)(2,1)S(1)} collective-permute-done((bf16[128,256]{1,0:T(8,128)(2,1)S(1)}, bf16[128,256]{1,0:T(8,128)(2,1)S(1)}, u32[]{:S(2)}, u32[]{:S(2)}) %collective-permute-start.10) | collective-permute-done | bytes 65568 | tf_op jit(solution)/shard_map/ppermute | solution.py:223
  97.8 1.3 %shard_map.89 = (bf16[128,512]{1,0:T(8,128)(2,1)}, bf16[128,512]{1,0:T(8,128)(2,1)}) custom-call(s32[2]{0:T(128)S(1)} %pad_add_fusion.pos_ref, bf16[128,256]{1,0:T(8,128)(2,1)S(1)} %get-tuple-element.19.refs_0_, bf16[128,256]{1,0:T(8,128)(2,1)S(1)} %collective-permute-done.9.refs_1_, bf16[128,256]{1,0:T(8,128)(2,1)S(1)} %collective-permute-done.10.refs_2_, ...), custom_call_target="tpu_custom_call" | custom-call | bytes 4194304 | tf_op jit(solution)/shard_map/pallas_call | solution.py:204
  (26 shorter events, 0.1 us)
Async XLA Ops:
  0.6 9.2 %copy-start.1 = (bf16[128,4096]{1,0:T(8,128)(2,1)S(1)}, bf16[128,4096]{1,0:T(8,128)(2,1)}, u32[]{:S(2)}) copy-start(bf16[128,4096]{1,0:T(8,128)(2,1)} %o_ref.1) | copy-start | bytes 3145732
  1.7 15.2 %collective-permute-start.1 = (bf16[128,256]{1,0:T(8,128)(2,1)S(1)}, bf16[128,256]{1,0:T(8,128)(2,1)S(1)}, u32[]{:S(2)}, u32[]{:S(2)}) collective-permute-start(bf16[128,256]{1,0:T(8,128)(2,1)S(1)} %pad_maximum_fusion.2), channel_id=1, source_target_pairs={{0,8},{1,9},{2,10},{3,11},{4,12},{5,13},{6,14},{7,15},{8,0},{9,1},... | collective-permute-start | bytes 196616 | tf_op jit(solution)/shard_map/ppermute | solution.py:223
  5.8 11.1 %collective-permute-start = (bf16[128,256]{1,0:T(8,128)(2,1)S(1)}, bf16[128,256]{1,0:T(8,128)(2,1)S(1)}, u32[]{:S(2)}, u32[]{:S(2)}) collective-permute-start(bf16[128,256]{1,0:T(8,128)(2,1)S(1)} %pad_maximum_fusion.1), channel_id=1, source_target_pairs={{0,4},{1,5},{2,6},{3,7},{4,8},{5,9},{6,10},{7,11},{8,12},{9,13},{1... | collective-permute-start | bytes 196616 | tf_op jit(solution)/shard_map/ppermute | solution.py:223
  7.5 9.5 %collective-permute-start.2 = (bf16[128,256]{1,0:T(8,128)(2,1)S(1)}, bf16[128,256]{1,0:T(8,128)(2,1)S(1)}, u32[]{:S(2)}, u32[]{:S(2)}) collective-permute-start(bf16[128,256]{1,0:T(8,128)(2,1)S(1)} %pad_maximum_fusion.3), channel_id=1, source_target_pairs={{0,12},{1,13},{2,14},{3,15},{4,0},{5,1},{6,2},{7,3},{8,4},{9,5},{1... | collective-permute-start | bytes 196616 | tf_op jit(solution)/shard_map/ppermute | solution.py:223
  9.8 1.2 %copy-start.2 = (bf16[128,4096]{1,0:T(8,128)(2,1)S(1)}, bf16[128,4096]{1,0:T(8,128)(2,1)}, u32[]{:S(2)}) copy-start(bf16[128,4096]{1,0:T(8,128)(2,1)} %g_ref.1) | copy-start | bytes 3145732
  13.1 29.7 %all-to-all-start = ((bf16[16,264,128]{2,1,0:T(8,128)(2,1)}), bf16[16,264,128]{2,1,0:T(8,128)(2,1)S(1)}, u32[]{:S(2)}, u32[]{:S(2)}) async-start(bf16[16,264,128]{2,1,0:T(8,128)(2,1)} %shard_map.85), calls=%async_computation | async-start | bytes 2162688 | tf_op jit(solution)/shard_map/all_to_all | solution.py:247
  16.9 25.9 %copy-start.3 = (bf16[2048,256]{1,0:T(8,128)(2,1)S(1)}, bf16[2048,256]{1,0:T(8,128)(2,1)}, u32[]{:S(2)}) copy-start(bf16[2048,256]{1,0:T(8,128)(2,1)} %q_ref.1) | copy-start | bytes 3145732
  16.9 25.9 %copy-start.5 = (f32[2,2048]{1,0:T(2,128)S(1)}, f32[2,2048]{1,0:T(2,128)}, u32[]{:S(2)}) copy-start(f32[2,2048]{1,0:T(2,128)} %lse_ref.1) | copy-start | bytes 49156
  17.0 25.8 %copy-start.4 = (bf16[4,128,256]{2,1,0:T(8,128)(2,1)}, bf16[4,128,256]{2,1,0:T(8,128)(2,1)S(1)}, u32[]{:S(2)}) copy-start(bf16[4,128,256]{2,1,0:T(8,128)(2,1)S(1)} %shard_map.86.refs_0_) | copy-start | bytes 786436
  17.0 20.5 %collective-permute-start.5 = (bf16[4,128,256]{2,1,0:T(8,128)(2,1)S(1)}, bf16[4,128,256]{2,1,0:T(8,128)(2,1)S(1)}, u32[]{:S(2)}, u32[]{:S(2)}) collective-permute-start(bf16[4,128,256]{2,1,0:T(8,128)(2,1)S(1)} %shard_map.86.refs_0_), channel_id=1, source_target_pairs={{0,3},{1,2},{2,1},{3,0},{4,7},{5,6},{6,5},{7,4},{8,11},{9,10},{10,... | collective-permute-start | bytes 786440 | tf_op jit(solution)/shard_map/ppermute | solution.py:228
  19.9 21.5 %collective-permute-start.4 = (bf16[4,128,256]{2,1,0:T(8,128)(2,1)S(1)}, bf16[4,128,256]{2,1,0:T(8,128)(2,1)S(1)}, u32[]{:S(2)}, u32[]{:S(2)}) collective-permute-start(bf16[4,128,256]{2,1,0:T(8,128)(2,1)S(1)} %shard_map.86.refs_0_), channel_id=1, source_target_pairs={{0,2},{1,3},{2,0},{3,1},{4,6},{5,7},{6,4},{7,5},{8,10},{9,11},{10,... | collective-permute-start | bytes 786440 | tf_op jit(solution)/shard_map/ppermute | solution.py:228
  20.5 21.4 %collective-permute-start.3 = (bf16[4,128,256]{2,1,0:T(8,128)(2,1)S(1)}, bf16[4,128,256]{2,1,0:T(8,128)(2,1)S(1)}, u32[]{:S(2)}, u32[]{:S(2)}) collective-permute-start(bf16[4,128,256]{2,1,0:T(8,128)(2,1)S(1)} %shard_map.86.refs_0_), channel_id=1, source_target_pairs={{0,1},{1,0},{2,3},{3,2},{4,5},{5,4},{6,7},{7,6},{8,9},{9,8},{10,11... | collective-permute-start | bytes 786440 | tf_op jit(solution)/shard_map/ppermute | solution.py:228
  37.5 4.3 %copy-start.6 = (bf16[4,128,256]{2,1,0:T(8,128)(2,1)}, bf16[4,128,256]{2,1,0:T(8,128)(2,1)S(1)}, u32[]{:S(2)}) copy-start(bf16[4,128,256]{2,1,0:T(8,128)(2,1)S(1)} %collective-permute-done.5.refs_3_) | copy-start | bytes 786436
  41.4 0.7 copy-start.7
  42.1 0.7 copy-start.8
  58.7 10.2 %collective-permute-start.6 = (bf16[4,128,256]{2,1,0:T(8,128)(2,1)S(1)}, bf16[4,128,256]{2,1,0:T(8,128)(2,1)S(1)}, u32[]{:S(2)}, u32[]{:S(2)}) collective-permute-start(bf16[4,128,256]{2,1,0:T(8,128)(2,1)S(1)} %get-tuple-element.16), channel_id=1, source_target_pairs={{0,1},{1,2},{2,3},{3,0},{4,5},{5,6},{6,7},{7,4},{8,9},{9,10},{10,1... | collective-permute-start | bytes 786440 | tf_op jit(solution)/shard_map/ppermute | solution.py:232
  60.1 17.0 %collective-permute-start.7 = (bf16[4,128,256]{2,1,0:T(8,128)(2,1)S(1)}, bf16[4,128,256]{2,1,0:T(8,128)(2,1)S(1)}, u32[]{:S(2)}, u32[]{:S(2)}) collective-permute-start(bf16[4,128,256]{2,1,0:T(8,128)(2,1)S(1)} %get-tuple-element.17), channel_id=1, source_target_pairs={{0,2},{1,3},{2,0},{3,1},{4,6},{5,7},{6,4},{7,5},{8,10},{9,11},{10,... | collective-permute-start | bytes 786440 | tf_op jit(solution)/shard_map/ppermute | solution.py:232
  61.4 15.6 %collective-permute-start.8 = (bf16[4,128,256]{2,1,0:T(8,128)(2,1)S(1)}, bf16[4,128,256]{2,1,0:T(8,128)(2,1)S(1)}, u32[]{:S(2)}, u32[]{:S(2)}) collective-permute-start(bf16[4,128,256]{2,1,0:T(8,128)(2,1)S(1)} %get-tuple-element.18), channel_id=1, source_target_pairs={{0,3},{1,0},{2,1},{3,2},{4,7},{5,4},{6,5},{7,6},{8,11},{9,8},{10,9... | collective-permute-start | bytes 786440 | tf_op jit(solution)/shard_map/ppermute | solution.py:232
  63.5 30.8 %all-to-all-start.1 = ((bf16[16,128,256]{2,1,0:T(8,128)(2,1)}), bf16[16,128,256]{2,1,0:T(8,128)(2,1)S(1)}, u32[]{:S(2)}, u32[]{:S(2)}) async-start(bf16[16,128,256]{2,1,0:T(8,128)(2,1)} %bitcast.2), calls=%async_computation.1 | async-start | bytes 2097152 | tf_op jit(solution)/shard_map/all_to_all | solution.py:251
  77.7 16.7 %collective-permute-start.9 = (bf16[128,256]{1,0:T(8,128)(2,1)S(1)}, bf16[128,256]{1,0:T(8,128)(2,1)S(1)}, u32[]{:S(2)}, u32[]{:S(2)}) collective-permute-start(bf16[128,256]{1,0:T(8,128)(2,1)S(1)} %get-tuple-element.20), channel_id=1, source_target_pairs={{0,4},{1,5},{2,6},{3,7},{4,8},{5,9},{6,10},{7,11},{8,12},{9,13},{1... | collective-permute-start | bytes 196616 | tf_op jit(solution)/shard_map/ppermute | solution.py:223
  77.8 20.0 %collective-permute-start.10 = (bf16[128,256]{1,0:T(8,128)(2,1)S(1)}, bf16[128,256]{1,0:T(8,128)(2,1)S(1)}, u32[]{:S(2)}, u32[]{:S(2)}) collective-permute-start(bf16[128,256]{1,0:T(8,128)(2,1)S(1)} %get-tuple-element.21), channel_id=1, source_target_pairs={{0,8},{1,9},{2,10},{3,11},{4,12},{5,13},{6,14},{7,15},{8,0},{9,1},... | collective-permute-start | bytes 196616 | tf_op jit(solution)/shard_map/ppermute | solution.py:223
  84.7 13.1 %collective-permute-start.11 = (bf16[128,256]{1,0:T(8,128)(2,1)S(1)}, bf16[128,256]{1,0:T(8,128)(2,1)S(1)}, u32[]{:S(2)}, u32[]{:S(2)}) collective-permute-start(bf16[128,256]{1,0:T(8,128)(2,1)S(1)} %get-tuple-element.22), channel_id=1, source_target_pairs={{0,12},{1,13},{2,14},{3,15},{4,0},{5,1},{6,2},{7,3},{8,4},{9,5},{1... | collective-permute-start | bytes 196616 | tf_op jit(solution)/shard_map/ppermute | solution.py:223
  94.4 4.7 %copy-start = (bf16[16,16,8,256]{3,2,0,1:T(8,128)(2,1)}, bf16[16,16,8,256]{3,2,0,1:T(8,128)(2,1)S(1)}, u32[]{:S(2)}) copy-start(bf16[16,16,8,256]{3,2,0,1:T(8,128)(2,1)S(1)} %copy.11) | copy-start | bytes 3145732

commit v7 on v5

--- a/solution.py
+++ b/solution.py
@@ -13,7 +13,7 @@
 VMEM = pl.BlockSpec(memory_space=pltpu.VMEM)
 ANY = pl.BlockSpec(memory_space=pl.ANY)
 SMEM = pl.BlockSpec(memory_space=pltpu.SMEM)
-LIMIT = 36 << 20
+LIMIT = 44 << 20
 
 
 def dot(a, b, dims):
@@ -77,7 +77,7 @@
 
     def body(pos_ref, q_ref, g_ref, lse_ref, *refs):
         ins, dq_ref, slots = refs[:copies], refs[copies], refs[copies + 1 : 2 * copies + 1]
-        kv_ref, kt_ref, l_ref, d_ref, acc_ref, dkv_ref, sems = refs[2 * copies + 1 :]
+        kv_ref, l_ref, d_ref, acc_ref, dkv_ref, sems = refs[2 * copies + 1 :]
         plane, place = pos_ref[0], pos_ref[1]
         coming = []
         for s in range(copies):
@@ -96,10 +96,9 @@
         for copy in coming:
             copy.wait()
         for k0 in range(0, total, block):
-            kt_ref[:, k0 : k0 + block] = kv_ref[k0 : k0 + block, :DH].T
-        for k0 in range(0, total, block):
             k1 = k0 + block
             kb, vb = kv_ref[k0:k1, :DH], kv_ref[k0:k1, DH:]
+            kt = kb.T
             dk = dv = None
             for q0 in range(k0, total, block):
                 q1 = q0 + block
@@ -120,7 +119,7 @@
                     ds = ds.astype(jnp.bfloat16)
                     t = dot(ds, qb, NN)
                     dk = t if dk is None else dk + t
-                    t = dot(kt_ref[:, k0:k1], ds, NN)
+                    t = dot(kt, ds, NN)
                     if k0 == 0:
                         acc_ref[c, q0:q1] = t
                     else:
@@ -146,7 +145,6 @@
         exps=heads * total * total // 2,
         scratch_shapes=[
             pltpu.VMEM((total, 2 * DH), jnp.bfloat16),
-            pltpu.VMEM((DH, total), jnp.bfloat16),
             pltpu.VMEM(lse.shape, jnp.float32),
             pltpu.VMEM((g.shape[1] - heads * rows, total), jnp.float32),
             pltpu.VMEM((width, total), jnp.float32),

time: 99.5 us -> 99.5 us (level)
  no operation moved by 1% of the time
where the time goes in v7:
time: 99.5 us; the launch traced here: 99.1 us
  waiting for transfers between devices  41.4 us (42%)
  starting transfers between devices  33.7 us (34%)
  Pallas kernels  19.9 us (20%)
  local copies, waits for them, and re-layouts  3.05 us (3%)
    ppermute x6, waiting for transfers between devices, inside(): return lax.ppermute(x, 'seq', turn)  28.4 us
    ppermute x6, starting transfers between devices, across(): return lax.ppermute(x, 'seq', turn)  16.6 us
    pallas_call x1, Pallas kernels, attend(): call(body, (jax.ShapeDtypeStruct((total, width), jnp.bfloat16),) + (part,...  15.9 us
    all_to_all x1, waiting for transfers between devices, per_device(): lax.all_to_all(query_local, 'seq', split_axis=0, concat_axis=0, tiled=True)  9.59 us
    ppermute x6, starting transfers between devices, inside(): return lax.ppermute(x, 'seq', turn)  6.98 us
    all_to_all x1, starting transfers between devices, per_device(): lax.all_to_all(query_local, 'seq', split_axis=0, concat_axis=0, tiled=True)  6.32 us
    all_to_all x1, starting transfers between devices, per_device(): grad = lax.all_to_all(send, 'seq', split_axis=0, concat_axis=0, tiled=True)  3.83 us
    ppermute x6, waiting for transfers between devices, across(): return lax.ppermute(x, 'seq', turn)  3.39 us
  transfers between devices with their start and end apart: 14, of which 6 were waited for; matrix products, arithmetic and copies ran while one was open for 0% of the time, Pallas kernels for 3%

profile of v7, /device:TPU:0, one launch (start us, length us, event | category | flops | bytes accessed | tf_op | source)
XLA Modules:
  0.0 99.1 jit_solution(13026978063088774370)
XLA Ops:
  0.7 1.0 constant_dynamic-slice_fusion
  1.7 4.1 %collective-permute-start.1 = (bf16[128,256]{1,0:T(8,128)(2,1)S(1)}, bf16[128,256]{1,0:T(8,128)(2,1)S(1)}, u32[]{:S(2)}, u32[]{:S(2)}) collective-permute-start(bf16[128,256]{1,0:T(8,128)(2,1)S(1)} %pad_maximum_fusion.2), channel_id=1, source_target_pairs={{0,8},{1,9},{2,10},{3,11},{4,12},{5,13},{6,14},{7,15},{8,0},{9,1},... | collective-permute-start | bytes 196616 | tf_op jit(solution)/shard_map/ppermute | solution.py:220
  5.8 1.6 %collective-permute-start = (bf16[128,256]{1,0:T(8,128)(2,1)S(1)}, bf16[128,256]{1,0:T(8,128)(2,1)S(1)}, u32[]{:S(2)}, u32[]{:S(2)}) collective-permute-start(bf16[128,256]{1,0:T(8,128)(2,1)S(1)} %pad_maximum_fusion.1), channel_id=1, source_target_pairs={{0,4},{1,5},{2,6},{3,7},{4,8},{5,9},{6,10},{7,11},{8,12},{9,13},{1... | collective-permute-start | bytes 196616 | tf_op jit(solution)/shard_map/ppermute | solution.py:220
  7.5 2.3 %collective-permute-start.2 = (bf16[128,256]{1,0:T(8,128)(2,1)S(1)}, bf16[128,256]{1,0:T(8,128)(2,1)S(1)}, u32[]{:S(2)}, u32[]{:S(2)}) collective-permute-start(bf16[128,256]{1,0:T(8,128)(2,1)S(1)} %pad_maximum_fusion.3), channel_id=1, source_target_pairs={{0,12},{1,13},{2,14},{3,15},{4,0},{5,1},{6,2},{7,3},{8,4},{9,5},{1... | collective-permute-start | bytes 196616 | tf_op jit(solution)/shard_map/ppermute | solution.py:220
  9.8 1.2 %copy-done.2 = bf16[128,4096]{1,0:T(8,128)(2,1)S(1)} copy-done((bf16[128,4096]{1,0:T(8,128)(2,1)S(1)}, bf16[128,4096]{1,0:T(8,128)(2,1)}, u32[]{:S(2)}) %copy-start.2) | copy-done | bytes 1048600
  11.0 2.1 %shard_map.85 = bf16[16,264,128]{2,1,0:T(8,128)(2,1)} custom-call(bf16[128,4096]{1,0:T(8,128)(2,1)S(1)} %copy-done.1, bf16[128,4096]{1,0:T(8,128)(2,1)S(1)} %copy-done.2), custom_call_target="tpu_custom_call" | custom-call | bytes 4194304 | tf_op jit(solution)/shard_map/pallas_call | solution.py:63
  13.1 3.8 %all-to-all-start = ((bf16[16,264,128]{2,1,0:T(8,128)(2,1)}), bf16[16,264,128]{2,1,0:T(8,128)(2,1)S(1)}, u32[]{:S(2)}, u32[]{:S(2)}) async-start(bf16[16,264,128]{2,1,0:T(8,128)(2,1)} %shard_map.85), calls=%async_computation | async-start | bytes 2162688 | tf_op jit(solution)/shard_map/all_to_all | solution.py:239
  16.9 0.0 copy-start.3
  16.9 0.0 copy-start.5
  17.0 0.0 collective-permute-done.2.refs_3_
  17.0 2.9 %collective-permute-start.5 = (bf16[4,128,256]{2,1,0:T(8,128)(2,1)S(1)}, bf16[4,128,256]{2,1,0:T(8,128)(2,1)S(1)}, u32[]{:S(2)}, u32[]{:S(2)}) collective-permute-start(bf16[4,128,256]{2,1,0:T(8,128)(2,1)S(1)} %shard_map.86.refs_0_), channel_id=1, source_target_pairs={{0,3},{1,0},{2,1},{3,2},{4,7},{5,4},{6,5},{7,6},{8,11},{9,8},{10,9... | collective-permute-start | bytes 786440 | tf_op jit(solution)/shard_map/ppermute | solution.py:224
  19.9 0.6 collective-permute-start.4
  20.5 0.6 collective-permute-start.3
  21.0 0.1 pad_add_fusion.pos_ref
  21.1 13.9 %collective-permute-done.5.refs_3_ = bf16[4,128,256]{2,1,0:T(8,128)(2,1)S(1)} collective-permute-done((bf16[4,128,256]{2,1,0:T(8,128)(2,1)S(1)}, bf16[4,128,256]{2,1,0:T(8,128)(2,1)S(1)}, u32[]{:S(2)}, u32[]{:S(2)}) %collective-permute-start.5) | collective-permute-done | bytes 262176 | tf_op jit(solution)/shard_map/ppermute | solution.py:224
  35.0 2.0 %collective-permute-done.4.refs_2_ = bf16[4,128,256]{2,1,0:T(8,128)(2,1)S(1)} collective-permute-done((bf16[4,128,256]{2,1,0:T(8,128)(2,1)S(1)}, bf16[4,128,256]{2,1,0:T(8,128)(2,1)S(1)}, u32[]{:S(2)}, u32[]{:S(2)}) %collective-permute-start.4) | collective-permute-done | bytes 262176 | tf_op jit(solution)/shard_map/ppermute | solution.py:224
  36.9 5.8 %collective-permute-done.3.refs_1_ = bf16[4,128,256]{2,1,0:T(8,128)(2,1)S(1)} collective-permute-done((bf16[4,128,256]{2,1,0:T(8,128)(2,1)S(1)}, bf16[4,128,256]{2,1,0:T(8,128)(2,1)S(1)}, u32[]{:S(2)}, u32[]{:S(2)}) %collective-permute-start.3) | collective-permute-done | bytes 262176 | tf_op jit(solution)/shard_map/ppermute | solution.py:224
  42.7 0.7 copy-done.8
  43.4 15.9 %shard_map.87 = (bf16[2048,256]{1,0:T(8,128)(2,1)}, bf16[4,128,256]{2,1,0:T(8,128)(2,1)S(1)}, bf16[4,128,256]{2,1,0:T(8,128)(2,1)S(1)}, bf16[4,128,256]{2,1,0:T(8,128)(2,1)S(1)}, bf16[4,128,256]{2,1,0:T(8,128)(2,1)S(1)}) custom-call(s32[2]{0:T(128)S(1)} %pad_add_fusion.pos_ref, bf16[2048,256]{1,0:T(8,128)(2,1)S(1)} %copy-done.3, ...), custom_call_target="tpu_custom_call" | custom-call | flops 5368709120 | bytes 4194304 | tf_op jit(solution)/shard_map/pallas_call | solution.py:139
  59.3 0.8 collective-permute-start.6
  60.1 1.3 %collective-permute-start.7 = (bf16[4,128,256]{2,1,0:T(8,128)(2,1)S(1)}, bf16[4,128,256]{2,1,0:T(8,128)(2,1)S(1)}, u32[]{:S(2)}, u32[]{:S(2)}) collective-permute-start(bf16[4,128,256]{2,1,0:T(8,128)(2,1)S(1)} %get-tuple-element.17), channel_id=1, source_target_pairs={{0,2},{1,3},{2,0},{3,1},{4,6},{5,7},{6,4},{7,5},{8,10},{9,11},{10,... | collective-permute-start | bytes 786440 | tf_op jit(solution)/shard_map/ppermute | solution.py:224
  61.4 0.9 collective-permute-start.8
  62.3 6.3 %all-to-all-start.1 = ((bf16[16,128,256]{2,1,0:T(8,128)(2,1)}), bf16[16,128,256]{2,1,0:T(8,128)(2,1)S(1)}, u32[]{:S(2)}, u32[]{:S(2)}) async-start(bf16[16,128,256]{2,1,0:T(8,128)(2,1)} %bitcast.2), calls=%async_computation.1 | async-start | bytes 2097152 | tf_op jit(solution)/shard_map/all_to_all | solution.py:243
  68.6 6.8 %collective-permute-done.7.refs_2_ = bf16[4,128,256]{2,1,0:T(8,128)(2,1)S(1)} collective-permute-done((bf16[4,128,256]{2,1,0:T(8,128)(2,1)S(1)}, bf16[4,128,256]{2,1,0:T(8,128)(2,1)S(1)}, u32[]{:S(2)}, u32[]{:S(2)}) %collective-permute-start.7) | collective-permute-done | bytes 262176 | tf_op jit(solution)/shard_map/ppermute | solution.py:224
  75.5 0.7 shard_map.88
  76.1 0.8 collective-permute-start.9
  76.9 7.8 %collective-permute-start.10 = (bf16[128,256]{1,0:T(8,128)(2,1)S(1)}, bf16[128,256]{1,0:T(8,128)(2,1)S(1)}, u32[]{:S(2)}, u32[]{:S(2)}) collective-permute-start(bf16[128,256]{1,0:T(8,128)(2,1)S(1)} %get-tuple-element.21), channel_id=1, source_target_pairs={{0,8},{1,9},{2,10},{3,11},{4,12},{5,13},{6,14},{7,15},{8,0},{9,1},... | collective-permute-start | bytes 196616 | tf_op jit(solution)/shard_map/ppermute | solution.py:220
  84.7 9.6 %all-to-all-done.1 = bf16[16,128,256]{2,1,0:T(8,128)(2,1)S(1)} async-done(((bf16[16,128,256]{2,1,0:T(8,128)(2,1)}), bf16[16,128,256]{2,1,0:T(8,128)(2,1)S(1)}, u32[]{:S(2)}, u32[]{:S(2)}) %all-to-all-start.1) | async-done | bytes 1048608 | tf_op jit(solution)/shard_map/all_to_all | solution.py:243
  94.3 0.1 copy.11
  94.4 0.0 copy-start
  94.4 3.4 %collective-permute-done.10.refs_2_ = bf16[128,256]{1,0:T(8,128)(2,1)S(1)} collective-permute-done((bf16[128,256]{1,0:T(8,128)(2,1)S(1)}, bf16[128,256]{1,0:T(8,128)(2,1)S(1)}, u32[]{:S(2)}, u32[]{:S(2)}) %collective-permute-start.10) | collective-permute-done | bytes 65568 | tf_op jit(solution)/shard_map/ppermute | solution.py:220
  97.8 1.3 %shard_map.89 = (bf16[128,512]{1,0:T(8,128)(2,1)}, bf16[128,512]{1,0:T(8,128)(2,1)}) custom-call(s32[2]{0:T(128)S(1)} %pad_add_fusion.pos_ref, bf16[128,256]{1,0:T(8,128)(2,1)S(1)} %get-tuple-element.19.refs_0_, bf16[128,256]{1,0:T(8,128)(2,1)S(1)} %collective-permute-done.9.refs_1_, bf16[128,256]{1,0:T(8,128)(2,1)S(1)} %collective-permute-done.10.refs_2_, ...), custom_call_target="tpu_custom_call" | custom-call | bytes 4194304 | tf_op jit(solution)/shard_map/pallas_call | solution.py:201
  (26 shorter events, 0.1 us)
Async XLA Ops:
  0.6 9.2 %copy-start.1 = (bf16[128,4096]{1,0:T(8,128)(2,1)S(1)}, bf16[128,4096]{1,0:T(8,128)(2,1)}, u32[]{:S(2)}) copy-start(bf16[128,4096]{1,0:T(8,128)(2,1)} %o_ref.1) | copy-start | bytes 3145732
  1.7 15.2 %collective-permute-start.1 = (bf16[128,256]{1,0:T(8,128)(2,1)S(1)}, bf16[128,256]{1,0:T(8,128)(2,1)S(1)}, u32[]{:S(2)}, u32[]{:S(2)}) collective-permute-start(bf16[128,256]{1,0:T(8,128)(2,1)S(1)} %pad_maximum_fusion.2), channel_id=1, source_target_pairs={{0,8},{1,9},{2,10},{3,11},{4,12},{5,13},{6,14},{7,15},{8,0},{9,1},... | collective-permute-start | bytes 196616 | tf_op jit(solution)/shard_map/ppermute | solution.py:220
  5.8 11.1 %collective-permute-start = (bf16[128,256]{1,0:T(8,128)(2,1)S(1)}, bf16[128,256]{1,0:T(8,128)(2,1)S(1)}, u32[]{:S(2)}, u32[]{:S(2)}) collective-permute-start(bf16[128,256]{1,0:T(8,128)(2,1)S(1)} %pad_maximum_fusion.1), channel_id=1, source_target_pairs={{0,4},{1,5},{2,6},{3,7},{4,8},{5,9},{6,10},{7,11},{8,12},{9,13},{1... | collective-permute-start | bytes 196616 | tf_op jit(solution)/shard_map/ppermute | solution.py:220
  7.5 9.5 %collective-permute-start.2 = (bf16[128,256]{1,0:T(8,128)(2,1)S(1)}, bf16[128,256]{1,0:T(8,128)(2,1)S(1)}, u32[]{:S(2)}, u32[]{:S(2)}) collective-permute-start(bf16[128,256]{1,0:T(8,128)(2,1)S(1)} %pad_maximum_fusion.3), channel_id=1, source_target_pairs={{0,12},{1,13},{2,14},{3,15},{4,0},{5,1},{6,2},{7,3},{8,4},{9,5},{1... | collective-permute-start | bytes 196616 | tf_op jit(solution)/shard_map/ppermute | solution.py:220
  9.8 1.2 %copy-start.2 = (bf16[128,4096]{1,0:T(8,128)(2,1)S(1)}, bf16[128,4096]{1,0:T(8,128)(2,1)}, u32[]{:S(2)}) copy-start(bf16[128,4096]{1,0:T(8,128)(2,1)} %g_ref.1) | copy-start | bytes 3145732
  13.1 30.3 %all-to-all-start = ((bf16[16,264,128]{2,1,0:T(8,128)(2,1)}), bf16[16,264,128]{2,1,0:T(8,128)(2,1)S(1)}, u32[]{:S(2)}, u32[]{:S(2)}) async-start(bf16[16,264,128]{2,1,0:T(8,128)(2,1)} %shard_map.85), calls=%async_computation | async-start | bytes 2162688 | tf_op jit(solution)/shard_map/all_to_all | solution.py:239
  16.9 26.5 %copy-start.3 = (bf16[2048,256]{1,0:T(8,128)(2,1)S(1)}, bf16[2048,256]{1,0:T(8,128)(2,1)}, u32[]{:S(2)}) copy-start(bf16[2048,256]{1,0:T(8,128)(2,1)} %q_ref.1) | copy-start | bytes 3145732
  16.9 26.5 %copy-start.5 = (f32[2,2048]{1,0:T(2,128)S(1)}, f32[2,2048]{1,0:T(2,128)}, u32[]{:S(2)}) copy-start(f32[2,2048]{1,0:T(2,128)} %lse_ref.1) | copy-start | bytes 49156
  17.0 26.4 %copy-start.4 = (bf16[4,128,256]{2,1,0:T(8,128)(2,1)}, bf16[4,128,256]{2,1,0:T(8,128)(2,1)S(1)}, u32[]{:S(2)}) copy-start(bf16[4,128,256]{2,1,0:T(8,128)(2,1)S(1)} %shard_map.86.refs_0_) | copy-start | bytes 786436
  17.0 17.9 %collective-permute-start.5 = (bf16[4,128,256]{2,1,0:T(8,128)(2,1)S(1)}, bf16[4,128,256]{2,1,0:T(8,128)(2,1)S(1)}, u32[]{:S(2)}, u32[]{:S(2)}) collective-permute-start(bf16[4,128,256]{2,1,0:T(8,128)(2,1)S(1)} %shard_map.86.refs_0_), channel_id=1, source_target_pairs={{0,3},{1,0},{2,1},{3,2},{4,7},{5,4},{6,5},{7,6},{8,11},{9,8},{10,9... | collective-permute-start | bytes 786440 | tf_op jit(solution)/shard_map/ppermute | solution.py:224
  19.9 17.0 %collective-permute-start.4 = (bf16[4,128,256]{2,1,0:T(8,128)(2,1)S(1)}, bf16[4,128,256]{2,1,0:T(8,128)(2,1)S(1)}, u32[]{:S(2)}, u32[]{:S(2)}) collective-permute-start(bf16[4,128,256]{2,1,0:T(8,128)(2,1)S(1)} %shard_map.86.refs_0_), channel_id=1, source_target_pairs={{0,2},{1,3},{2,0},{3,1},{4,6},{5,7},{6,4},{7,5},{8,10},{9,11},{10,... | collective-permute-start | bytes 786440 | tf_op jit(solution)/shard_map/ppermute | solution.py:224
  20.5 22.2 %collective-permute-start.3 = (bf16[4,128,256]{2,1,0:T(8,128)(2,1)S(1)}, bf16[4,128,256]{2,1,0:T(8,128)(2,1)S(1)}, u32[]{:S(2)}, u32[]{:S(2)}) collective-permute-start(bf16[4,128,256]{2,1,0:T(8,128)(2,1)S(1)} %shard_map.86.refs_0_), channel_id=1, source_target_pairs={{0,1},{1,2},{2,3},{3,0},{4,5},{5,6},{6,7},{7,4},{8,9},{9,10},{10,1... | collective-permute-start | bytes 786440 | tf_op jit(solution)/shard_map/ppermute | solution.py:224
  35.0 7.7 %copy-start.6 = (bf16[4,128,256]{2,1,0:T(8,128)(2,1)}, bf16[4,128,256]{2,1,0:T(8,128)(2,1)S(1)}, u32[]{:S(2)}) copy-start(bf16[4,128,256]{2,1,0:T(8,128)(2,1)S(1)} %collective-permute-done.5.refs_3_) | copy-start | bytes 786436
  36.9 5.8 %copy-start.7 = (bf16[4,128,256]{2,1,0:T(8,128)(2,1)}, bf16[4,128,256]{2,1,0:T(8,128)(2,1)S(1)}, u32[]{:S(2)}) copy-start(bf16[4,128,256]{2,1,0:T(8,128)(2,1)S(1)} %collective-permute-done.4.refs_2_) | copy-start | bytes 786436
  42.7 0.7 copy-start.8
  59.3 9.3 %collective-permute-start.6 = (bf16[4,128,256]{2,1,0:T(8,128)(2,1)S(1)}, bf16[4,128,256]{2,1,0:T(8,128)(2,1)S(1)}, u32[]{:S(2)}, u32[]{:S(2)}) collective-permute-start(bf16[4,128,256]{2,1,0:T(8,128)(2,1)S(1)} %get-tuple-element.16), channel_id=1, source_target_pairs={{0,1},{1,2},{2,3},{3,0},{4,5},{5,6},{6,7},{7,4},{8,9},{9,10},{10,1... | collective-permute-start | bytes 786440 | tf_op jit(solution)/shard_map/ppermute | solution.py:224
  60.1 15.4 %collective-permute-start.7 = (bf16[4,128,256]{2,1,0:T(8,128)(2,1)S(1)}, bf16[4,128,256]{2,1,0:T(8,128)(2,1)S(1)}, u32[]{:S(2)}, u32[]{:S(2)}) collective-permute-start(bf16[4,128,256]{2,1,0:T(8,128)(2,1)S(1)} %get-tuple-element.17), channel_id=1, source_target_pairs={{0,2},{1,3},{2,0},{3,1},{4,6},{5,7},{6,4},{7,5},{8,10},{9,11},{10,... | collective-permute-start | bytes 786440 | tf_op jit(solution)/shard_map/ppermute | solution.py:224
  61.4 14.1 %collective-permute-start.8 = (bf16[4,128,256]{2,1,0:T(8,128)(2,1)S(1)}, bf16[4,128,256]{2,1,0:T(8,128)(2,1)S(1)}, u32[]{:S(2)}, u32[]{:S(2)}) collective-permute-start(bf16[4,128,256]{2,1,0:T(8,128)(2,1)S(1)} %get-tuple-element.18), channel_id=1, source_target_pairs={{0,3},{1,0},{2,1},{3,2},{4,7},{5,4},{6,5},{7,6},{8,11},{9,8},{10,9... | collective-permute-start | bytes 786440 | tf_op jit(solution)/shard_map/ppermute | solution.py:224
  62.3 32.0 %all-to-all-start.1 = ((bf16[16,128,256]{2,1,0:T(8,128)(2,1)}), bf16[16,128,256]{2,1,0:T(8,128)(2,1)S(1)}, u32[]{:S(2)}, u32[]{:S(2)}) async-start(bf16[16,128,256]{2,1,0:T(8,128)(2,1)} %bitcast.2), calls=%async_computation.1 | async-start | bytes 2097152 | tf_op jit(solution)/shard_map/all_to_all | solution.py:243
  76.1 18.3 %collective-permute-start.9 = (bf16[128,256]{1,0:T(8,128)(2,1)S(1)}, bf16[128,256]{1,0:T(8,128)(2,1)S(1)}, u32[]{:S(2)}, u32[]{:S(2)}) collective-permute-start(bf16[128,256]{1,0:T(8,128)(2,1)S(1)} %get-tuple-element.20), channel_id=1, source_target_pairs={{0,4},{1,5},{2,6},{3,7},{4,8},{5,9},{6,10},{7,11},{8,12},{9,13},{1... | collective-permute-start | bytes 196616 | tf_op jit(solution)/shard_map/ppermute | solution.py:220
  76.9 20.9 %collective-permute-start.10 = (bf16[128,256]{1,0:T(8,128)(2,1)S(1)}, bf16[128,256]{1,0:T(8,128)(2,1)S(1)}, u32[]{:S(2)}, u32[]{:S(2)}) collective-permute-start(bf16[128,256]{1,0:T(8,128)(2,1)S(1)} %get-tuple-element.21), channel_id=1, source_target_pairs={{0,8},{1,9},{2,10},{3,11},{4,12},{5,13},{6,14},{7,15},{8,0},{9,1},... | collective-permute-start | bytes 196616 | tf_op jit(solution)/shard_map/ppermute | solution.py:220
  84.7 13.1 %collective-permute-start.11 = (bf16[128,256]{1,0:T(8,128)(2,1)S(1)}, bf16[128,256]{1,0:T(8,128)(2,1)S(1)}, u32[]{:S(2)}, u32[]{:S(2)}) collective-permute-start(bf16[128,256]{1,0:T(8,128)(2,1)S(1)} %get-tuple-element.22), channel_id=1, source_target_pairs={{0,12},{1,13},{2,14},{3,15},{4,0},{5,1},{6,2},{7,3},{8,4},{9,5},{1... | collective-permute-start | bytes 196616 | tf_op jit(solution)/shard_map/ppermute | solution.py:220
  94.4 4.7 %copy-start = (bf16[16,16,8,256]{3,2,0,1:T(8,128)(2,1)}, bf16[16,16,8,256]{3,2,0,1:T(8,128)(2,1)S(1)}, u32[]{:S(2)}) copy-start(bf16[16,16,8,256]{3,2,0,1:T(8,128)(2,1)S(1)} %copy.11) | copy-start | bytes 3145732
